TPU v7x, 32 devices: a whole 2x2x4 slice. The times are simulated.
32 devices in a mesh: dp: 8 (over y, x, core), tensor: 4 (over z).
Axes of the slice: x: 2, y: 2, z: 4, core: 2. Of those that a mesh axis runs over, the one named last changes fastest.
Arguments:
- tokens_in: bfloat16 [8192, 2048], P(('dp', 'tensor')), may hold values from -6 to 6
- segment_ids: int32 [8192], P('dp'), may hold values from 0 to 26, never falling along the last dimension, each value on 1 to 800 neighbouring positions
- cotangent: bfloat16 [8192, 2048], P(('dp', 'tensor')), may hold values from -6 to 6
- norm_first: bfloat16 [2048], P('dp'), may hold values from 0.5 to 1.5
- query_weight: bfloat16 [2048, 1024], P('dp', 'tensor'), may hold values from -0.125 to 0.125
- key_value_weight: bfloat16 [2048, 512], P('dp'), may hold values from -0.125 to 0.125
- output_weight: bfloat16 [1024, 2048], P('tensor', 'dp'), may hold values from -1.5 to 1.5
- inner_weight: bfloat16 [2048, 2, 3072], P('dp', None, 'tensor'), may hold values from -0.125 to 0.125
- state_weight: bfloat16 [2048, 512], P('dp'), may hold values from -0.125 to 0.125
- step_weight: bfloat16 [2048, 48], P('dp', 'tensor'), may hold values from -0.125 to 0.125
- conv_inner: bfloat16 [5, 48, 64], P(None, 'tensor'), may hold values from -0.5 to 0.5
- conv_state: bfloat16 [5, 512], replicated, may hold values from -0.5 to 0.5
- head_params: float32 [3, 48], P(None, 'tensor'), may hold values from -7 to 3, as said below
- gate_gain: bfloat16 [48, 64], P('tensor'), may hold values from 0.5 to 1.5
- mamba_weight: bfloat16 [3072, 2048], P('tensor', 'dp'), may hold values from -0.109375 to 0.109375
- norm_second: bfloat16 [2048], P('dp'), may hold values from 0.5 to 1.5
- expand_weight: bfloat16 [2048, 2, 4096], P('dp', None, 'tensor'), may hold values from -0.125 to 0.125
- shrink_weight: bfloat16 [4096, 2048], P('tensor', 'dp'), may hold values from -0.09375 to 0.09375
Outputs:
- block_out: bfloat16 [8192, 2048], P(('dp', 'tensor'))
- grad_tokens: float32 [8192, 2048], P(('dp', 'tensor'))
- grad_norm_first: float32 [2048], P(('dp', 'tensor'))
- grad_query: float32 [2048, 1024], P('dp', 'tensor')
- grad_keyval: float32 [2048, 512], P(('dp', 'tensor'))
- grad_output: float32 [1024, 2048], P('tensor', 'dp')
- grad_inner: float32 [2048, 2, 3072], P('dp', None, 'tensor')
- grad_state: float32 [2048, 512], P(('dp', 'tensor'))
- grad_step: float32 [2048, 48], P('dp', 'tensor')
- grad_conv_inner: float32 [5, 48, 64], P(None, 'tensor', 'dp')
- grad_conv_state: float32 [5, 512], P(None, ('dp', 'tensor'))
- grad_head_params: float32 [3, 48], P(None, 'tensor')
- grad_gate_gain: float32 [48, 64], P('tensor', 'dp')
- grad_mamba: float32 [3072, 2048], P('tensor', 'dp')
- grad_norm_second: float32 [2048], P(('dp', 'tensor'))
- grad_expand: float32 [2048, 2, 4096], P('dp', None, 'tensor')
- grad_shrink: float32 [4096, 2048], P('tensor', 'dp')
Inputs may be any that keep to these rules, and one draw needn't show every extreme that they name: `segment_ids`: ids never fall along the tokens; each id covers 1 to 800 consecutive tokens and one covers exactly 800. `head_params`: row 0 lies in [0, log 16], row 1 is the inverse softplus of a value in [0.001, 0.1], row 2 lies in [0.5, 1.5].
All inputs are finite; a program needn't handle non-finite values.
Results may differ from a plain program's by a relative error of at most 0.025.
Values may be sent and summed in bfloat16 or wider, within the bound.
A program may use at most 320 MiB of HBM per device.

v0:
```python
import math

import jax
import jax.numpy as jnp
from jax import lax
from jax.sharding import PartitionSpec as P

QUERY_HEADS = 8
KEY_HEADS = 2
HEAD_SIZE = 128
PM = 64
NS = 256
KC = 4
SEQ_LEN = 1024
DSSM = 3072


EPS = 1e-05
THETA = 100000000000.0
PRECISION_HIGH = lax.Precision.HIGHEST


def matrix_plain_product(left_side, right_side):
    return jnp.dot(left_side, right_side, preferred_element_type=jnp.float32)


def mat_nt(left_side, right_side):
    return lax.dot_general(
        left_side, right_side, (((1,), (1,)), ((), ())), preferred_element_type=jnp.float32
    )


def mat_tn(left_side, right_side):
    return lax.dot_general(
        left_side, right_side, (((0,), (0,)), ((), ())), preferred_element_type=jnp.float32
    )


def rms_norm(values, gain_vec):
    return values * lax.rsqrt(jnp.mean(values * values, -1, keepdims=True) + EPS) * gain_vec


def rotate(values, angles):
    halfway = values.shape[-1] // 2
    frequency = jnp.exp(
        jnp.arange(halfway).astype(jnp.float32) * (-2.0 * math.log(THETA) / values.shape[-1])
    )
    turned = angles[:, None] * frequency[None, :]
    cosine = jnp.cos(turned)[:, None, :]
    sine_part = jnp.sin(turned)[:, None, :]
    front_half = values[..., :halfway]
    back_half = values[..., halfway:]
    return jnp.concatenate(
        [front_half * cosine - back_half * sine_part, back_half * cosine + front_half * sine_part],
        -1,
    )


def short_conv(inputs, conv_weight, seg_ids, position):
    taps = conv_weight.shape[0] - 1
    segment_length = inputs.shape[0]
    result = conv_weight[taps] + conv_weight[taps - 1] * inputs
    for lag_steps in range(1, taps):
        moved = jnp.concatenate(
            [
                jnp.zeros((lag_steps, inputs.shape[1]), inputs.dtype),
                inputs[: segment_length - lag_steps],
            ],
            0,
        )
        earlier = jnp.concatenate(
            [jnp.full((lag_steps,), -1, jnp.int32), seg_ids[: segment_length - lag_steps]], 0
        )
        keep_mask = ((earlier == seg_ids) & (position >= lag_steps)).astype(inputs.dtype)
        result = result + conv_weight[taps - 1 - lag_steps] * moved * keep_mask[:, None]
    return result


def prepare(lin_x, lin_bc, lin_dt, conv_weight, heads_vec, seg_ids, position):
    mixed = jax.nn.silu(
        short_conv(jnp.concatenate([lin_x, lin_bc], 1), conv_weight, seg_ids, position)
    )
    step_size = jax.nn.softplus(lin_dt + heads_vec[1])
    return (mixed, step_size, -step_size * jnp.exp(heads_vec[0]))


def state_space(inner_x, state_b, state_c, step_size, log_decay, skip_gain, seg_ids):
    segment_length = inner_x.shape[0]
    index = jnp.arange(segment_length)
    allowed = (index[:, None] >= index[None, :]) & (seg_ids[:, None] == seg_ids[None, :])
    running = jnp.cumsum(log_decay, 0).T
    decay_gap = running[:, :, None] - running[:, None, :]
    decay = jnp.where(allowed[None], jnp.exp(jnp.where(allowed[None], decay_gap, 0.0)), 0.0)
    gram_mat = jnp.dot(state_c, state_b.T, precision=PRECISION_HIGH)
    mixing = gram_mat[None] * decay * step_size.T[:, None, :]
    return (
        jnp.einsum("hts,shp->thp", mixing, inner_x, precision=PRECISION_HIGH)
        + skip_gain[None, :, None] * inner_x
    )


def gate_apply(signal, gate_value):
    return signal * jax.nn.silu(gate_value)


def swiglu(hidden_lin):
    halfway = hidden_lin.shape[1] // 2
    return jax.nn.silu(hidden_lin[:, :halfway]) * hidden_lin[:, halfway:]


def allowed_pairs(seg_ids):
    index = jnp.arange(seg_ids.shape[0])
    return (index[:, None] >= index[None, :]) & (seg_ids[:, None] == seg_ids[None, :])


def attend_forward(query_rows, key_rows, value_rows, seg_ids):
    scores = jnp.einsum(
        "thd,shd->hts", query_rows, key_rows, preferred_element_type=jnp.float32
    ) / math.sqrt(query_rows.shape[-1])
    scores = jnp.where(allowed_pairs(seg_ids)[None], scores, -1e30)
    row_top = jnp.max(scores, -1, keepdims=True)
    shifted = jnp.exp(scores - row_top)
    row_total = jnp.sum(shifted, -1, keepdims=True)
    weights_low = (shifted / row_total).astype(jnp.bfloat16)
    outcome = jnp.einsum(
        "hts,shd->thd", weights_low, value_rows, preferred_element_type=jnp.float32
    )
    return (outcome, row_top + jnp.log(row_total))


def attend_backward(query_rows, key_rows, value_rows, seg_ids, log_total, grad_out):
    root_size = math.sqrt(query_rows.shape[-1])
    scores = (
        jnp.einsum("thd,shd->hts", query_rows, key_rows, preferred_element_type=jnp.float32)
        / root_size
    )
    scores = jnp.where(allowed_pairs(seg_ids)[None], scores, -1e30)
    weights_full = jnp.exp(scores - log_total)
    grad_values = jnp.einsum(
        "hts,thd->shd",
        weights_full.astype(jnp.bfloat16),
        grad_out,
        preferred_element_type=jnp.float32,
    )
    grad_weights = jnp.einsum(
        "thd,shd->hts", grad_out, value_rows, preferred_element_type=jnp.float32
    )
    inner_sum = jnp.sum(grad_weights * weights_full, -1, keepdims=True)
    grad_scores = (weights_full * (grad_weights - inner_sum)).astype(jnp.bfloat16)
    grad_query = (
        jnp.einsum("hts,shd->thd", grad_scores, key_rows, preferred_element_type=jnp.float32)
        / root_size
    )
    grad_keys = (
        jnp.einsum("hts,thd->shd", grad_scores, query_rows, preferred_element_type=jnp.float32)
        / root_size
    )
    return (grad_query, grad_keys, grad_values)


def per_device(
    tokens_in,
    segment_ids,
    cotangent,
    norm_first,
    query_weight,
    key_value_weight,
    output_weight,
    inner_weight,
    state_weight,
    step_weight,
    conv_inner,
    conv_state,
    head_params,
    gate_gain,
    mamba_weight,
    norm_second,
    expand_weight,
    shrink_weight,
):
    data_shard_count = lax.axis_size("dp")
    tensor_shard_count = lax.axis_size("tensor")
    row_grand_total = segment_ids.shape[0]
    model_width = tokens_in.shape[1]
    seq_count = row_grand_total // SEQ_LEN
    (
        gain_first,
        query_full,
        key_value_whole,
        output_full,
        inner_full,
        state_full,
        step_full,
        mamba_full,
        gain_second,
        expand_full,
        shrink_full,
    ) = (
        lax.all_gather(norm_first, "dp", axis=0, tiled=True),
        lax.all_gather(query_weight, "dp", axis=0, tiled=True),
        lax.all_gather(key_value_weight, "dp", axis=0, tiled=True),
        lax.all_gather(output_weight, "dp", axis=1, tiled=True),
        lax.all_gather(inner_weight, "dp", axis=0, tiled=True),
        lax.all_gather(state_weight, "dp", axis=0, tiled=True),
        lax.all_gather(step_weight, "dp", axis=0, tiled=True),
        lax.all_gather(mamba_weight, "dp", axis=1, tiled=True),
        lax.all_gather(norm_second, "dp", axis=0, tiled=True),
        lax.all_gather(expand_weight, "dp", axis=0, tiled=True),
        lax.all_gather(shrink_weight, "dp", axis=1, tiled=True),
    )
    shard_heads = query_full.shape[1] // HEAD_SIZE
    channels = inner_full.shape[2]
    ssm_local = step_full.shape[1]
    hidden_local = expand_full.shape[2]
    position = jnp.arange(row_grand_total) % SEQ_LEN
    angles = position.astype(jnp.float32)
    seg_seq = segment_ids.reshape(seq_count, SEQ_LEN)
    tokens_all = lax.all_gather(tokens_in, "tensor", axis=0, tiled=True)
    tokens_wide = tokens_all.astype(jnp.float32)
    gain_one = gain_first.astype(jnp.float32)
    first_val, norm_one_pull = jax.vjp(rms_norm, tokens_wide, gain_one)
    leading_rows = first_val.astype(jnp.bfloat16)
    query_lin = matrix_plain_product(leading_rows, query_full).reshape(
        row_grand_total, shard_heads, HEAD_SIZE
    )
    query_rot, query_pull = jax.vjp(lambda values: rotate(values, angles), query_lin)
    query_low = query_rot.astype(jnp.bfloat16)
    pair_linear = matrix_plain_product(leading_rows, key_value_whole).reshape(
        row_grand_total, 2, KEY_HEADS, HEAD_SIZE
    )
    key_rot, key_pull = jax.vjp(lambda values: rotate(values, angles), pair_linear[:, 0])
    key_value_head = lax.axis_index("tensor") * shard_heads // (QUERY_HEADS // KEY_HEADS)
    key_one = lax.dynamic_slice_in_dim(key_rot.astype(jnp.bfloat16), key_value_head, 1, 1)
    value_one = lax.dynamic_slice_in_dim(
        pair_linear[:, 1].astype(jnp.bfloat16), key_value_head, 1, 1
    )
    key_mine = jnp.broadcast_to(key_one, (row_grand_total, shard_heads, HEAD_SIZE))
    value_mine = jnp.broadcast_to(value_one, (row_grand_total, shard_heads, HEAD_SIZE))
    seq_heads = (seq_count, SEQ_LEN, shard_heads, HEAD_SIZE)
    attn_inputs = (
        query_low.reshape(seq_heads),
        key_mine.reshape(seq_heads),
        value_mine.reshape(seq_heads),
        seg_seq,
    )

    def attend_one(seq_items):
        return attend_forward(seq_items[0], seq_items[1], seq_items[2], seq_items[3])

    attn_raw, log_total = lax.map(attend_one, attn_inputs)
    attended = attn_raw.reshape(row_grand_total, shard_heads * HEAD_SIZE).astype(jnp.bfloat16)
    inner_flat = inner_full.reshape(model_width, 2 * channels)
    inner_lin = matrix_plain_product(leading_rows, inner_flat)
    gate_lin = inner_lin[:, :channels]
    state_lin = matrix_plain_product(leading_rows, state_full)
    step_lin = matrix_plain_product(leading_rows, step_full)
    conv_weight = jnp.concatenate(
        [conv_inner.astype(jnp.float32).reshape(KC + 1, channels), conv_state.astype(jnp.float32)],
        1,
    )

    def prep_local(lin_x, lin_bc, lin_dt, weight_all, heads_all):
        return prepare(lin_x, lin_bc, lin_dt, weight_all, heads_all, segment_ids, position)

    (mixed, step_size, log_decay), prep_pull = jax.vjp(
        prep_local, inner_lin[:, channels:], state_lin, step_lin, conv_weight, head_params
    )
    mixed_low = lax.optimization_barrier(mixed.astype(jnp.bfloat16)).astype(jnp.float32)
    ssm_inputs = (
        mixed_low[:, :channels].reshape(seq_count, SEQ_LEN, ssm_local, PM),
        mixed_low[:, channels : channels + NS].reshape(seq_count, SEQ_LEN, NS),
        mixed_low[:, channels + NS :].reshape(seq_count, SEQ_LEN, NS),
        step_size.reshape(seq_count, SEQ_LEN, ssm_local),
        log_decay.reshape(seq_count, SEQ_LEN, ssm_local),
        seg_seq,
    )

    def ssd_one(seq_items):
        return state_space(
            seq_items[0],
            seq_items[1],
            seq_items[2],
            seq_items[3],
            seq_items[4],
            head_params[2],
            seq_items[5],
        )

    ssm_flat = lax.map(ssd_one, ssm_inputs).reshape(row_grand_total, channels)
    gated, gate_pull = jax.vjp(gate_apply, ssm_flat, gate_lin)
    square_sum = lax.psum(jnp.sum(gated * gated, -1), "tensor")
    inverse = lax.rsqrt(square_sum / DSSM + EPS)[:, None]
    gain_gate = gate_gain.astype(jnp.float32).reshape(channels)
    normed = (gated * inverse * gain_gate).astype(jnp.bfloat16)
    mix_sum = lax.psum_scatter(
        (
            matrix_plain_product(attended, output_full) + matrix_plain_product(normed, mamba_full)
        ).astype(jnp.bfloat16),
        "tensor",
        scatter_dimension=0,
        tiled=True,
    ).astype(jnp.float32)
    middle = tokens_in.astype(jnp.float32) + mix_sum
    gain_two = gain_second.astype(jnp.float32)
    second_val, norm_two_pull = jax.vjp(rms_norm, middle, gain_two)
    second_all = lax.all_gather(second_val.astype(jnp.bfloat16), "tensor", axis=0, tiled=True)
    expand_flat = expand_full.reshape(model_width, 2 * hidden_local)
    hidden_lin = matrix_plain_product(second_all, expand_flat)
    activated, swiglu_pull = jax.vjp(swiglu, hidden_lin)
    act_low = activated.astype(jnp.bfloat16)
    ffn_out = lax.psum_scatter(
        matrix_plain_product(act_low, shrink_full).astype(jnp.bfloat16),
        "tensor",
        scatter_dimension=0,
        tiled=True,
    ).astype(jnp.float32)
    block_out = (middle + ffn_out).astype(jnp.bfloat16)
    grad_top = cotangent.astype(jnp.float32)
    cot_all = lax.all_gather(cotangent, "tensor", axis=0, tiled=True)
    grad_shrink_full = mat_tn(act_low, cot_all)
    grad_hidden = swiglu_pull(mat_nt(cot_all, shrink_full))[0].astype(jnp.bfloat16)
    grad_expand_full = mat_tn(second_all, grad_hidden).reshape(model_width, 2, hidden_local)
    grad_second_own = lax.psum_scatter(
        mat_nt(grad_hidden, expand_flat).astype(jnp.bfloat16),
        "tensor",
        scatter_dimension=0,
        tiled=True,
    ).astype(jnp.float32)
    grad_mid_part, grad_gain_two = norm_two_pull(grad_second_own)
    grad_middle = grad_top + grad_mid_part
    mix_all = lax.all_gather(grad_middle.astype(jnp.bfloat16), "tensor", axis=0, tiled=True)
    grad_attended = mat_nt(mix_all, output_full).astype(jnp.bfloat16)
    grad_output_full = mat_tn(attended, mix_all)
    grad_normed = mat_nt(mix_all, mamba_full)
    grad_mamba_full = mat_tn(normed, mix_all)
    scaled = grad_normed * gain_gate
    cross = lax.psum(jnp.sum(gated * scaled, -1), "tensor")
    grad_gated = inverse * scaled - gated * (inverse * inverse * inverse) * (cross / DSSM)[:, None]
    grad_gate_gain = jnp.sum(gated * inverse * grad_normed, 0).reshape(ssm_local, PM)
    grad_ssm_flat, grad_gate_lin = gate_pull(grad_gated)

    def ssd_back(seq_items):

        def local_ssd(x_part, b_part, c_part, step_part, decay_part, skip_part):
            return state_space(
                x_part, b_part, c_part, step_part, decay_part, skip_part, seq_items[5]
            )

        ignored_val, ssd_pull = jax.vjp(
            local_ssd,
            seq_items[0],
            seq_items[1],
            seq_items[2],
            seq_items[3],
            seq_items[4],
            head_params[2],
        )
        return ssd_pull(seq_items[6])

    grad_x_in, grad_b_in, grad_c_in, grad_step_in, grad_decay_in, grad_skip_in = lax.map(
        ssd_back, ssm_inputs + (grad_ssm_flat.reshape(seq_count, SEQ_LEN, ssm_local, PM),)
    )
    grad_mixed = jnp.concatenate(
        [
            grad_x_in.reshape(row_grand_total, channels),
            grad_b_in.reshape(row_grand_total, NS),
            grad_c_in.reshape(row_grand_total, NS),
        ],
        1,
    )
    grad_lin_x, grad_lin_bc, grad_lin_dt, grad_conv_weight, grad_heads_part = prep_pull(
        (
            grad_mixed,
            grad_step_in.reshape(row_grand_total, ssm_local),
            grad_decay_in.reshape(row_grand_total, ssm_local),
        )
    )
    grad_bc_low = grad_lin_bc.astype(jnp.bfloat16)
    grad_dt_low = grad_lin_dt.astype(jnp.bfloat16)
    grad_heads = jnp.stack(
        [grad_heads_part[0], grad_heads_part[1], grad_heads_part[2] + jnp.sum(grad_skip_in, 0)]
    )
    grad_inner_lin = jnp.concatenate([grad_gate_lin, grad_lin_x], 1).astype(jnp.bfloat16)

    def attend_back_one(seq_items):
        return attend_backward(
            seq_items[0], seq_items[1], seq_items[2], seq_items[3], seq_items[4], seq_items[5]
        )

    grad_q_rot, grad_k_mine, grad_v_mine = lax.map(
        attend_back_one, attn_inputs + (log_total, grad_attended.reshape(seq_heads))
    )
    grad_query_lin = (
        query_pull(grad_q_rot.reshape(row_grand_total, shard_heads, HEAD_SIZE))[0]
        .reshape(row_grand_total, shard_heads * HEAD_SIZE)
        .astype(jnp.bfloat16)
    )
    blank_head_slots = jnp.zeros((row_grand_total, KEY_HEADS, HEAD_SIZE), jnp.float32)
    grad_key_one = jnp.sum(
        grad_k_mine.reshape(row_grand_total, shard_heads, HEAD_SIZE), 1, keepdims=True
    )
    grad_value_one = jnp.sum(
        grad_v_mine.reshape(row_grand_total, shard_heads, HEAD_SIZE), 1, keepdims=True
    )
    grad_key_all = lax.dynamic_update_slice_in_dim(
        blank_head_slots, grad_key_one, key_value_head, 1
    )
    grad_value_all = lax.dynamic_update_slice_in_dim(
        blank_head_slots, grad_value_one, key_value_head, 1
    )
    grad_key_lin = key_pull(grad_key_all)[0]
    grad_pair = (
        jnp.stack([grad_key_lin, grad_value_all], 1)
        .reshape(row_grand_total, 2 * KEY_HEADS * HEAD_SIZE)
        .astype(jnp.bfloat16)
    )
    grad_query_full = mat_tn(leading_rows, grad_query_lin)
    grad_inner_full = mat_tn(leading_rows, grad_inner_lin).reshape(model_width, 2, channels)
    gradient_pair_whole = mat_tn(leading_rows, grad_pair)
    grad_state_full = mat_tn(leading_rows, grad_bc_low)
    grad_step_full = mat_tn(leading_rows, grad_dt_low)
    grad_first = (
        mat_nt(grad_query_lin, query_full)
        + mat_nt(grad_inner_lin, inner_flat)
        + mat_nt(grad_pair, key_value_whole)
        + mat_nt(grad_bc_low, state_full)
        + mat_nt(grad_dt_low, step_full)
    )
    grad_tokens_part, grad_gain_one = norm_one_pull(grad_first)
    slice_part = model_width // (data_shard_count * tensor_shard_count)
    conv_piece = 2 * NS // (data_shard_count * tensor_shard_count)
    grad_tokens_own, gain_one_part, gain_two_part, pair_part, state_part, conv_state_part = (
        lax.psum_scatter(
            grad_tokens_part.astype(jnp.bfloat16), "tensor", scatter_dimension=0, tiled=True
        ).astype(jnp.float32),
        lax.psum_scatter(
            grad_gain_one.reshape(data_shard_count, tensor_shard_count, slice_part).astype(
                jnp.bfloat16
            ),
            "tensor",
            scatter_dimension=1,
            tiled=True,
        ).astype(jnp.float32),
        lax.psum_scatter(
            grad_gain_two.reshape(data_shard_count, tensor_shard_count, slice_part).astype(
                jnp.bfloat16
            ),
            "tensor",
            scatter_dimension=1,
            tiled=True,
        ).astype(jnp.float32),
        lax.psum_scatter(
            gradient_pair_whole.reshape(
                data_shard_count, tensor_shard_count, slice_part, 2 * KEY_HEADS * HEAD_SIZE
            ).astype(jnp.bfloat16),
            "tensor",
            scatter_dimension=1,
            tiled=True,
        ).astype(jnp.float32),
        lax.psum_scatter(
            grad_state_full.reshape(
                data_shard_count, tensor_shard_count, slice_part, 2 * NS
            ).astype(jnp.bfloat16),
            "tensor",
            scatter_dimension=1,
            tiled=True,
        ).astype(jnp.float32),
        lax.psum_scatter(
            grad_conv_weight[:, channels:]
            .reshape(KC + 1, data_shard_count, tensor_shard_count, conv_piece)
            .astype(jnp.bfloat16),
            "tensor",
            scatter_dimension=2,
            tiled=True,
        ).astype(jnp.float32),
    )
    grad_tokens = grad_middle + grad_tokens_own
    grad_conv_inner_full = grad_conv_weight[:, :channels].reshape(KC + 1, ssm_local, PM)
    head_slots = jnp.broadcast_to(grad_heads[None], (data_shard_count, 3, ssm_local))
    (
        query_sum,
        output_sum,
        inner_sum,
        step_sum,
        conv_inner_sum,
        gate_gain_sum,
        mamba_sum,
        head_sum,
        gain_one_sum,
        gain_two_sum,
        pair_total_sum,
        state_sum,
        conv_state_sum,
        expand_sum,
        shrink_sum,
    ) = (
        lax.psum_scatter(
            grad_query_full.astype(jnp.bfloat16), "dp", scatter_dimension=0, tiled=True
        ).astype(jnp.float32),
        lax.psum_scatter(
            grad_output_full.astype(jnp.bfloat16), "dp", scatter_dimension=1, tiled=True
        ).astype(jnp.float32),
        lax.psum_scatter(
            grad_inner_full.astype(jnp.bfloat16), "dp", scatter_dimension=0, tiled=True
        ).astype(jnp.float32),
        lax.psum_scatter(
            grad_step_full.astype(jnp.bfloat16), "dp", scatter_dimension=0, tiled=True
        ).astype(jnp.float32),
        lax.psum_scatter(
            grad_conv_inner_full.astype(jnp.bfloat16), "dp", scatter_dimension=2, tiled=True
        ).astype(jnp.float32),
        lax.psum_scatter(
            grad_gate_gain.astype(jnp.bfloat16), "dp", scatter_dimension=1, tiled=True
        ).astype(jnp.float32),
        lax.psum_scatter(
            grad_mamba_full.astype(jnp.bfloat16), "dp", scatter_dimension=1, tiled=True
        ).astype(jnp.float32),
        lax.psum_scatter(
            head_slots.astype(jnp.bfloat16), "dp", scatter_dimension=0, tiled=True
        ).astype(jnp.float32),
        lax.psum_scatter(
            gain_one_part.astype(jnp.bfloat16), "dp", scatter_dimension=0, tiled=True
        ).astype(jnp.float32),
        lax.psum_scatter(
            gain_two_part.astype(jnp.bfloat16), "dp", scatter_dimension=0, tiled=True
        ).astype(jnp.float32),
        lax.psum_scatter(
            pair_part.astype(jnp.bfloat16), "dp", scatter_dimension=0, tiled=True
        ).astype(jnp.float32),
        lax.psum_scatter(
            state_part.astype(jnp.bfloat16), "dp", scatter_dimension=0, tiled=True
        ).astype(jnp.float32),
        lax.psum_scatter(
            conv_state_part.astype(jnp.bfloat16), "dp", scatter_dimension=1, tiled=True
        ).astype(jnp.float32),
        lax.psum_scatter(
            grad_expand_full.astype(jnp.bfloat16), "dp", scatter_dimension=0, tiled=True
        ).astype(jnp.float32),
        lax.psum_scatter(
            grad_shrink_full.astype(jnp.bfloat16), "dp", scatter_dimension=1, tiled=True
        ).astype(jnp.float32),
    )
    return (
        block_out,
        grad_tokens,
        gain_one_sum.reshape(slice_part),
        query_sum,
        pair_total_sum.reshape(slice_part, 2 * KEY_HEADS * HEAD_SIZE),
        output_sum,
        inner_sum,
        state_sum.reshape(slice_part, 2 * NS),
        step_sum,
        conv_inner_sum,
        conv_state_sum.reshape(KC + 1, conv_piece),
        head_sum.reshape(3, ssm_local),
        gate_gain_sum,
        mamba_sum,
        gain_two_sum.reshape(slice_part),
        expand_sum,
        shrink_sum,
    )


def solution(mesh):
    return jax.shard_map(
        per_device,
        mesh=mesh,
        in_specs=(
            P(("dp", "tensor"), None),
            P("dp"),
            P(("dp", "tensor"), None),
            P("dp"),
            P("dp", "tensor"),
            P("dp", None),
            P("tensor", "dp"),
            P("dp", None, "tensor"),
            P("dp", None),
            P("dp", "tensor"),
            P(None, "tensor", None),
            P(),
            P(None, "tensor"),
            P("tensor", None),
            P("tensor", "dp"),
            P("dp"),
            P("dp", None, "tensor"),
            P("tensor", "dp"),
        ),
        out_specs=(
            P(("dp", "tensor"), None),
            P(("dp", "tensor"), None),
            P(("dp", "tensor")),
            P("dp", "tensor"),
            P(("dp", "tensor"), None),
            P("tensor", "dp"),
            P("dp", None, "tensor"),
            P(("dp", "tensor"), None),
            P("dp", "tensor"),
            P(None, "tensor", "dp"),
            P(None, ("dp", "tensor")),
            P(None, "tensor"),
            P("tensor", "dp"),
            P("tensor", "dp"),
            P(("dp", "tensor")),
            P("dp", None, "tensor"),
            P("tensor", "dp"),
        ),
        check_vma=False,
    )
```

profile of v0, /device:TPU:0, one launch (start us, length us, event | category | flops | bytes accessed | tf_op | source)
XLA Modules:
  0.0 1953.8 jit_solution(15845200435030363081)
XLA Ops:
  12.7 10.3 all-gather
  23.0 9.0 all_gather.52
  39.9 53.2 %all-gather.15.cloned.1.call-done = bf16[1024,2048]{1,0:T(8,128)(2,1)} async-done(((bf16[256,2048]{1,0:T(8,128)(2,1)}), bf16[1024,2048]{1,0:T(8,128)(2,1)}) %all-gather.15.cloned.1.call-update) | async-done | bytes 4194320 | tf_op jit(solution)/shard_map/all_gather | solution.py:218
  100.0 21.4 %all-gather.17.cloned.1.call-done = bf16[2048,512]{1,0:T(8,128)(2,1)} async-done(((bf16[256,512]{1,0:T(8,128)(2,1)}), bf16[2048,512]{1,0:T(8,128)(2,1)}) %all-gather.17.cloned.1.call-update) | async-done | bytes 2097168 | tf_op jit(solution)/shard_map/all_gather | solution.py:201
  121.5 5.4 fusion.144
  134.7 12.2 all-gather.19.cloned.1.call-done
  168.0 8.5 all-gather.25.cloned.1.call-done
  176.6 5.2 fusion.147
  181.8 42.1 %all-gather.23.cloned.1.call-done = bf16[2048,2,768]{2,1,0:T(2,128)(2,1)} async-done(((bf16[256,2,768]{2,1,0:T(2,128)(2,1)}), bf16[2048,2,768]{2,1,0:T(2,128)(2,1)}) %all-gather.23.cloned.1.call-update) | async-done | bytes 6291472 | tf_op jit(solution)/shard_map/all_gather | solution.py:203
  223.9 6.9 copy.277
  230.8 9.1 fusion.146
  247.8 6.9 multiply_convert_fusion.1
  264.5 42.1 %bitcast_add_fusion.1 = f32[1024,12,64]{0,2,1:T(8,128)} fusion(f32[1024,12,64]{0,2,1:T(8,128)} %bitcast.237, bf16[1024,12,64]{0,2,1:T(8,128)(2,1)S(1)} %bitcast.246, f32[12,1024]{1,0:T(8,128)S(1)} %get-tuple-element.278, f32[12,1024]{1,0:T(8,128)S(1)} %bitcast.274, f32[1024,1024]{1,0:T(8,128)} %fusion.73, pred[1024,1024]{1,0:T(8,128)(4,1)} %copy.211, ...), kind=kOutput, calls=%fused_computation.94 | convolution fusion | flops 9728163840 | bytes 13205552 | tf_op jit(solution)/shard_map/while/body/eval_jaxpr/hts,shp->thp/dot_general | solution.py:97
  309.0 5.5 multiply_reduce_fusion.10
  314.5 11.7 psum.14
  326.3 9.7 fusion.134
  336.0 7.1 add_convert_fusion.1
  344.0 8.8 all-gather.1
  352.8 64.5 %reduce-scatter.23.cloned.1.call-done = bf16[256,2048]{1,0:T(8,128)(2,1)} async-done(((bf16[1024,2048]{1,0:T(8,128)(2,1)}), bf16[256,2048]{1,0:T(8,128)(2,1)}) %reduce-scatter.23.cloned.1.call-update) | async-done | bytes 1048592 | tf_op jit(solution)/shard_map/reduce_scatter | solution.py:295
  423.0 51.3 %all-gather.31.cloned.1.call-done = bf16[2048,2,1024]{2,1,0:T(2,128)(2,1)} async-done(((bf16[256,2,1024]{2,1,0:T(2,128)(2,1)}), bf16[2048,2,1024]{2,1,0:T(2,128)(2,1)}) %all-gather.31.cloned.1.call-update) | async-done | bytes 8388624 | tf_op jit(solution)/shard_map/all_gather | solution.py:208
  474.3 10.4 copy.280
  484.7 72.5 %all-gather.29.cloned.1.call-done = bf16[1024,2048]{1,0:T(8,128)(2,1)} async-done(((bf16[256,2048]{1,0:T(8,128)(2,1)}), bf16[1024,2048]{1,0:T(8,128)(2,1)}) %all-gather.29.cloned.1.call-update) | async-done | bytes 4194320 | tf_op jit(solution)/shard_map/all_gather | solution.py:306
  557.2 14.6 fusion.148
  571.8 66.4 %all-gather.35.cloned.1.call-done = bf16[1024,2048]{1,0:T(8,128)(2,1)} async-done(((bf16[256,2048]{1,0:T(8,128)(2,1)}), bf16[1024,2048]{1,0:T(8,128)(2,1)}) %all-gather.35.cloned.1.call-update) | async-done | bytes 4194320 | tf_op jit(solution)/shard_map/all_gather | solution.py:319
  638.2 37.9 %all-gather.33.cloned.1.call-done = bf16[1024,2048]{1,0:T(8,128)(2,1)} async-done(((bf16[1024,256]{1,0:T(8,128)(2,1)}), bf16[1024,2048]{1,0:T(8,128)(2,1)}) %all-gather.33.cloned.1.call-update) | async-done | bytes 4194320 | tf_op jit(solution)/shard_map/all_gather | solution.py:209
  676.0 13.2 fusion.70
  692.7 12.7 convolution_convert_fusion.2
  705.7 76.6 %reduce-scatter.27.cloned.1.call-done = bf16[256,2048]{1,0:T(8,128)(2,1)} async-done(((bf16[1024,2048]{1,0:T(8,128)(2,1)}), bf16[256,2048]{1,0:T(8,128)(2,1)}) %reduce-scatter.27.cloned.1.call-update) | async-done | bytes 1048592 | tf_op jit(solution)/shard_map/reduce_scatter | solution.py:323
  793.6 6.5 copy.236
  800.1 69.7 %all-gather.37.cloned.1.call-done = bf16[1024,2048]{1,0:T(8,128)(2,1)} async-done(((bf16[256,2048]{1,0:T(8,128)(2,1)}), bf16[1024,2048]{1,0:T(8,128)(2,1)}) %all-gather.37.cloned.1.call-update) | async-done | bytes 4194320 | tf_op jit(solution)/shard_map/all_gather | solution.py:331
  869.8 10.2 multiply_reduce_fusion.7
  879.9 9.4 psum.15
  889.3 7.4 multiply_reduce_fusion.8
  899.1 56.3 %fusion.8 = (f32[12,1024]{1,0:T(8,128)S(1)}, f32[12,1024]{1,0:T(8,128)S(1)}, f32[12,1024]{1,0:T(8,128)S(1)}, f32[1024,1024]{1,0:T(8,128)S(1)}) fusion(f32[12,1024]{1,0:T(8,128)S(1)} %get-tuple-element.278, f32[12,1024]{1,0:T(8,128)S(1)} %bitcast.275, f32[1024,1024]{1,0:T(8,128)} %fusion.73, pred[1024,1024]{1,0:T(8,128)(4,1)} %copy.211, ...), kind=kOutput, calls=%fused_computation.10 | convolution fusion | flops 9851334656 | bytes 14401536 | tf_op jit(solution)/shard_map/while/body/eval_jaxpr/transpose(jvp(hts,shp->thp))/dot_general | solution.py:97
  958.7 5.7 fusion.75
  974.1 49.4 %bitcast_add_fusion = f32[1024,12,64]{0,2,1:T(8,128)} fusion(f32[1024,12,64]{0,2,1:T(8,128)} %bitcast.235, f32[12,64,1024]{2,1,0:T(8,128)} %bitcast.234, f32[12,1024]{1,0:T(8,128)S(1)} %get-tuple-element.278, f32[12,1024]{1,0:T(8,128)S(1)} %bitcast.276, f32[1024,1024]{1,0:T(8,128)} %fusion.73, pred[1024,1024]{1,0:T(8,128)(4,1)S(1)} %copy-done.45, ...), kind=kOutput, calls=%fused_computation.93 | convolution fusion | flops 9728163840 | bytes 14778416 | tf_op jit(solution)/shard_map/while/body/eval_jaxpr/transpose(jvp(hts,shp->thp))/dot_general | solution.py:97
  1027.2 7.1 multiply_reduce_fusion.6
  1034.3 8.0 multiply_reduce_fusion.5
  1042.3 5.3 slice_multiply_fusion
  1062.3 9.4 multiply_reduce_fusion.3
  1080.9 8.3 convolution_convert_fusion.3
  1089.4 14.9 reduce-window.16
  1121.0 7.2 convolution_convert_fusion.5
  1128.9 105.0 %all-reduce.42.cloned.1.call-done = (bf16[8,4,64,512]{3,2,1,0:T(8,128)(2,1)}, bf16[8,4,64,512]{3,2,1,0:T(8,128)(2,1)}) async-done(((bf16[8,4,64,512]{3,2,1,0:T(8,128)(2,1)}, bf16[8,4,64,512]{3,2,1,0:T(8,128)(2,1)}), (bf16[8,4,64,512]{3,2,1,0:T(8,128)(2,1)}, bf16[8,4,64,512]{3,2,1,0:T(8,128)(2,1)})) %all-reduce.42.cloned.1.call-update) | async-done | bytes 4194320
  1236.5 15.2 convolution_convert_fusion
  1251.7 21.7 %copy.245 = bf16[2048,2,1024]{2,1,0:T(2,128)(2,1)} copy(bf16[2048,2,1024]{0,2,1:T(8,128)(2,1)} %bitcast.225) | data formatting | bytes 16777216 | tf_op jit(solution)/shard_map/convert_element_type | solution.py:537
  1277.3 11.6 convolution_convert_fusion.1
  1288.8 16.3 copy.238
  1305.3 9.4 convolution_convert_fusion.4
  1315.7 6.0 fusion.149
  1321.8 5.8 fusion.68
  1327.6 5.7 fusion.150
  1333.4 9.0 fusion.52
  1342.4 16.2 fusion.24
  1358.6 5.8 fusion.25
  1369.2 16.3 all-reduce.35
  1388.0 23.2 %all-reduce.33 = (bf16[8,1,64]{2,1,0:T(2,128)(2,1)S(1)}, bf16[5,8,1,16]{3,0,2,1:T(8,128)(2,1)S(1)}, bf16[8,3,12]{2,1,0:T(4,128)(2,1)S(1)}, bf16[12,64]{1,0:T(8,128)(2,1)S(1)}, bf16[8,1,64]{2,1,0:T(2,128)(2,1)S(1)}) all-reduce(bf16[8,1,64]{2,1,0:T(2,128)(2,1)S(1)} %copy.235, ...), channel_id=7, replica_groups=mesh['dp'=8,'tensor'=4] {'dp'}, use_global_device_ids=true, to_apply=%region_26.27.clone | all-reduce | flops 2720 | bytes 10880
  1421.1 37.9 %reduce-scatter.35.cloned.1.call-done = bf16[256,256]{1,0:T(8,128)(2,1)} async-done(((bf16[256,2048]{1,0:T(8,128)(2,1)}), bf16[256,256]{1,0:T(8,128)(2,1)}) %reduce-scatter.35.cloned.1.call-update) | async-done | bytes 131088 | tf_op jit(solution)/shard_map/reduce_scatter | solution.py:500
  1460.7 48.4 %reduce-scatter.43.cloned.1.call-done = bf16[768,256]{1,0:T(8,128)(2,1)} async-done(((bf16[768,2048]{1,0:T(8,128)(2,1)}), bf16[768,256]{1,0:T(8,128)(2,1)}) %reduce-scatter.43.cloned.1.call-update) | async-done | bytes 393232 | tf_op jit(solution)/shard_map/reduce_scatter | solution.py:515
  1511.0 35.3 %reduce-scatter.33.cloned.1.call-done = bf16[1,1,64,512]{3,2,1,0:T(8,128)(2,1)} async-done(((bf16[8,1,64,512]{3,2,1,0:T(8,128)(2,1)}), bf16[1,1,64,512]{3,2,1,0:T(8,128)(2,1)}) %reduce-scatter.33.cloned.1.call-update) | async-done | bytes 65552 | tf_op jit(solution)/shard_map/reduce_scatter | solution.py:527
  1547.9 35.9 %reduce-scatter.37.cloned.1.call-done = bf16[1,1,64,512]{3,2,1,0:T(8,128)(2,1)} async-done(((bf16[8,1,64,512]{3,2,1,0:T(8,128)(2,1)}), bf16[1,1,64,512]{3,2,1,0:T(8,128)(2,1)}) %reduce-scatter.37.cloned.1.call-update) | async-done | bytes 65552 | tf_op jit(solution)/shard_map/reduce_scatter | solution.py:530
  1585.3 197.8 %all-reduce.40.cloned.1.call-done = (bf16[2048,2,768]{2,1,0:T(2,128)(2,1)}, bf16[2048,2,1024]{2,1,0:T(2,128)(2,1)}) async-done(((bf16[2048,2,768]{2,1,0:T(2,128)(2,1)}, bf16[2048,2,1024]{2,1,0:T(2,128)(2,1)}), (bf16[2048,2,768]{2,1,0:T(2,128)(2,1)}, bf16[2048,2,1024]{2,1,0:T(2,128)(2,1)})) %all-reduce.40.cloned.1.call-update) | async-done | bytes 14680080
  1789.2 73.1 %reduce-scatter.25.cloned.1.call-done = bf16[256,2048]{1,0:T(8,128)(2,1)} async-done(((bf16[1024,2048]{1,0:T(8,128)(2,1)}), bf16[256,2048]{1,0:T(8,128)(2,1)}) %reduce-scatter.25.cloned.1.call-update) | async-done | bytes 1048592 | tf_op jit(solution)/shard_map/reduce_scatter | solution.py:311
  1862.3 79.4 %reduce-scatter.29.cloned.1.call-done = bf16[256,2048]{1,0:T(8,128)(2,1)} async-done(((bf16[1024,2048]{1,0:T(8,128)(2,1)}), bf16[256,2048]{1,0:T(8,128)(2,1)}) %reduce-scatter.29.cloned.1.call-update) | async-done | bytes 1048592 | tf_op jit(solution)/shard_map/reduce_scatter | solution.py:433
  (456 shorter events, 191.3 us)
Async XLA Ops:
  7.2 32.6 %copy-start.62 = (s32[1024]{0:T(1024)S(1)}, s32[1024]{0:T(1024)}, u32[]{:S(2)}) copy-start(s32[1024]{0:T(1024)} %param.19) | copy-start | bytes 12292
  7.2 30.5 %copy-start.99 = (bf16[12,64]{1,0:T(8,128)(2,1)S(1)}, bf16[12,64]{1,0:T(8,128)(2,1)}, u32[]{:S(2)}) copy-start(bf16[12,64]{1,0:T(8,128)(2,1)} %param.31) | copy-start | bytes 4612
  7.2 30.5 %copy-start.98 = (bf16[5,512]{1,0:T(8,128)(2,1)S(1)}, bf16[5,512]{1,0:T(8,128)(2,1)}, u32[]{:S(2)}) copy-start(bf16[5,512]{1,0:T(8,128)(2,1)} %param.29) | copy-start | bytes 15364
  7.2 85.9 %all-gather.15.cloned.1.call-start = ((), (), s32[]{:S(2)}) async-start(), calls=%async_computation.13 | async-start | bytes 5242880 | tf_op jit(solution)/shard_map/all_gather | solution.py:218
  8.0 113.5 %all-gather.17.cloned.1.call-start = ((), (), s32[]{:S(2)}) async-start(), calls=%async_computation.14 | async-start | bytes 2359296 | tf_op jit(solution)/shard_map/all_gather | solution.py:201
  8.7 138.2 %all-gather.19.cloned.1.call-start = ((), (), s32[]{:S(2)}) async-start(), calls=%async_computation.15 | async-start | bytes 1179648 | tf_op jit(solution)/shard_map/all_gather | solution.py:200
  9.4 167.1 %all-gather.25.cloned.1.call-start = ((), (), s32[]{:S(2)}) async-start(), calls=%async_computation.18 | async-start | bytes 2359296 | tf_op jit(solution)/shard_map/all_gather | solution.py:204
  10.0 213.8 %all-gather.23.cloned.1.call-start = ((), (), s32[]{:S(2)}) async-start(), calls=%async_computation.17 | async-start | bytes 7077888 | tf_op jit(solution)/shard_map/all_gather | solution.py:203
  10.6 315.7 %all-gather.27.cloned.1.call-start = ((), (), s32[]{:S(2)}) async-start(), calls=%async_computation.19 | async-start | bytes 3538944 | tf_op jit(solution)/shard_map/all_gather | solution.py:206
  11.2 324.9 %all-gather.21.cloned.1.call-start = ((), (), s32[]{:S(2)}) async-start(), calls=%async_computation.16 | async-start | bytes 1179648 | tf_op jit(solution)/shard_map/all_gather | solution.py:202
  11.9 405.4 %reduce-scatter.23.cloned.1.call-start = ((), (), s32[]{:S(2)}) async-start(), calls=%async_computation.20 | async-start | bytes 5242880 | tf_op jit(solution)/shard_map/reduce_scatter | solution.py:295
  23.0 73.4 %copy-start.57 = (f32[8,1,256]{2,1,0:T(1,128)}, f32[8,1,256]{2,1,0:T(1,128)S(1)}, u32[]{:S(2)}) copy-start(f32[8,1,256]{2,1,0:T(1,128)S(1)} %convert_element_type.377) | copy-start | bytes 24580
  32.1 96.7 %copy-start.50 = (bf16[2048,12]{0,1:T(8,128)(2,1)}, bf16[2048,12]{0,1:T(8,128)(2,1)S(1)}, u32[]{:S(2)}) copy-start(bf16[2048,12]{0,1:T(8,128)(2,1)S(1)} %all_gather.52) | copy-start | bytes 147460
  32.9 95.9 %copy-start.96 = (f32[12]{0:T(128)}, f32[12]{0:T(128)S(1)}, u32[]{:S(2)}) copy-start(f32[12]{0:T(128)S(1)} %get-tuple-element.288) | copy-start | bytes 148
  32.9 231.6 %copy-start.101 = (f32[12]{0:T(128)}, f32[12]{0:T(128)S(1)}, u32[]{:S(2)}) copy-start(f32[12]{0:T(128)S(1)} %get-tuple-element.286) | copy-start | bytes 148
  35.1 65.0 %copy-start.33 = (pred[1024,1024]{0,1:T(8,128)(4,1)}, pred[1024,1024]{0,1:T(8,128)(4,1)S(1)}, u32[]{:S(2)}) copy-start(pred[1024,1024]{0,1:T(8,128)(4,1)S(1)} %fusion.41) | copy-start | bytes 3145732
  37.7 851.6 %copy-start.92 = (f32[768]{0:T(1024)}, f32[768]{0:T(1024)S(1)}, u32[]{:S(2)}) copy-start(f32[768]{0:T(1024)S(1)} %reshape.477) | copy-start | bytes 9220
  37.8 206.1 %copy-start.66 = (f32[1280]{0:T(1024)}, f32[1280]{0:T(1024)S(1)}, u32[]{:S(2)}) copy-start(f32[1280]{0:T(1024)S(1)} %get-tuple-element.224) | copy-start | bytes 15364
  37.8 206.1 %copy-start.68 = (f32[1280]{0:T(1024)}, f32[1280]{0:T(1024)S(1)}, u32[]{:S(2)}) copy-start(f32[1280]{0:T(1024)S(1)} %get-tuple-element.221) | copy-start | bytes 15364
  37.8 206.1 %copy-start.70 = (f32[1280]{0:T(1024)}, f32[1280]{0:T(1024)S(1)}, u32[]{:S(2)}) copy-start(f32[1280]{0:T(1024)S(1)} %get-tuple-element.222) | copy-start | bytes 15364
  37.9 206.1 %copy-start.72 = (f32[1280]{0:T(1024)}, f32[1280]{0:T(1024)S(1)}, u32[]{:S(2)}) copy-start(f32[1280]{0:T(1024)S(1)} %get-tuple-element.223) | copy-start | bytes 15364
  39.8 114.2 %copy-start.26 = (f32[1024,64]{1,0:T(8,128)}, f32[1024,64]{1,0:T(8,128)S(1)}, u32[]{:S(2)}) copy-start(f32[1024,64]{1,0:T(8,128)S(1)} %get-tuple-element.279) | copy-start | bytes 786436
  39.8 114.2 %copy-start.28 = (f32[1024,64]{1,0:T(8,128)}, f32[1024,64]{1,0:T(8,128)S(1)}, u32[]{:S(2)}) copy-start(f32[1024,64]{1,0:T(8,128)S(1)} %get-tuple-element.280) | copy-start | bytes 786436
  39.9 204.1 %copy-start.74 = (f32[1024]{0:T(1024)}, f32[1024]{0:T(1024)S(1)}, u32[]{:S(2)}) copy-start(f32[1024]{0:T(1024)S(1)} %get-tuple-element.285) | copy-start | bytes 12292
  39.9 204.1 %copy-start.78 = (f32[1024]{0:T(1024)}, f32[1024]{0:T(1024)S(1)}, u32[]{:S(2)}) copy-start(f32[1024]{0:T(1024)S(1)} %get-tuple-element.283) | copy-start | bytes 12292
  39.9 204.2 %copy-start.80 = (f32[1024]{0:T(1024)}, f32[1024]{0:T(1024)S(1)}, u32[]{:S(2)}) copy-start(f32[1024]{0:T(1024)S(1)} %get-tuple-element.284) | copy-start | bytes 12292
  181.8 62.3 %copy-start.5 = (f32[1024,512]{1,0:T(8,128)}, f32[1024,512]{1,0:T(8,128)S(1)}, u32[]{:S(2)}) copy-start(f32[1024,512]{1,0:T(8,128)S(1)} %fusion.147) | copy-start | bytes 6291460
  264.5 42.1 %copy-start.42 = (bf16[1024,768]{0,1:T(8,128)(2,1)}, bf16[1024,768]{0,1:T(8,128)(2,1)S(1)}, u32[]{:S(2)}) copy-start(bf16[1024,768]{0,1:T(8,128)(2,1)S(1)} %copy.210) | copy-start | bytes 4718596
  326.3 563.0 %copy-start.90 = (f32[1024]{0:T(1024)}, f32[1024]{0:T(1024)S(1)}, u32[]{:S(2)}) copy-start(f32[1024]{0:T(1024)S(1)} %get-tuple-element.282) | copy-start | bytes 12292
  343.1 74.2 %copy-start.13 = (bf16[256,2048]{1,0:T(8,128)(2,1)S(1)}, bf16[256,2048]{1,0:T(8,128)(2,1)}, u32[]{:S(2)}) copy-start(bf16[256,2048]{1,0:T(8,128)(2,1)} %param.18) | copy-start | bytes 3145732
  343.2 131.1 %all-gather.31.cloned.1.call-start = ((), (), s32[]{:S(2)}) async-start(), calls=%async_computation.22 | async-start | bytes 9437184 | tf_op jit(solution)/shard_map/all_gather | solution.py:208
  343.9 213.3 %all-gather.29.cloned.1.call-start = ((), (), s32[]{:S(2)}) async-start(), calls=%async_computation.21 | async-start | bytes 5242880 | tf_op jit(solution)/shard_map/all_gather | solution.py:306
  352.8 432.3 %copy-start.60 = (f32[8,1,256]{2,1,0:T(1,128)}, f32[8,1,256]{2,1,0:T(1,128)S(1)}, u32[]{:S(2)}) copy-start(f32[8,1,256]{2,1,0:T(1,128)S(1)} %convert_element_type.378) | copy-start | bytes 24580
  419.0 366.1 %copy-start.86 = (f32[256]{0:T(256)}, f32[256]{0:T(256)S(1)}, u32[]{:S(2)}) copy-start(f32[256]{0:T(256)S(1)} %fusion.118) | copy-start | bytes 3076
  421.6 216.6 %all-gather.35.cloned.1.call-start = ((), (), s32[]{:S(2)}) async-start(), calls=%async_computation.25 | async-start | bytes 5242880 | tf_op jit(solution)/shard_map/all_gather | solution.py:319
  422.3 253.7 %all-gather.33.cloned.1.call-start = ((), (), s32[]{:S(2)}) async-start(), calls=%async_computation.23 | async-start | bytes 4718592 | tf_op jit(solution)/shard_map/all_gather | solution.py:209
  422.9 359.4 %reduce-scatter.27.cloned.1.call-start = ((), (), s32[]{:S(2)}) async-start(), calls=%async_computation.26 | async-start | bytes 5242880 | tf_op jit(solution)/shard_map/reduce_scatter | solution.py:323
  705.4 76.9 %copy-start.17 = (bf16[256,2048]{1,0:T(8,128)(2,1)S(1)}, bf16[256,2048]{1,0:T(8,128)(2,1)}, u32[]{:S(2)}) copy-start(bf16[256,2048]{1,0:T(8,128)(2,1)} %reduce-scatter.23.cloned.1.call-done) | copy-start | bytes 3145732
  705.4 79.8 %copy-start.22 = (bf16[256,2048]{1,0:T(8,128)(2,1)S(1)}, bf16[256,2048]{1,0:T(8,128)(2,1)}, u32[]{:S(2)}) copy-start(bf16[256,2048]{1,0:T(8,128)(2,1)} %param.20) | copy-start | bytes 3145732
  705.4 83.0 %copy-start.58 = (f32[8,1,256]{2,1,0:T(1,128)S(1)}, f32[8,1,256]{2,1,0:T(1,128)}, u32[]{:S(2)}) copy-start(f32[8,1,256]{2,1,0:T(1,128)} %copy-done.57) | copy-start | bytes 24580
  705.4 83.0 %copy-start.64 = (f32[1024]{0:T(1024)S(1)}, f32[1024]{0:T(1024)}, u32[]{:S(2)}) copy-start(f32[1024]{0:T(1024)} %copy-done.63) | copy-start | bytes 12292
  705.4 164.4 %all-gather.37.cloned.1.call-start = ((), (), s32[]{:S(2)}) async-start(), calls=%async_computation.27 | async-start | bytes 5242880 | tf_op jit(solution)/shard_map/all_gather | solution.py:331
  788.3 445.5 %all-reduce.42.cloned.1.call-start = ((), (), s32[]{:S(2)}) async-start(), calls=%async_computation.39 | async-start | bytes 8388608
  800.1 89.2 %copy-start.16 = (f32[1024,768]{1,0:T(8,128)S(1)}, f32[1024,768]{1,0:T(8,128)}, u32[]{:S(2)}) copy-start(f32[1024,768]{1,0:T(8,128)} %copy-done.15) | copy-start | bytes 9437188
  899.1 56.4 %copy-start.34 = (f32[1024,768]{0,1:T(8,128)}, f32[1024,768]{0,1:T(8,128)S(1)}, u32[]{:S(2)}) copy-start(f32[1024,768]{0,1:T(8,128)S(1)} %copy.222) | copy-start | bytes 9437188
  899.1 65.3 %copy-start.103 = (bf16[1024,2048]{1,0:T(8,128)(2,1)S(1)}, bf16[1024,2048]{1,0:T(8,128)(2,1)}, u32[]{:S(2)}) copy-start(bf16[1024,2048]{1,0:T(8,128)(2,1)} %all-gather.37.cloned.1.call-done) | copy-start | bytes 12582916
  1079.4 287.5 %reduce-scatter.45.cloned.1.call-start = ((), (), s32[]{:S(2)}) async-start(), calls=%async_computation.36 | async-start | bytes 4718592 | tf_op jit(solution)/shard_map/reduce_scatter | solution.py:539
  1089.3 298.0 %reduce-scatter.47.cloned.1.call-start = ((), (), s32[]{:S(2)}) async-start(), calls=%async_computation.37 | async-start | bytes 51200
  1109.2 307.5 %reduce-scatter.41.cloned.1.call-start = ((), (), s32[]{:S(2)}) async-start(), calls=%async_computation.34 | async-start | bytes 147456 | tf_op jit(solution)/shard_map/reduce_scatter | solution.py:509
  1110.2 307.8 %reduce-scatter.39.cloned.1.call-start = ((), (), s32[]{:S(2)}) async-start(), calls=%async_computation.33 | async-start | bytes 73728 | tf_op jit(solution)/shard_map/reduce_scatter | solution.py:506
  1110.9 308.6 %reduce-scatter.31.cloned.1.call-start = ((), (), s32[]{:S(2)}) async-start(), calls=%async_computation.29 | async-start | bytes 1179648 | tf_op jit(solution)/shard_map/reduce_scatter | solution.py:497
  1115.6 343.5 %reduce-scatter.35.cloned.1.call-start = ((), (), s32[]{:S(2)}) async-start(), calls=%async_computation.31 | async-start | bytes 1179648 | tf_op jit(solution)/shard_map/reduce_scatter | solution.py:500
  1121.0 388.2 %reduce-scatter.43.cloned.1.call-start = ((), (), s32[]{:S(2)}) async-start(), calls=%async_computation.35 | async-start | bytes 3538944 | tf_op jit(solution)/shard_map/reduce_scatter | solution.py:515
  1128.3 418.1 %reduce-scatter.33.cloned.1.call-start = ((), (), s32[]{:S(2)}) async-start(), calls=%async_computation.30 | async-start | bytes 589824 | tf_op jit(solution)/shard_map/reduce_scatter | solution.py:527
  1236.4 347.3 %reduce-scatter.37.cloned.1.call-start = ((), (), s32[]{:S(2)}) async-start(), calls=%async_computation.32 | async-start | bytes 589824 | tf_op jit(solution)/shard_map/reduce_scatter | solution.py:530
  1277.2 505.9 %all-reduce.40.cloned.1.call-start = ((), (), s32[]{:S(2)}) async-start(), calls=%async_computation.38 | async-start | bytes 29360128
  1305.1 557.1 %reduce-scatter.25.cloned.1.call-start = ((), (), s32[]{:S(2)}) async-start(), calls=%async_computation.24 | async-start | bytes 5242880 | tf_op jit(solution)/shard_map/reduce_scatter | solution.py:311
  1314.7 627.0 %reduce-scatter.29.cloned.1.call-start = ((), (), s32[]{:S(2)}) async-start(), calls=%async_computation.28 | async-start | bytes 5242880 | tf_op jit(solution)/shard_map/reduce_scatter | solution.py:433
  1369.0 572.7 %copy-start.14 = (bf16[256,2048]{1,0:T(8,128)(2,1)S(1)}, bf16[256,2048]{1,0:T(8,128)(2,1)}, u32[]{:S(2)}) copy-start(bf16[256,2048]{1,0:T(8,128)(2,1)} %param.18) | copy-start | bytes 3145732
  1369.0 572.7 %copy-start.18 = (bf16[256,2048]{1,0:T(8,128)(2,1)S(1)}, bf16[256,2048]{1,0:T(8,128)(2,1)}, u32[]{:S(2)}) copy-start(bf16[256,2048]{1,0:T(8,128)(2,1)} %reduce-scatter.23.cloned.1.call-done) | copy-start | bytes 3145732
  1369.0 572.7 %copy-start.23 = (bf16[256,2048]{1,0:T(8,128)(2,1)S(1)}, bf16[256,2048]{1,0:T(8,128)(2,1)}, u32[]{:S(2)}) copy-start(bf16[256,2048]{1,0:T(8,128)(2,1)} %param.20) | copy-start | bytes 3145732
  1369.0 572.7 %copy-start.61 = (f32[8,1,256]{2,1,0:T(1,128)S(1)}, f32[8,1,256]{2,1,0:T(1,128)}, u32[]{:S(2)}) copy-start(f32[8,1,256]{2,1,0:T(1,128)} %copy-done.60) | copy-start | bytes 24580
  1369.0 572.7 %copy-start.87 = (f32[256]{0:T(256)S(1)}, f32[256]{0:T(256)}, u32[]{:S(2)}) copy-start(f32[256]{0:T(256)} %copy-done.86) | copy-start | bytes 3076
  1369.0 572.7 %copy-start.95 = (f32[256]{0:T(256)S(1)}, f32[256]{0:T(256)}, u32[]{:S(2)}) copy-start(f32[256]{0:T(256)} %copy-done.94) | copy-start | bytes 3076
  (83 other events, 528.3 us)
Sparse Core Ops, SparseCore 0:
  9.6 83.4 all-gather.14
  95.0 26.4 all-gather.16
  123.4 23.4 all-gather.18
  148.6 27.8 all-gather.24
  178.3 45.5 all-gather.22
  225.6 32.8 all-gather.26
  260.3 23.5 all-gather.20
  343.3 73.9 reduce-scatter.22
  419.4 54.8 all-gather.30
  476.4 80.7 all-gather.28
  558.8 79.2 all-gather.34
  640.0 35.9 all-gather.32
  705.5 76.7 reduce-scatter.26
  788.5 81.2 all-gather.36
  1079.5 154.3 all-reduce.41
  1237.5 50.3 reduce-scatter.44
  1290.5 18.5 reduce-scatter.46
  1312.8 31.4 reduce-scatter.40
  1347.9 31.4 reduce-scatter.38
  1383.3 36.1 reduce-scatter.30
  1423.0 36.0 reduce-scatter.34
  1462.8 46.2 reduce-scatter.42
  1512.2 34.1 reduce-scatter.32
  1549.6 34.1 reduce-scatter.36
  1587.5 195.5 all-reduce.39
  1785.4 76.8 reduce-scatter.24
  1864.4 77.2 reduce-scatter.28
where the time goes:
time: 1960 us; the launch traced here: 1950 us
  waiting for transfers between devices  1200 us (61%)
  matrix products  383 us (20%)
  other arithmetic  147 us (8%)
  local copies, waits for them, and re-layouts  119 us (6%)
  blocking collectives  88.8 us (5%)
    unnamed x30, waiting for transfers between devices  309 us
    dot_general x3, matrix products, state_space(): jnp.einsum('hts,shp->thp', mixing, inner_x, precision=PRECISION_HIGH)  148 us
    dot_general x9, matrix products, mat_nt(): lax.dot_general(left_side, right_side, (((1,), (1,)), ((), ())), preferre...  80.1 us
    reduce_scatter x1, waiting for transfers between devices, per_device(): lax.psum_scatter(grad_tokens_part.astype(jnp.bfloat16), 'tensor', scatter...  79.4 us
    reduce_scatter x1, waiting for transfers between devices, per_device(): lax.psum_scatter(mat_nt(grad_hidden, expand_flat).astype(jnp.bfloat16), '...  76.6 us
    reduce_scatter x1, waiting for transfers between devices, per_device(): lax.psum_scatter(matrix_plain_product(act_low, shrink_full).astype(jnp.bf...  73.1 us
    all_gather x1, waiting for transfers between devices, per_device(): lax.all_gather(second_val.astype(jnp.bfloat16), 'tensor', axis=0, tiled=T...  72.5 us
    all_gather x1, waiting for transfers between devices, per_device(): lax.all_gather(grad_middle.astype(jnp.bfloat16), 'tensor', axis=0, tiled=...  69.7 us
  transfers between devices with their start and end apart: 27, of which 21 were waited for; matrix products, arithmetic and copies ran while one was open for 20% of the time, Pallas kernels for 0%

commit v1 on v0

v1 whole, which is shorter than its diff:
```python
import functools
import math

import jax
import jax.numpy as jnp
from jax import lax
from jax.experimental import pallas as pl
from jax.experimental.pallas import tpu as pltpu
from jax.sharding import PartitionSpec as P

QUERY_HEADS = 8
KEY_HEADS = 2
HEAD_SIZE = 128
PM = 64
NS = 256
KC = 4
SEQ_LEN = 1024
DSSM = 3072
LANES = 128
CHUNK = 128
FAR = -1e30


EPS = 1e-05
THETA = 100000000000.0
HIGH = lax.Precision.HIGHEST
F32 = jnp.float32
BF16 = jnp.bfloat16


def mat(left_side, right_side):
    return jnp.dot(left_side, right_side, preferred_element_type=F32)


def mat_nt(left_side, right_side):
    return lax.dot_general(
        left_side, right_side, (((1,), (1,)), ((), ())), preferred_element_type=F32
    )


def mat_tn(left_side, right_side):
    return lax.dot_general(
        left_side, right_side, (((0,), (0,)), ((), ())), preferred_element_type=F32
    )


def iota(shape, dim):
    return lax.broadcasted_iota(jnp.int32, shape, dim)


def halves(value):
    high = value.astype(BF16)
    return high, (value - high.astype(F32)).astype(BF16)


def spread(value, heads_map):
    high, rest = halves(value)
    return mat(high, heads_map) + mat(rest, heads_map)


def gather_heads(value, heads_map):
    high, rest = halves(value)
    return mat_nt(high, heads_map) + mat_nt(rest, heads_map)


def sigmoid(value):
    return 1.0 / (1.0 + jnp.exp(-value))


def softplus(value):
    return jnp.maximum(value, 0.0) + jnp.log(1.0 + jnp.exp(-jnp.abs(value)))


def conv_rows(inputs, before, seg, seg_before, weight):
    rows = inputs.shape[0]
    longer = jnp.concatenate([before, inputs], 0)
    seg_longer = jnp.concatenate([seg_before, seg], 0)
    result = weight[KC : KC + 1] + weight[KC - 1 : KC] * inputs
    moved_list = []
    for lag in range(1, KC):
        keep = seg_longer[8 - lag : 8 - lag + rows] == seg
        moved = jnp.where(keep, longer[8 - lag : 8 - lag + rows], 0.0)
        moved_list.append(moved)
        result = result + weight[KC - 1 - lag : KC - lag] * moved
    return result, moved_list


def chunk_decay(step_lin, heads_vec, heads, seg, seg_last_before):
    rows = step_lin.shape[0]
    head_lane = iota((1, LANES), 1) < heads
    shifted = step_lin + heads_vec[1:2]
    step = jnp.where(head_lane, softplus(shifted), 0.0)
    rate = jnp.exp(heads_vec[0:1])
    log_decay = -step * rate
    lower = (iota((rows, rows), 0) >= iota((rows, rows), 1)).astype(F32)
    running = jnp.dot(lower, log_decay, precision=HIGH, preferred_element_type=F32)
    last = running[rows - 1 : rows]
    seg_last = seg[rows - 1 : rows]
    into = jnp.where(seg == seg_last_before, jnp.exp(running), 0.0)
    out = jnp.where(seg == seg_last, jnp.exp(last - running), 0.0)
    across = jnp.where(seg_last == seg_last_before, jnp.exp(last), 0.0)
    return shifted, step, rate, log_decay, running, into, out, across


def two_heads(pair):
    front = iota(pair.shape, 1) < PM
    nothing = jnp.zeros_like(pair)
    return jnp.concatenate(
        [jnp.where(front, pair, nothing), jnp.where(front, nothing, pair)], 0
    )


def pair_decay(running, running_t, bias, index):
    parts = []
    for head in (2 * index, 2 * index + 1):
        gap = running[:, head : head + 1] - running_t[head : head + 1, :] + bias
        parts.append(jnp.exp(gap))
    return parts


def as_column(row):
    return jnp.broadcast_to(row, (8, row.shape[1])).T[:, 0:1]


def row_sums_as_row(values):
    return jnp.sum(values.T, 0, keepdims=True)


def chunk_bias(seg, seg_row):
    rows = seg.shape[0]
    allowed = (iota((rows, rows), 0) >= iota((rows, rows), 1)) & (seg == seg_row)
    return jnp.where(allowed, 0.0, FAR)


def mixer_forward_kernel(
    heads, lin_ref, seg_ref, segr_ref, conv_ref, hp_ref, map_ref,
    ssm_ref, mixed_ref, sums_ref, states_ref, state, tail, seg_tail,
):
    channels = heads * PM
    rows = lin_ref.shape[0]

    @pl.when(lax.rem(pl.program_id(0), SEQ_LEN // CHUNK) == 0)
    def _():
        state[...] = jnp.zeros_like(state)
        tail[...] = jnp.zeros_like(tail)
        seg_tail[...] = jnp.full_like(seg_tail, -1)

    heads_map = map_ref[...]
    seg = seg_ref[...]
    seg_before = seg_tail[...]
    inputs = lin_ref[:, channels : 2 * channels + 2 * NS]
    conv, _ = conv_rows(inputs, tail[...], seg, seg_before, conv_ref[...])
    mixed = (conv * sigmoid(conv)).astype(BF16)
    mixed_ref[...] = mixed
    tail[...] = inputs[rows - 8 :]
    seg_tail[...] = seg[rows - 8 :]

    step_lin = lin_ref[:, 2 * channels + 2 * NS :]
    _, step, _, _, running, into, out, across = chunk_decay(
        step_lin, hp_ref[...], heads, seg, seg_before[7:8]
    )
    inner = mixed[:, :channels].astype(F32)
    state_b = mixed[:, channels : channels + NS]
    state_c = mixed[:, channels + NS :]
    few = jnp.concatenate([across, hp_ref[2:3], jnp.zeros((6, LANES), F32)], 0)
    wide = spread(jnp.concatenate([step, into, out, few], 0), heads_map)
    stepped = (inner * wide[:rows]).astype(BF16)
    leaving = (stepped.astype(F32) * wide[2 * rows : 3 * rows]).astype(BF16)
    held = state[...]
    held_low = held.astype(BF16)
    states_ref[0] = held_low
    base = wide[rows : 2 * rows] * mat(state_c, held_low) + wide[3 * rows + 1 : 3 * rows + 2] * inner
    state[...] = wide[3 * rows : 3 * rows + 1] * held + mat_tn(state_b, leaving)

    gram = mat_nt(state_c, state_b)
    bias = chunk_bias(seg, segr_ref[...])
    running_t = running.T
    total = jnp.zeros((rows, LANES), F32)
    for index in range(heads // 2):
        cols = slice(index * LANES, (index + 1) * LANES)
        first, second = pair_decay(running, running_t, bias, index)
        mixing = jnp.concatenate([first * gram, second * gram], 1).astype(BF16)
        outcome = mat(mixing, two_heads(stepped[:, cols])) + base[:, cols]
        ssm_ref[:, cols] = outcome
        gate = lin_ref[:, cols]
        gated = outcome * gate * sigmoid(gate)
        total = total + gated * gated
    sums_ref[0] = row_sums_as_row(total)


def mixer_backward_kernel(
    heads, lin_ref, before_ref, seg_ref, segb_ref, segr_ref, conv_ref, hp_ref, map_ref, gain_ref,
    gn_ref, inv_ref, cross_ref, ssm_ref, mixed_ref, states_ref,
    dlin_ref, dconv_ref, dhp_ref, dgain_ref, dstate, dnext, seg_next,
):
    channels = heads * PM
    rows = lin_ref.shape[0]
    chunks = SEQ_LEN // CHUNK
    chunk = pl.num_programs(0) - 1 - pl.program_id(0)
    place = lax.rem(chunk, chunks)

    @pl.when(pl.program_id(0) == 0)
    def _():
        dconv_ref[...] = jnp.zeros_like(dconv_ref)
        dhp_ref[...] = jnp.zeros_like(dhp_ref)
        dgain_ref[...] = jnp.zeros_like(dgain_ref)

    @pl.when(place == chunks - 1)
    def _():
        dstate[...] = jnp.zeros_like(dstate)
        dnext[...] = jnp.zeros_like(dnext)
        seg_next[...] = jnp.full_like(seg_next, -1)

    heads_map = map_ref[...]
    seg = seg_ref[...]
    seg_before = jnp.where(place == 0, -1, segb_ref[...])

    gate = lin_ref[:, :channels]
    sig = sigmoid(gate)
    silu = gate * sig
    ssm = ssm_ref[...]
    gated = ssm * silu
    grad_normed = gn_ref[...]
    inverse = as_column(inv_ref[0])
    dgain_ref[0:1] += jnp.sum(gated * inverse * grad_normed, 0, keepdims=True)
    cube = inverse * inverse * inverse * (as_column(cross_ref[0]) * (1.0 / DSSM))
    grad_gated = inverse * (grad_normed * gain_ref[...]) - gated * cube
    grad_out = grad_gated * silu
    grad_gate = grad_gated * ssm * (sig * (1.0 + gate * (1.0 - sig)))
    dlin_ref[:, :channels] = grad_gate.astype(BF16)
    grad_low = grad_out.astype(BF16)

    step_lin = lin_ref[:, 2 * channels + 2 * NS :]
    shifted, step, rate, log_decay, running, into, out, across = chunk_decay(
        step_lin, hp_ref[...], heads, seg, seg_before[7:8]
    )
    mixed = mixed_ref[...]
    inner = mixed[:, :channels].astype(F32)
    state_b = mixed[:, channels : channels + NS]
    state_c = mixed[:, channels + NS :]
    few = jnp.concatenate([across, hp_ref[2:3], jnp.zeros((6, LANES), F32)], 0)
    wide = spread(jnp.concatenate([step, into, out, few], 0), heads_map)
    step_wide = wide[:rows]
    out_wide = wide[2 * rows : 3 * rows]
    skip_wide = wide[3 * rows + 1 : 3 * rows + 2]
    stepped = (inner * step_wide).astype(BF16)
    stepped_wide = stepped.astype(F32)
    leaving = (stepped_wide * out_wide).astype(BF16)

    held = states_ref[0]
    grad_state = dstate[...]
    grad_state_low = grad_state.astype(BF16)
    grad_leaving = mat(state_b, grad_state_low)
    grad_b = mat_nt(leaving, grad_state_low)
    entering = wide[rows : 2 * rows] * grad_out
    entering_low = entering.astype(BF16)
    grad_c = mat_nt(entering_low, held)
    carried = mat(state_c, held)
    dstate[...] = wide[3 * rows : 3 * rows + 1] * grad_state + mat_tn(state_c, entering_low)
    grad_across = jnp.sum(grad_state * held.astype(F32), 0, keepdims=True)

    gram = mat_nt(state_c, state_b)
    bias = chunk_bias(seg, segr_ref[...])
    running_t = running.T
    head_lane = iota((1, LANES), 1)
    head_row = iota((LANES, 1), 0)
    grad_gram = jnp.zeros((rows, rows), F32)
    row_sums = jnp.zeros((rows, LANES), F32)
    column_sums = jnp.zeros((LANES, rows), F32)
    grad_stepped = []
    for index in range(heads // 2):
        cols = slice(index * LANES, (index + 1) * LANES)
        grads = mat_nt(grad_low[:, cols], two_heads(stepped[:, cols]))
        mixings = []
        for side, decay in enumerate(pair_decay(running, running_t, bias, index)):
            part = grads[:, side * rows : (side + 1) * rows] * decay
            grad_gram = grad_gram + part
            part = part * gram
            head = 2 * index + side
            row_sums = jnp.where(head_lane == head, jnp.sum(part, 1, keepdims=True), row_sums)
            column_sums = jnp.where(head_row == head, jnp.sum(part, 0, keepdims=True), column_sums)
            mixings.append((decay * gram).astype(BF16))
        both = mat_tn(jnp.concatenate(mixings, 1), grad_low[:, cols])
        front = iota((rows, LANES), 1) < PM
        grad_stepped.append(jnp.where(front, both[:rows], both[rows:]))
    grad_gram_low = grad_gram.astype(BF16)
    grad_c = grad_c + mat(grad_gram_low, state_b)
    grad_b = grad_b + mat_tn(grad_gram_low, state_c)
    grad_stepped = jnp.concatenate(grad_stepped, 1) + out_wide * grad_leaving
    grad_inner = grad_stepped * step_wide + skip_wide * grad_out

    few = jnp.concatenate([grad_across, jnp.zeros((7, channels), F32)], 0)
    sums = gather_heads(
        jnp.concatenate(
            [stepped_wide * grad_leaving, entering * carried, grad_stepped * inner, grad_out * inner, few], 0
        ),
        heads_map,
    )
    leave = sums[:rows] * out
    grad_running = row_sums - column_sums.T + sums[rows : 2 * rows] - leave
    grad_last = jnp.sum(leave, 0, keepdims=True) + sums[4 * rows : 4 * rows + 1] * across
    grad_running = grad_running + jnp.where(iota((rows, 1), 0) == rows - 1, grad_last, 0.0)
    upper = (iota((rows, rows), 0) <= iota((rows, rows), 1)).astype(F32)
    grad_log = jnp.dot(upper, grad_running, precision=HIGH, preferred_element_type=F32)
    grad_step = sums[2 * rows : 3 * rows] - grad_log * rate
    grad_shifted = jnp.where(head_lane < heads, grad_step * sigmoid(shifted), 0.0)
    first_spare = 2 * channels + 2 * NS + LANES
    dlin_ref[:, first_spare - LANES : first_spare] = grad_shifted.astype(BF16)
    dlin_ref[:, first_spare:] = jnp.zeros((rows, dlin_ref.shape[1] - first_spare), BF16)
    dhp_ref[0:1] += jnp.sum(grad_log * log_decay, 0, keepdims=True)
    dhp_ref[1:2] += jnp.sum(grad_shifted, 0, keepdims=True)
    dhp_ref[2:3] += jnp.sum(sums[3 * rows : 4 * rows], 0, keepdims=True)

    grad_mixed = jnp.concatenate([grad_inner, grad_b, grad_c], 1)
    weight = conv_ref[...]
    inputs = lin_ref[:, channels : 2 * channels + 2 * NS]
    before = before_ref[:, channels : 2 * channels + 2 * NS]
    conv, moved_list = conv_rows(inputs, before, seg, seg_before, weight)
    sig = sigmoid(conv)
    grad_conv = grad_mixed * (sig * (1.0 + conv * (1.0 - sig)))
    dconv_ref[KC : KC + 1] += jnp.sum(grad_conv, 0, keepdims=True)
    dconv_ref[KC - 1 : KC] += jnp.sum(grad_conv * inputs, 0, keepdims=True)
    longer = jnp.concatenate([grad_conv, dnext[...]], 0)
    seg_longer = jnp.concatenate([seg, seg_next[...]], 0)
    grad_inputs = weight[KC - 1 : KC] * grad_conv
    for lag in range(1, KC):
        tap = slice(KC - 1 - lag, KC - lag)
        dconv_ref[tap] += jnp.sum(grad_conv * moved_list[lag - 1], 0, keepdims=True)
        keep = seg_longer[lag : lag + rows] == seg
        grad_inputs = grad_inputs + weight[tap] * jnp.where(keep, longer[lag : lag + rows], 0.0)
    dlin_ref[:, channels : 2 * channels + 2 * NS] = grad_inputs.astype(BF16)
    dnext[...] = grad_conv[:8]
    seg_next[...] = seg[:8]


def whole_block(array):
    return pl.BlockSpec(array.shape, lambda *_: (0,) * array.ndim)


def mixer_forward(lin, seg, conv_weight, heads_vec, heads_map, heads):
    total = lin.shape[0]
    channels = heads * PM
    width = 2 * channels + 2 * NS + LANES
    mixed_width = channels + 2 * NS
    steps = total // CHUNK
    by_rows = lambda cols: pl.BlockSpec((CHUNK, cols), lambda c: (c, 0))
    return pl.pallas_call(
        functools.partial(mixer_forward_kernel, heads),
        grid=(steps,),
        in_specs=[
            by_rows(width),
            by_rows(1),
            pl.BlockSpec((1, CHUNK), lambda c: (0, c)),
            whole_block(conv_weight),
            whole_block(heads_vec),
            whole_block(heads_map),
        ],
        out_specs=[
            by_rows(channels),
            by_rows(mixed_width),
            pl.BlockSpec((1, 1, CHUNK), lambda c: (c, 0, 0)),
            pl.BlockSpec((1, NS, channels), lambda c: (c, 0, 0)),
        ],
        out_shape=[
            jax.ShapeDtypeStruct((total, channels), F32),
            jax.ShapeDtypeStruct((total, mixed_width), BF16),
            jax.ShapeDtypeStruct((steps, 1, CHUNK), F32),
            jax.ShapeDtypeStruct((steps, NS, channels), BF16),
        ],
        scratch_shapes=[
            pltpu.VMEM((NS, channels), F32),
            pltpu.VMEM((8, mixed_width), F32),
            pltpu.VMEM((8, 1), jnp.int32),
        ],
        compiler_params=pltpu.CompilerParams(vmem_limit_bytes=48 << 20),
        name="mixer_forward",
    )(lin, seg.reshape(total, 1), seg.reshape(1, total), conv_weight, heads_vec, heads_map)


def mixer_backward(
    lin, seg, conv_weight, heads_vec, heads_map, gain, grad_normed, inverse, cross, ssm, mixed, states, heads, lead
):
    total = lin.shape[0]
    channels = heads * PM
    width = 2 * channels + 2 * NS + LANES
    mixed_width = channels + 2 * NS
    steps = total // CHUNK
    by_rows = lambda cols: pl.BlockSpec((CHUNK, cols), lambda c: (steps - 1 - c, 0))
    ahead = lambda cols: pl.BlockSpec(
        (8, cols), lambda c: (jnp.maximum((steps - 1 - c) * (CHUNK // 8) - 1, 0), 0)
    )
    seg_column = seg.reshape(total, 1)
    return pl.pallas_call(
        functools.partial(mixer_backward_kernel, heads),
        grid=(steps,),
        in_specs=[
            by_rows(width),
            ahead(width),
            by_rows(1),
            ahead(1),
            pl.BlockSpec((1, CHUNK), lambda c: (0, steps - 1 - c)),
            whole_block(conv_weight),
            whole_block(heads_vec),
            whole_block(heads_map),
            whole_block(gain),
            by_rows(channels),
            pl.BlockSpec((1, 1, CHUNK), lambda c: (steps - 1 - c, 0, 0)),
            pl.BlockSpec((1, 1, CHUNK), lambda c: (steps - 1 - c, 0, 0)),
            by_rows(channels),
            by_rows(mixed_width),
            pl.BlockSpec((1, NS, channels), lambda c: (steps - 1 - c, 0, 0)),
        ],
        out_specs=[
            by_rows(lead),
            pl.BlockSpec((8, mixed_width), lambda c: (0, 0)),
            pl.BlockSpec((8, LANES), lambda c: (0, 0)),
            pl.BlockSpec((8, channels), lambda c: (0, 0)),
        ],
        out_shape=[
            jax.ShapeDtypeStruct((total, lin.shape[1]), BF16),
            jax.ShapeDtypeStruct((8, mixed_width), F32),
            jax.ShapeDtypeStruct((8, LANES), F32),
            jax.ShapeDtypeStruct((8, channels), F32),
        ],
        scratch_shapes=[
            pltpu.VMEM((NS, channels), F32),
            pltpu.VMEM((8, mixed_width), F32),
            pltpu.VMEM((8, 1), jnp.int32),
        ],
        compiler_params=pltpu.CompilerParams(vmem_limit_bytes=48 << 20),
        name="mixer_backward",
    )(
        lin, lin, seg_column, seg_column, seg.reshape(1, total), conv_weight, heads_vec, heads_map, gain,
        grad_normed, inverse, cross, ssm, mixed, states,
    )


ROWS = 256


def turn(values, cosine, sine):
    return values * cosine + pltpu.roll(values, HEAD_SIZE // 2, 1) * sine


def attend_weights(query, keys, seg, seg_row, start):
    stop = start + ROWS
    scores = mat_nt(query, keys[:stop]) * (1.0 / math.sqrt(HEAD_SIZE))
    allowed = (iota((ROWS, stop), 0) + start >= iota((ROWS, stop), 1)) & (
        seg[start:stop] == seg_row[:, :stop]
    )
    scores = jnp.where(allowed, scores, FAR)
    shifted = jnp.exp(scores - jnp.max(scores, 1, keepdims=True))
    return shifted * (1.0 / jnp.sum(shifted, 1, keepdims=True))


def attend_forward_kernel(head_ref, q_ref, k_ref, v_ref, seg_ref, segr_ref, cos_ref, sin_ref, out_ref):
    cosine, sine = cos_ref[...], sin_ref[...]
    seg, seg_row = seg_ref[...], segr_ref[...]
    query = turn(q_ref[...], cosine, sine).astype(BF16)
    keys = turn(k_ref[...], cosine, sine).astype(BF16)
    values = v_ref[...].astype(BF16)
    for start in range(0, SEQ_LEN, ROWS):
        weights = attend_weights(query[start : start + ROWS], keys, seg, seg_row, start)
        out_ref[start : start + ROWS, :] = mat(
            weights.astype(BF16), values[: start + ROWS]
        ).astype(BF16)


def attend_backward_kernel(
    first_block, lead, head_ref, q_ref, k_ref, v_ref, seg_ref, segr_ref, cos_ref, sin_ref, do_ref, old_ref,
    dlin_ref, dkeys, dvalues, dq_ref, dkv_ref, sem,
):
    step = pl.program_id(1)
    here = pl.ds(pl.program_id(0) * SEQ_LEN, SEQ_LEN)
    cosine, sine = cos_ref[...], sin_ref[...]
    seg, seg_row = seg_ref[...], segr_ref[...]
    scale = 1.0 / math.sqrt(HEAD_SIZE)

    @pl.when(step == 0)
    def _():
        dkeys[...] = jnp.zeros_like(dkeys)
        dvalues[...] = jnp.zeros_like(dvalues)

    query = turn(q_ref[...], cosine, sine).astype(BF16)
    keys = turn(k_ref[...], cosine, sine).astype(BF16)
    values = v_ref[...].astype(BF16)
    for start in range(0, SEQ_LEN, ROWS):
        stop = start + ROWS
        rows = slice(start, stop)
        weights = attend_weights(query[rows], keys, seg, seg_row, start)
        grad_out = do_ref[rows, :]
        dvalues[:stop] += mat_tn(weights.astype(BF16), grad_out)
        grads = mat_nt(grad_out, values[:stop])
        inner = jnp.sum(grads * weights, 1, keepdims=True)
        scores = (weights * (grads - inner)).astype(BF16)
        dq = mat(scores, keys[:stop]) * scale
        dq_ref[rows, :] = turn(dq, cosine[rows], -sine[rows]).astype(BF16)
        dkeys[:stop] += mat_tn(scores, query[rows]) * scale
    place = pl.ds(pl.multiple_of((first_block + step) * HEAD_SIZE, HEAD_SIZE), HEAD_SIZE)
    out = pltpu.make_async_copy(dq_ref, dlin_ref.at[here, place], sem)
    out.start()
    out.wait()

    @pl.when(step == pl.num_programs(1) - 1)
    def _():
        mine = head_ref[0]
        grad_keys = turn(dkeys[...], cosine, -sine)
        grad_values = dvalues[...]
        for head in range(KEY_HEADS):
            same = mine == head
            cols = slice(head * HEAD_SIZE, (head + 1) * HEAD_SIZE)
            dkv_ref[:, cols] = jnp.where(same, grad_keys, 0.0).astype(BF16)
            cols = slice((KEY_HEADS + head) * HEAD_SIZE, (KEY_HEADS + head + 1) * HEAD_SIZE)
            dkv_ref[:, cols] = jnp.where(same, grad_values, 0.0).astype(BF16)
        both = pltpu.make_async_copy(dkv_ref, dlin_ref.at[here, pl.ds(lead, dkv_ref.shape[1])], sem)
        both.start()
        both.wait()


def attend_specs(first_block, lead):
    column = lambda first: pl.BlockSpec((SEQ_LEN, HEAD_SIZE), first)
    pair_block = lead // HEAD_SIZE
    return [
        column(lambda b, h, s: (b, first_block + h)),
        column(lambda b, h, s: (b, pair_block + s[0])),
        column(lambda b, h, s: (b, pair_block + KEY_HEADS + s[0])),
        pl.BlockSpec((SEQ_LEN, 1), lambda b, h, s: (b, 0)),
        pl.BlockSpec((1, SEQ_LEN), lambda b, h, s: (0, b)),
        pl.BlockSpec((SEQ_LEN, HEAD_SIZE), lambda b, h, s: (0, 0)),
        pl.BlockSpec((SEQ_LEN, HEAD_SIZE), lambda b, h, s: (0, 0)),
    ]


def attend_forward(lin, first_block, lead, heads, key_head, seg, cosine, sine):
    total = lin.shape[0]
    return pl.pallas_call(
        attend_forward_kernel,
        grid_spec=pltpu.PrefetchScalarGridSpec(
            num_scalar_prefetch=1,
            grid=(total // SEQ_LEN, heads),
            in_specs=attend_specs(first_block, lead),
            out_specs=pl.BlockSpec((SEQ_LEN, HEAD_SIZE), lambda b, h, s: (b, h)),
        ),
        out_shape=jax.ShapeDtypeStruct((total, heads * HEAD_SIZE), BF16),
        compiler_params=pltpu.CompilerParams(vmem_limit_bytes=48 << 20),
        name="attend_forward",
    )(key_head, lin, lin, lin, seg.reshape(total, 1), seg.reshape(1, total), cosine, sine)


def attend_backward(lin, first_block, lead, heads, key_head, seg, cosine, sine, grad_out, grad_lin):
    total = lin.shape[0]
    return pl.pallas_call(
        functools.partial(attend_backward_kernel, first_block, lead),
        grid_spec=pltpu.PrefetchScalarGridSpec(
            num_scalar_prefetch=1,
            grid=(total // SEQ_LEN, heads),
            in_specs=attend_specs(first_block, lead)
            + [
                pl.BlockSpec((SEQ_LEN, HEAD_SIZE), lambda b, h, s: (b, h)),
                pl.BlockSpec(memory_space=pl.ANY),
            ],
            out_specs=pl.BlockSpec(memory_space=pl.ANY),
            scratch_shapes=[
                pltpu.VMEM((SEQ_LEN, HEAD_SIZE), F32),
                pltpu.VMEM((SEQ_LEN, HEAD_SIZE), F32),
                pltpu.VMEM((SEQ_LEN, HEAD_SIZE), BF16),
                pltpu.VMEM((SEQ_LEN, 2 * KEY_HEADS * HEAD_SIZE), BF16),
                pltpu.SemaphoreType.DMA,
            ],
        ),
        out_shape=jax.ShapeDtypeStruct(grad_lin.shape, BF16),
        input_output_aliases={9: 0},
        compiler_params=pltpu.CompilerParams(vmem_limit_bytes=48 << 20),
        name="attend_backward",
    )(key_head, lin, lin, lin, seg.reshape(total, 1), seg.reshape(1, total), cosine, sine, grad_out, grad_lin)


def rms_rows(values):
    return lax.rsqrt(jnp.mean(values * values, -1, keepdims=True) + EPS)


def rms_back(values, inverse, gain, grad):
    scaled = grad * gain
    inner = jnp.mean(scaled * values, -1, keepdims=True)
    return inverse * scaled - values * (inverse * inverse * inverse * inner)


def angle_tables():
    half = HEAD_SIZE // 2
    frequency = jnp.exp(jnp.arange(half).astype(F32) * (-2.0 * math.log(THETA) / HEAD_SIZE))
    turned = jnp.arange(SEQ_LEN).astype(F32)[:, None] * frequency[None, :]
    cosine, sine = jnp.cos(turned), jnp.sin(turned)
    return jnp.concatenate([cosine, cosine], 1), jnp.concatenate([-sine, sine], 1)


MESH = pl.DeviceIdType.MESH
LINE_CHUNKS = 4


CORE, ACROSS, ALONG, CORNER = 1, 2, 4, 6
PLANE_PARTS = 4


def partner(index, bits):
    for bit in (CORE, ACROSS, ALONG):
        if bits & bit:
            index = index + jnp.where(lax.rem(index // bit, 2) == 0, bit, -bit)
    return index


def greet(place, group, owner, plane, everyone=False):
    barrier = pltpu.get_barrier_semaphore()
    if everyone:
        for hop in range(1, group):
            pl.semaphore_signal(
                barrier, inc=1, device_id={"tensor": lax.rem(place + hop, group)}, device_id_type=MESH
            )
        count = group - 1
    else:

        @pl.when(place > 0)
        def _():
            pl.semaphore_signal(barrier, inc=1, device_id={"tensor": place - 1}, device_id_type=MESH)

        @pl.when(place < group - 1)
        def _():
            pl.semaphore_signal(barrier, inc=1, device_id={"tensor": place + 1}, device_id_type=MESH)

        count = jnp.where((place > 0) & (place < group - 1), 2, 1)
    if plane:
        for bits in (CORE, ACROSS, ALONG):
            pl.semaphore_signal(barrier, inc=1, device_id={"dp": partner(owner, bits)}, device_id_type=MESH)
        count = count + 3
    pl.semaphore_wait(barrier, count)


def plane_gather_steps(own_ref, out_ref, local_sem, send_sem, recv_sem):
    owner = lax.axis_index("dp")
    share = own_ref.shape[0]
    parts = PLANE_PARTS
    rows = share // parts
    half = parts // 2

    def copy(slot, origin, to, part, own=False):
        block = out_ref.at[pl.ds(origin * share + part * rows, rows)]
        return pltpu.make_async_remote_copy(
            own_ref.at[pl.ds(part * rows, rows)] if own else block,
            block,
            send_sem.at[slot, part],
            recv_sem.at[slot, part],
            device_id={"dp": partner(owner, to)},
            device_id_type=MESH,
        )

    keep = pltpu.make_async_copy(own_ref, out_ref.at[pl.ds(owner * share, share)], local_sem)
    first = [
        copy(slot, owner, to, part, True)
        for part in range(parts)
        for slot, to in ((1, ACROSS), (2, ALONG), (0, CORE))
    ]
    later = []

    def begin():
        keep.start()
        for item in first:
            item.start()

    def go(item):
        item.start()
        later.append(item)

    def neighbours(part):
        copy(1, owner, ACROSS, part, True).wait_recv()
        if part < half:
            go(copy(3, partner(owner, ACROSS), ALONG, part))
        go(copy(4, partner(owner, ACROSS), CORE, part))
        other = (part + half) % parts
        copy(2, owner, ALONG, other, True).wait_recv()
        if other >= half:
            go(copy(3, partner(owner, ALONG), ACROSS, other))
        go(copy(5, partner(owner, ALONG), CORE, other))

    def corner(part):
        copy(3, partner(owner, ACROSS), ALONG if part < half else ACROSS, part).wait_recv()
        go(copy(6, partner(owner, CORNER), CORE, part))

    def end():
        for part in range(parts):
            for slot in (0, 4, 5, 6):
                copy(slot, owner, CORE, part).wait_recv()
        for item in first + later:
            item.wait_send()
        keep.wait()

    return begin, neighbours, corner, end


def entry_gather_kernel(
    group, parts, own_ref, weight_ref, out_ref, full_ref, local_sem, send_sem, recv_sem, keep_sem, plane_send, plane_recv
):
    place = lax.axis_index("tensor")
    rows = own_ref.shape[0] // parts
    greet(place, group, lax.axis_index("dp"), True)

    def copy(side, source, part, own=False):
        block = out_ref.at[source, pl.ds(part * rows, rows)]
        return pltpu.make_async_remote_copy(
            own_ref.at[pl.ds(part * rows, rows)] if own else block,
            block,
            send_sem.at[side, source, part],
            recv_sem.at[side, source, part],
            device_id={"tensor": place + 1 - 2 * side},
            device_id_type=MESH,
        )

    begin, neighbours, corner, end = plane_gather_steps(weight_ref, full_ref, keep_sem, plane_send, plane_recv)
    keep = pltpu.make_async_copy(own_ref, out_ref.at[place], local_sem)
    keep.start()
    more = (place < group - 1, place > 0)
    for part in range(parts):
        for side in (0, 1):

            @pl.when(more[side])
            def _():
                copy(side, place, part, True).start()

    begin()
    plane_steps = [functools.partial(neighbours, part) for part in range(PLANE_PARTS)] + [
        functools.partial(corner, part)
        for pair in range(PLANE_PARTS // 2)
        for part in (pair, pair + PLANE_PARTS // 2)
    ]
    line_steps = (group - 1) * parts
    done = 0
    for hop in range(1, group):
        for part in range(parts):
            for side in (0, 1):
                source = place - hop if side == 0 else place + hop

                @pl.when((source >= 0) & (source < group))
                def _():
                    copy(side, source, part).wait_recv()

                    @pl.when(more[side])
                    def _():
                        copy(side, source, part).start()

            index = (hop - 1) * parts + part + 1
            while done < len(plane_steps) * index // line_steps:
                plane_steps[done]()
                done += 1

    end()
    keep.wait()
    for hop in range(group):
        for part in range(parts):
            for side in (0, 1):
                source = place - hop if side == 0 else place + hop

                @pl.when((source >= 0) & (source < group) & more[side])
                def _():
                    copy(side, source, part, hop == 0).wait_send()


def line_gather_kernel(group, parts, own_ref, out_ref, local_sem, send_sem, recv_sem):
    place = lax.axis_index("tensor")
    rows = own_ref.shape[0] // parts
    greet(place, group, None, False)

    def copy(side, source, part, own=False):
        block = out_ref.at[source, pl.ds(part * rows, rows)]
        return pltpu.make_async_remote_copy(
            own_ref.at[pl.ds(part * rows, rows)] if own else block,
            block,
            send_sem.at[side, source, part],
            recv_sem.at[side, source, part],
            device_id={"tensor": place + 1 - 2 * side},
            device_id_type=MESH,
        )

    keep = pltpu.make_async_copy(own_ref, out_ref.at[place], local_sem)
    keep.start()
    more = (place < group - 1, place > 0)
    for part in range(parts):
        for side in (0, 1):

            @pl.when(more[side])
            def _():
                copy(side, place, part, True).start()

    for hop in range(1, group):
        for part in range(parts):
            for side in (0, 1):
                source = place - hop if side == 0 else place + hop

                @pl.when((source >= 0) & (source < group))
                def _():
                    copy(side, source, part).wait_recv()

                    @pl.when(more[side])
                    def _():
                        copy(side, source, part).start()

    keep.wait()
    for hop in range(group):
        for part in range(parts):
            for side in (0, 1):
                source = place - hop if side == 0 else place + hop

                @pl.when((source >= 0) & (source < group) & more[side])
                def _():
                    copy(side, source, part, hop == 0).wait_send()


def entry_gather(own, weight, dp_size, group, collective_id):
    rows, cols = own.shape
    parts = 2
    anywhere = pl.BlockSpec(memory_space=pl.ANY)
    line_sems = pltpu.SemaphoreType.DMA((2, group, parts))
    plane_sems = pltpu.SemaphoreType.DMA((7, PLANE_PARTS))
    if dp_size != 8:
        all_rows = pl.pallas_call(
            functools.partial(line_gather_kernel, group, parts),
            in_specs=[anywhere],
            out_specs=anywhere,
            out_shape=jax.ShapeDtypeStruct((group, rows, cols), own.dtype),
            scratch_shapes=[pltpu.SemaphoreType.DMA, line_sems, line_sems],
            compiler_params=pltpu.CompilerParams(collective_id=collective_id, has_side_effects=True),
            name="line_gather",
        )(own)
        return all_rows.reshape(group * rows, cols), gather(weight, "dp", 0)
    all_rows, full = pl.pallas_call(
        functools.partial(entry_gather_kernel, group, parts),
        in_specs=[anywhere] * 2,
        out_specs=[anywhere] * 2,
        out_shape=[
            jax.ShapeDtypeStruct((group, rows, cols), own.dtype),
            jax.ShapeDtypeStruct((dp_size * weight.shape[0], weight.shape[1]), weight.dtype),
        ],
        scratch_shapes=[
            pltpu.SemaphoreType.DMA, line_sems, line_sems, pltpu.SemaphoreType.DMA, plane_sems, plane_sems,
        ],
        compiler_params=pltpu.CompilerParams(collective_id=collective_id, has_side_effects=True),
        name="entry_gather",
    )(own, weight)
    return all_rows.reshape(group * rows, cols), full


def plane_scatter_steps(piece_refs, out_ref, got, staged, near_x, near_y, last, sems):
    owner = lax.axis_index("dp")
    share, width = out_ref.shape
    parts = LINE_CHUNKS
    half = share // 2
    rows = half // parts
    targets = (0, ACROSS, CORNER, ALONG)
    core_send, core_recv, stage_sem, x_send, x_recv, y_send, y_recv, last_send, last_recv = sems

    def block(piece_ref, target, side, part):
        return piece_ref.at[pl.ds(target * share + side * half + part * rows, rows)]

    def whole_core(part):
        return pltpu.make_async_remote_copy(
            got.at[part], got.at[part], core_send.at[part], core_recv.at[part],
            device_id={"dp": partner(owner, CORE)}, device_id_type=MESH,
        )

    def to_x(part):
        return pltpu.make_async_remote_copy(
            got.at[part, 0, pl.ds(1, 2)], near_x.at[part], x_send.at[part], x_recv.at[part],
            device_id={"dp": partner(owner, ACROSS)}, device_id_type=MESH,
        )

    def to_y(part):
        return pltpu.make_async_remote_copy(
            got.at[part, 1, pl.ds(2, 2)], near_y.at[part], y_send.at[part], y_recv.at[part],
            device_id={"dp": partner(owner, ALONG)}, device_id_type=MESH,
        )

    def on_to_y(part):
        return pltpu.make_async_remote_copy(
            near_x.at[part, 1], last.at[part, 0], last_send.at[0, part], last_recv.at[0, part],
            device_id={"dp": partner(owner, ALONG)}, device_id_type=MESH,
        )

    def on_to_x(part):
        return pltpu.make_async_remote_copy(
            near_y.at[part, 0], last.at[part, 1], last_send.at[1, part], last_recv.at[1, part],
            device_id={"dp": partner(owner, ACROSS)}, device_id_type=MESH,
        )

    def begin():
        def send(part, carry):
            for side in (0, 1):
                for index, bits in enumerate(targets):
                    first = 0
                    for piece_ref in piece_refs:
                        cols = pl.ds(first, piece_ref.shape[1])
                        first += piece_ref.shape[1]
                        pltpu.make_async_remote_copy(
                            block(piece_ref, partner(owner, bits | CORE), side, part),
                            got.at[part, side, index, :, cols],
                            core_send.at[part],
                            core_recv.at[part],
                            device_id={"dp": partner(owner, CORE)},
                            device_id_type=MESH,
                        ).start()
            return carry

        lax.fori_loop(0, parts, send, 0)
        stage(0)

    def stage(part):
        for side in (0, 1):
            for index, bits in enumerate(targets):
                first = 0
                for piece_ref in piece_refs:
                    cols = pl.ds(first, piece_ref.shape[1])
                    first += piece_ref.shape[1]
                    pltpu.make_async_copy(
                        block(piece_ref, partner(owner, bits), side, part), staged.at[side, index, :, cols], stage_sem
                    ).start()

    def add_core(part):
        whole_core(part).wait_recv()
        pltpu.make_async_copy(staged, staged, stage_sem).wait()

        def add(step, carry):
            side, index = step // 4, lax.rem(step, 4)
            total = got[part, side, index].astype(F32) + staged[side, index].astype(F32)
            got[part, side, index] = total.astype(BF16)
            return carry

        lax.fori_loop(0, 8, add, 0)
        to_x(part).start()
        to_y(part).start()

        @pl.when(part + 1 < parts)
        def _():
            stage(part + 1)

    def add_near(part):
        to_x(part).wait_recv()
        near_x[part, 1] = (near_x[part, 1].astype(F32) + got[part, 0, 3].astype(F32)).astype(BF16)
        on_to_y(part).start()
        to_y(part).wait_recv()
        near_y[part, 0] = (near_y[part, 0].astype(F32) + got[part, 1, 1].astype(F32)).astype(BF16)
        on_to_x(part).start()

    def add_last(part):
        for side, near, step in ((0, near_x.at[part, 0], on_to_y), (1, near_y.at[part, 1], on_to_x)):
            step(part).wait_recv()
            total = got[part, side, 0].astype(F32) + near[...].astype(F32)
            out_ref[pl.ds(side * half + part * rows, rows), :] = total + last[part, side].astype(F32)

    def end(part):
        whole_core(part).wait_send()
        to_x(part).wait_send()
        to_y(part).wait_send()
        on_to_y(part).wait_send()
        on_to_x(part).wait_send()

    return begin, add_core, add_near, add_last, end


def plane_scatter_scratch(share, width):
    rows = share // 2 // LINE_CHUNKS
    by_part = pltpu.SemaphoreType.DMA((LINE_CHUNKS,))
    by_side = pltpu.SemaphoreType.DMA((2, LINE_CHUNKS))
    return [
        pltpu.VMEM((LINE_CHUNKS, 2, 4, rows, width), BF16),
        pltpu.VMEM((2, 4, rows, width), BF16),
        pltpu.VMEM((LINE_CHUNKS, 2, rows, width), BF16),
        pltpu.VMEM((LINE_CHUNKS, 2, rows, width), BF16),
        pltpu.VMEM((LINE_CHUNKS, 2, rows, width), BF16),
        by_part, by_part, pltpu.SemaphoreType.DMA, by_part, by_part, by_part, by_part, by_side, by_side,
    ]


def common_sum(group, place, piece_out, weight_ref, lanes_ref, common_ref, outbox, inbox, send_sem, recv_sem, ranges):
    rows, width = common_ref.shape
    first = 0
    for start, count in ranges:
        outbox[:, first : first + count] = piece_out[:, start : start + count].astype(BF16)
        first += count
    lanes = lanes_ref[...]
    lane = iota(lanes.shape, 1)
    own = jnp.sum(weight_ref[...].astype(F32) * piece_out[:, : weight_ref.shape[1]], 1, keepdims=True)
    last = piece_out[:, piece_out.shape[1] - LANES :]
    last = jnp.where(lane == LANES - 2, own * lanes, jnp.where(lane == LANES - 1, lanes, last))
    outbox[:, first:] = last.astype(BF16)
    copies = []
    for hop in range(1, group):
        peer = lax.rem(place + hop, group)
        copies.append(
            pltpu.make_async_remote_copy(
                outbox.at[pl.ds(peer * rows, rows)], inbox.at[hop - 1], send_sem.at[hop - 1], recv_sem.at[hop - 1],
                device_id={"tensor": peer}, device_id_type=MESH,
            )
        )
    for copy in copies:
        copy.start()
    total = outbox[pl.ds(place * rows, rows), :].astype(F32)
    for hop, copy in enumerate(copies):
        copy.wait_recv()
        total = total + inbox[hop].astype(F32)
    common_ref[...] = total
    for copy in copies:
        copy.wait_send()


def common_plain(group, summed, weight, lanes, ranges):
    own = jnp.sum(weight.astype(F32) * summed[:, : weight.shape[1]], 1, keepdims=True)
    lane = jnp.arange(LANES)[None]
    last = summed[:, summed.shape[1] - LANES :]
    last = jnp.where(lane == LANES - 2, own * lanes, jnp.where(lane == LANES - 1, lanes, last))
    parts = [summed[:, start : start + count] for start, count in ranges] + [last]
    return scatter(jnp.concatenate(parts, 1).astype(BF16), "tensor", 0).astype(F32)


def line_sum_kernel(
    group, spread, dot, finish, own_count, side_count, piece_count, ranges, *refs,
):
    x_ref, w_ref, refs = refs[0], refs[1], refs[2:]
    own_refs, refs = refs[:own_count], refs[own_count:]
    piece_refs, refs = refs[:piece_count], refs[piece_count:]
    if ranges:
        weight_ref, lanes_ref, refs = refs[0], refs[1], refs[2:]
    out_ref, refs = refs[0], refs[1:]
    side_refs, refs = refs[:side_count], refs[side_count:]
    if piece_count:
        piece_out, refs = refs[0], refs[1:]
    if ranges:
        common_ref, refs = refs[0], refs[1:]
    held, part, sum_send, sum_recv, out_send, out_recv = refs[:6]
    place = lax.axis_index("tensor")
    away = group - 1 - place
    chunks = LINE_CHUNKS
    rows = x_ref.shape[1] // chunks
    few = rows // 2
    model = out_ref.shape[-1]
    tile = model // group
    more = (place < group - 1, place > 0)
    ahead = (place > 0, place < group - 1)
    greet(place, group, lax.axis_index("dp"), piece_count > 0, bool(ranges))
    if piece_count:
        begin, add_core, add_near, add_last, end = plane_scatter_steps(
            piece_refs, piece_out, *refs[6:11], refs[11:20]
        )
        begin()

    def multiply(chunk, index):
        left = x_ref[:, pl.ds(chunk * rows, rows), :].reshape(group * rows, x_ref.shape[2])
        cols = pl.ds(index * tile, tile)
        part[lax.rem(chunk, 2), :, :, cols] = dot(left, w_ref, cols).reshape(group, rows, tile)

    def sum_copy(side, chunk, share, half):
        block = held.at[chunk, share + 1 - side, pl.ds(half * few, few)]
        index = 2 * chunk + half
        return pltpu.make_async_remote_copy(
            block, block, sum_send.at[side, index, share], sum_recv.at[side, index, share],
            device_id={"tensor": place + 1 - 2 * side}, device_id_type=MESH,
        )

    def out_copy(side, chunk, source, half):
        block = out_ref.at[source, pl.ds(chunk * rows + half * few, few)]
        index = 2 * chunk + half
        return pltpu.make_async_remote_copy(
            block, block, out_send.at[side, index, source], out_recv.at[side, index, source],
            device_id={"tensor": place + 1 - 2 * side}, device_id_type=MESH,
        )

    for index in range(group):
        multiply(0, index)

    def pass_out(chunk, slot, half):
        for side in (0, 1):
            source = place - (slot + 1) if side == 0 else place + (slot + 1)

            @pl.when((chunk > 0) & (source >= 0) & (source < group))
            def _():
                out_copy(side, chunk - 1, source, half).wait_recv()

                @pl.when(more[side])
                def _():
                    out_copy(side, chunk - 1, source, half).start()

    def add_on(chunk, slot, half):
        local = pl.ds(half * few, few)
        for side in (0, 1):
            depth = place if side == 0 else away
            share = group - 1 - slot + place if side == 0 else slot - away

            @pl.when((chunk < chunks) & (depth <= slot))
            def _():
                mine = part[lax.rem(chunk, 2), share, local]
                spot = share + 1 - side

                @pl.when(ahead[side])
                def _():
                    sum_copy(side, chunk, share, half).wait_recv()
                    held[chunk, spot, local] = (held[chunk, spot, local].astype(F32) + mine).astype(BF16)

                @pl.when(jnp.logical_not(ahead[side]))
                def _():
                    held[chunk, spot, local] = mine.astype(BF16)

                sum_copy(side, chunk, share, half).start()

    def complete(chunk, half):
        local = pl.ds(half * few, few)

        @pl.when(chunk < chunks)
        def _():
            total = part.at[lax.rem(chunk, 2), place, local]
            for side in (0, 1):

                @pl.when(ahead[side])
                def _():
                    sum_copy(side, chunk, place, half).wait_recv()
                    total[...] += held[chunk, place + 1 - side, local].astype(F32)

            mine = pl.ds(chunk * rows + half * few, few)
            result = finish(total[...], mine, own_refs, side_refs)
            if spread:
                out_ref[place, mine, :] = result
                for side in (0, 1):

                    @pl.when(more[side])
                    def _():
                        out_copy(side, chunk, place, half).start()
            else:
                out_ref[mine, :] = result

    def one_chunk(chunk, carry):
        for slot in range(group):
            for half in (0, 1):
                if slot + 1 < group and spread:
                    pass_out(chunk, slot, half)
                if slot < group - 1:
                    add_on(chunk, slot, half)
                else:
                    complete(chunk, half)

            @pl.when(chunk + 1 < chunks)
            def _():
                multiply(chunk + 1, slot)

            if piece_count and slot == 0:

                @pl.when(chunk < chunks)
                def _():
                    add_core(chunk)

            if piece_count and slot == group // 2:

                @pl.when(chunk < chunks)
                def _():
                    add_near(chunk)

            if piece_count and slot == 1:

                @pl.when(chunk > 0)
                def _():
                    add_last(chunk - 1)

        return carry

    lax.fori_loop(0, chunks + 1 if spread or piece_count else chunks, one_chunk, 0)
    if ranges:
        common_sum(group, place, piece_out, weight_ref, lanes_ref, common_ref, *refs[20:], ranges)

    def finish_sends(chunk, carry):
        for half in (0, 1):
            for slot in range(group):
                for side in (0, 1):
                    depth = place if side == 0 else away
                    share = group - 1 - slot + place if side == 0 else slot - away
                    if slot < group - 1:

                        @pl.when(depth <= slot)
                        def _():
                            sum_copy(side, chunk, share, half).wait_send()

                    source = place - slot if side == 0 else place + slot
                    if spread:

                        @pl.when((source >= 0) & (source < group) & more[side])
                        def _():
                            out_copy(side, chunk, source, half).wait_send()

        if piece_count:
            end(chunk)
        return carry

    lax.fori_loop(0, chunks, finish_sends, 0)


def line_sum(
    x, w, own, dot, finish, side_shapes, group, model, collective_id, name, spread=True, pieces=(), dp_size=8, common=None
):
    total = x.shape[0]
    rows = total // group
    vmem = pl.BlockSpec(memory_space=pltpu.VMEM)
    anywhere = pl.BlockSpec(memory_space=pl.ANY)
    piece_rows = rows // LINE_CHUNKS
    sems = pltpu.SemaphoreType.DMA((2, 2 * LINE_CHUNKS, group))
    out_shape = [jax.ShapeDtypeStruct((group, rows, model), BF16) if spread else jax.ShapeDtypeStruct((rows, model), F32)]
    out_shape += side_shapes
    scratch = [
        pltpu.VMEM((LINE_CHUNKS, group + 1, piece_rows, model), BF16),
        pltpu.VMEM((2, group, piece_rows, model), F32),
        sems, sems, sems, sems,
    ]
    summed, ranges, last = None, (), []
    if pieces and dp_size != 8:
        summed = [jnp.concatenate([scatter(piece, "dp", 0) for piece in pieces], 1).astype(F32)]
        if common:
            summed.append(common_plain(group, summed[0], *common))
        pieces, common = (), None
    if pieces:
        share, width = pieces[0].shape[0] // dp_size, sum(piece.shape[1] for piece in pieces)
        out_shape += [jax.ShapeDtypeStruct((share, width), F32)]
        scratch += plane_scatter_scratch(share, width)
    if common:
        ranges, last = common[2], list(common[:2])
        common_width = sum(count for _, count in ranges) + LANES
        out_shape += [jax.ShapeDtypeStruct((share // group, common_width), F32)]
        scratch += [
            pltpu.VMEM((share, common_width), BF16),
            pltpu.VMEM((group - 1, share // group, common_width), BF16),
            pltpu.SemaphoreType.DMA((group - 1,)),
            pltpu.SemaphoreType.DMA((group - 1,)),
        ]
    results = pl.pallas_call(
        functools.partial(line_sum_kernel, group, spread, dot, finish, len(own), len(side_shapes), len(pieces), ranges),
        in_specs=[vmem] * (2 + len(own)) + [anywhere] * len(pieces) + [vmem] * len(last),
        out_specs=[vmem] * len(out_shape),
        out_shape=out_shape,
        scratch_shapes=scratch,
        compiler_params=pltpu.CompilerParams(
            collective_id=collective_id, has_side_effects=True, vmem_limit_bytes=60 << 20
        ),
        name=name,
    )(x.reshape(group, rows, x.shape[1]), w, *own, *pieces, *last)
    results = list(results)
    if spread:
        results[0] = results[0].reshape(total, model)
    return results if summed is None else results + summed


def project_kernel(tokens_ref, gains_ref, w_ref, lin_ref, first_ref, gain_rows_ref):
    @pl.when(pl.program_id(0) == 0)
    def _():
        picks = (iota((8, LANES), 0) + LANES - 2 == iota((8, LANES), 1)).astype(BF16)
        gain_rows_ref[...] = mat_nt(picks, gains_ref[...])
        gain = gain_rows_ref[0:1]

        def normalise(step, carry):
            rows = pl.ds(step * CHUNK, CHUNK)
            values = tokens_ref[rows, :].astype(F32)
            first_ref[rows, :] = (values * rms_rows(values) * gain).astype(BF16)
            return carry

        lax.fori_loop(0, tokens_ref.shape[0] // CHUNK, normalise, 0)

    lin_ref[...] = mat(first_ref[...], w_ref[...])


def project(tokens, weight, gain_block):
    total, model = tokens.shape
    cols = weight.shape[1]
    tile = 512
    return pl.pallas_call(
        project_kernel,
        grid=(cols // tile,),
        in_specs=[
            whole_block(tokens),
            pl.BlockSpec((model, LANES), lambda c: (0, gain_block)),
            pl.BlockSpec((model, tile), lambda c: (0, c)),
        ],
        out_specs=[
            pl.BlockSpec((total, tile), lambda c: (0, c)),
            pl.BlockSpec((total, model), lambda c: (0, 0)),
            pl.BlockSpec((8, model), lambda c: (0, 0)),
        ],
        out_shape=[
            jax.ShapeDtypeStruct((total, cols), F32),
            jax.ShapeDtypeStruct((total, model), BF16),
            jax.ShapeDtypeStruct((8, model), F32),
        ],
        compiler_params=pltpu.CompilerParams(vmem_limit_bytes=56 << 20),
        name="project",
    )(tokens, weight, weight)


def exchange_copies(group, own_ref, slots, send_sem, recv_sem):
    place = lax.axis_index("tensor")
    return [
        pltpu.make_async_remote_copy(
            own_ref, slots.at[hop - 1], send_sem.at[hop - 1], recv_sem.at[hop - 1],
            device_id={"tensor": lax.rem(place + hop, group)}, device_id_type=MESH,
        )
        for hop in range(1, group)
    ]


def exchange_scratch(group, shape):
    return [
        pltpu.VMEM((group - 1,) + shape, F32),
        pltpu.SemaphoreType.DMA((group - 1,)),
        pltpu.SemaphoreType.DMA((group - 1,)),
    ]


def gate_norm_kernel(
    group, square_ref, ssm_ref, gate_ref, gain_ref, attended_ref, mix_ref, inverse_ref, slots, send_sem, recv_sem
):
    greet(lax.axis_index("tensor"), group, None, False, True)
    copies = exchange_copies(group, square_ref, slots, send_sem, recv_sem)
    for copy in copies:
        copy.start()
    total = square_ref[...]
    for hop, copy in enumerate(copies):
        copy.wait_recv()
        total = total + slots[hop]
    inverse_ref[...] = lax.rsqrt(total * (1.0 / DSSM) + EPS)
    query_cols = attended_ref.shape[1]
    mix_ref[:, :query_cols] = attended_ref[...]

    def norm(step, carry):
        rows = pl.ds(step * CHUNK, CHUNK)
        gate = gate_ref[rows, :]
        gated = ssm_ref[rows, :] * gate * sigmoid(gate)
        mix_ref[rows, query_cols:] = (gated * as_column(inverse_ref[step]) * gain_ref[...]).astype(BF16)
        return carry

    lax.fori_loop(0, square_ref.shape[0], norm, 0)
    for copy in copies:
        copy.wait_send()


def gate_norm(square, ssm, lin, gain, attended, group, collective_id):
    total, channels = ssm.shape
    width = attended.shape[1] + channels
    return pl.pallas_call(
        functools.partial(gate_norm_kernel, group),
        grid=(1,),
        in_specs=[
            whole_block(square),
            whole_block(ssm),
            pl.BlockSpec((total, channels), lambda c: (0, 0)),
            whole_block(gain),
            whole_block(attended),
        ],
        out_specs=[pl.BlockSpec((total, width), lambda c: (0, 0)), whole_block(square)],
        out_shape=[jax.ShapeDtypeStruct((total, width), BF16), jax.ShapeDtypeStruct(square.shape, F32)],
        scratch_shapes=exchange_scratch(group, square.shape),
        compiler_params=pltpu.CompilerParams(
            collective_id=collective_id, has_side_effects=True, vmem_limit_bytes=56 << 20
        ),
        name="gate_norm",
    )(square, ssm, lin, gain, attended)


def gate_back_kernel(
    group, query_cols, mix_ref, w_ref, ssm_ref, gate_ref, gain_ref, attended_ref, normed_ref, cross_ref,
    own, slots, send_sem, recv_sem,
):
    step = pl.program_id(0)

    @pl.when(step == 0)
    def _():
        greet(lax.axis_index("tensor"), group, None, False, True)

    grads = mat_nt(mix_ref[...], w_ref[...])
    attended_ref[...] = grads[:, :query_cols].astype(BF16)
    grads = grads[:, query_cols:]
    normed_ref[...] = grads
    gate = gate_ref[...]
    products = ssm_ref[...] * gate * sigmoid(gate) * (grads * gain_ref[...])
    total = products[:, :LANES]
    for index in range(1, products.shape[1] // LANES):
        total = total + products[:, index * LANES : (index + 1) * LANES]
    per_step = ROWS // CHUNK
    for index in range(per_step):
        own[step * per_step + index] = row_sums_as_row(total[index * CHUNK : (index + 1) * CHUNK])

    @pl.when(step == pl.num_programs(0) - 1)
    def _():
        copies = exchange_copies(group, own, slots, send_sem, recv_sem)
        for copy in copies:
            copy.start()
        result = own[...]
        for hop, copy in enumerate(copies):
            copy.wait_recv()
            result = result + slots[hop]
        cross_ref[...] = result
        for copy in copies:
            copy.wait_send()


def gate_back(mix_all, weight_mix, ssm, lin, gain, query_cols, group, collective_id):
    total, channels = ssm.shape
    model = mix_all.shape[1]
    cross = (total // CHUNK, 1, CHUNK)
    by_rows = lambda cols: pl.BlockSpec((ROWS, cols), lambda c: (c, 0))
    return pl.pallas_call(
        functools.partial(gate_back_kernel, group, query_cols),
        grid=(total // ROWS,),
        in_specs=[by_rows(model), whole_block(weight_mix), by_rows(channels), by_rows(channels), whole_block(gain)],
        out_specs=[by_rows(query_cols), by_rows(channels), pl.BlockSpec(cross, lambda c: (0, 0, 0))],
        out_shape=[
            jax.ShapeDtypeStruct((total, query_cols), BF16),
            jax.ShapeDtypeStruct((total, channels), F32),
            jax.ShapeDtypeStruct(cross, F32),
        ],
        scratch_shapes=[pltpu.VMEM(cross, F32)] + exchange_scratch(group, cross),
        compiler_params=pltpu.CompilerParams(
            collective_id=collective_id, has_side_effects=True, vmem_limit_bytes=56 << 20
        ),
        name="gate_back",
    )(mix_all, weight_mix, ssm, lin, gain)


HIDDEN_TILE = 256


def feed_forward_kernel(second_ref, cot_ref, expand_ref, shrink_ref, act_ref, hidden_ref, out_ref, total):
    step = pl.program_id(0)
    expand = expand_ref[...]
    shrink = shrink_ref[...]
    for first in range(0, second_ref.shape[0], ROWS):
        rows = slice(first, first + ROWS)
        lin = mat(second_ref[rows, :], expand)
        gate, up = lin[:, :HIDDEN_TILE], lin[:, HIDDEN_TILE:]
        sig = sigmoid(gate)
        silu = gate * sig
        act = (silu * up).astype(BF16)
        act_ref[rows, :] = act
        grad = mat_nt(cot_ref[rows, :], shrink)
        hidden_ref[rows, :HIDDEN_TILE] = (grad * up * (sig * (1.0 + gate * (1.0 - sig)))).astype(BF16)
        hidden_ref[rows, HIDDEN_TILE:] = (grad * silu).astype(BF16)
        part = mat(act, shrink)

        @pl.when(step == 0)
        def _():
            total[rows, :] = part

        @pl.when(step > 0)
        def _():
            total[rows, :] += part

    @pl.when(step == pl.num_programs(0) - 1)
    def _():
        out_ref[...] = total[...].astype(BF16)


def feed_forward(second, cot, expand, shrink):
    total, model = second.shape
    hidden = shrink.shape[0]
    return pl.pallas_call(
        feed_forward_kernel,
        grid=(hidden // HIDDEN_TILE,),
        in_specs=[
            pl.BlockSpec(memory_space=pltpu.VMEM),
            pl.BlockSpec(memory_space=pltpu.VMEM),
            pl.BlockSpec((model, 2 * HIDDEN_TILE), lambda c: (0, c)),
            pl.BlockSpec((HIDDEN_TILE, model), lambda c: (c, 0)),
        ],
        out_specs=[
            pl.BlockSpec((total, HIDDEN_TILE), lambda c: (0, c)),
            pl.BlockSpec((total, 2 * HIDDEN_TILE), lambda c: (0, c)),
            pl.BlockSpec((total, model), lambda c: (0, 0)),
        ],
        out_shape=[
            jax.ShapeDtypeStruct((total, hidden), BF16),
            jax.ShapeDtypeStruct((total, 2 * hidden), BF16),
            jax.ShapeDtypeStruct((total, model), BF16),
        ],
        scratch_shapes=[pltpu.VMEM((total, model), F32)],
        compiler_params=pltpu.CompilerParams(vmem_limit_bytes=60 << 20),
        name="feed_forward",
    )(second, cot, expand, shrink)


def mix_finish(total, mine, own_refs, side_refs):
    tokens_ref, gain_ref = own_refs
    middle = tokens_ref[mine, :].astype(F32) + total
    side_refs[0][mine, :] = middle
    return (middle * rms_rows(middle) * gain_ref[...]).astype(BF16)


def second_finish(total, mine, own_refs, side_refs):
    cot_ref, middle_ref, gain_ref = own_refs
    middle = middle_ref[mine, :]
    grad = cot_ref[mine, :].astype(F32) + rms_back(middle, rms_rows(middle), gain_ref[...], total)
    side_refs[0][mine, :] = grad
    return grad.astype(BF16)


def first_finish(total, mine, own_refs, side_refs):
    tokens_ref, middle_ref, gain_ref = own_refs
    tokens = tokens_ref[mine, :].astype(F32)
    return middle_ref[mine, :] + rms_back(tokens, rms_rows(tokens), gain_ref[...], total)


def dot_columns(left, w_ref, cols):
    return mat(left, w_ref[:, cols])


def dot_rows(left, w_ref, cols):
    return mat_nt(left, w_ref[cols, :])


def gather(array, axis_name, axis):
    return lax.all_gather(array, axis_name, axis=axis, tiled=True)


def scatter(array, axis_name, axis):
    return lax.psum_scatter(array, axis_name, scatter_dimension=axis, tiled=True)


def per_device(
    tokens_in, segment_ids, cotangent, norm_first, query_weight, key_value_weight, output_weight,
    inner_weight, state_weight, step_weight, conv_inner, conv_state, head_params, gate_gain,
    mamba_weight, norm_second, expand_weight, shrink_weight,
):
    dp_size = lax.axis_size("dp")
    group = lax.axis_size("tensor")
    place = lax.axis_index("tensor")
    total = segment_ids.shape[0]
    own_rows, model = tokens_in.shape
    share = query_weight.shape[0]
    heads = step_weight.shape[1]
    channels = heads * PM
    query_cols = query_weight.shape[1]
    query_heads = query_cols // HEAD_SIZE
    pair_cols = key_value_weight.shape[1]
    hidden = shrink_weight.shape[0]
    state_cols = 2 * channels + 2 * NS
    mixer_cols = state_cols + LANES
    lead = -(-(mixer_cols + query_cols) // pair_cols) * pair_cols

    step_block = jnp.concatenate(
        [
            step_weight,
            jnp.zeros((share, LANES - 2 - heads), BF16),
            norm_first[:, None],
            norm_second[:, None],
        ],
        1,
    )
    spare = jnp.zeros((share, lead - mixer_cols - query_cols), BF16)
    weight_own = jnp.concatenate(
        [inner_weight.reshape(share, 2 * channels), state_weight, step_block, query_weight, spare, key_value_weight], 1
    )
    weight_mix = gather(jnp.concatenate([output_weight, mamba_weight], 0), "dp", 1)
    tokens_all, weight_in = entry_gather(tokens_in, weight_own, dp_size, group, 1)
    cot_mine, tokens_all, weight_in = lax.optimization_barrier((cotangent, tokens_all, weight_in))
    cot_all = gather(cot_mine, "tensor", 0)

    cosine, sine = angle_tables()
    key_head = (place * query_heads // (QUERY_HEADS // KEY_HEADS)).astype(jnp.int32).reshape(1)
    heads_map = (jnp.arange(channels)[None, :] // PM == jnp.arange(LANES)[:, None]).astype(BF16)
    conv_weight = jnp.concatenate(
        [conv_inner.reshape(KC + 1, channels), conv_state], 1
    ).astype(F32)
    conv_weight = jnp.pad(conv_weight, ((0, 8 - KC - 1), (0, 0)))
    heads_vec = jnp.pad(head_params, ((0, 5), (0, LANES - heads)))
    gate_row = gate_gain.astype(F32).reshape(1, channels)

    lin, first, gains = project(tokens_all, weight_in, mixer_cols // LANES - 1)
    gain_one, gain_two = gains[0:1], gains[1:2]
    query_block = mixer_cols // LANES
    ssm, mixed, square, states = mixer_forward(lin, segment_ids, conv_weight, heads_vec, heads_map, heads)
    attended = attend_forward(lin, query_block, lead, query_heads, key_head, segment_ids, cosine, sine)
    expand_own = jnp.moveaxis(expand_weight.reshape(share, 2, -1, HIDDEN_TILE), 1, 2).reshape(share, 2 * hidden)
    weight_expand = gather(expand_own, "dp", 0)
    weight_shrink = gather(shrink_weight, "dp", 1)
    mix_in, inverse = gate_norm(square, ssm, lin, gate_row, attended, group, 4)
    mix_in, cot_all = lax.optimization_barrier((mix_in, cot_all))
    second_all, middle = line_sum(
        mix_in, weight_mix, [tokens_in, gain_two], dot_columns, mix_finish,
        [jax.ShapeDtypeStruct((own_rows, model), F32)], group, model, 2, "mix_sum",
    )
    act, grad_hidden, ffn_part = feed_forward(second_all, cot_all, weight_expand, weight_shrink)
    grad_expand = mat_tn(second_all, grad_hidden).astype(BF16)
    grad_shrink = mat_tn(cot_all, act).astype(BF16)
    mix_all, grad_middle, ffn_sum = line_sum(
        grad_hidden, weight_expand, [cotangent, middle, gain_two], dot_rows, second_finish,
        [jax.ShapeDtypeStruct((own_rows, model), F32)], group, model, 3, "second_sum",
        pieces=[grad_expand, grad_shrink], dp_size=dp_size,
    )
    ffn_part, mix_all = lax.optimization_barrier((ffn_part, mix_all))
    ffn_out = scatter(ffn_part, "tensor", 0)

    grad_attended, grad_normed, cross = gate_back(mix_all, weight_mix, ssm, lin, gate_row, query_cols, group, 5)
    grad_mix_weight = mat_tn(mix_all, mix_in).astype(BF16)
    grad_lin, grad_conv, grad_heads, grad_gate_gain = mixer_backward(
        lin, segment_ids, conv_weight, heads_vec, heads_map, gate_row, grad_normed, inverse, cross,
        ssm, mixed, states, heads, lead,
    )
    grad_lin = attend_backward(
        lin, query_block, lead, query_heads, key_head, segment_ids, cosine, sine, grad_attended, grad_lin
    )
    piece = PM // dp_size
    by_owner = lambda array: jnp.moveaxis(array.reshape(array.shape[0], -1, dp_size, array.shape[-1] // dp_size), 2, 0)
    small = jnp.concatenate(
        [
            by_owner(grad_conv[: KC + 1, :channels].reshape(KC + 1, heads, PM)).reshape(dp_size, -1),
            by_owner(grad_gate_gain[0].reshape(1, heads, PM)).reshape(dp_size, -1),
            jnp.broadcast_to(grad_heads[None, :3, :heads], (dp_size, 3, heads)).reshape(dp_size, -1),
            by_owner(grad_conv[: KC + 1, channels:].reshape(KC + 1, 1, 2 * NS)).reshape(dp_size, -1),
        ],
        1,
    )
    conv_cut = (KC + 1) * heads * piece
    gain_cut = conv_cut + heads * piece
    head_cut = gain_cut + 3 * heads
    state_piece = 2 * NS // (dp_size * group)
    gain_piece = share // group
    small_cols = -(-head_cut // share)
    local = jnp.pad(small[:, :head_cut], ((0, 0), (0, small_cols * share - head_cut)))
    state_count = (KC + 1) * state_piece
    state_extra = -(-state_count // gain_piece)
    common = small[:, head_cut:].reshape(dp_size, KC + 1, group, state_piece).transpose(0, 2, 1, 3)
    common = jnp.pad(
        common.reshape(dp_size, group, state_count), ((0, 0), (0, 0), (0, state_extra * gain_piece - state_count))
    )
    small = jnp.concatenate(
        [
            local.reshape(model, small_cols),
            common.reshape(model, state_extra),
            jnp.zeros((model, LANES - small_cols - state_extra), F32),
        ],
        1,
    ).astype(BF16)
    gain_two_part = jnp.sum(
        expand_own.astype(F32) * ffn_sum[:, : 2 * hidden], 1
    ) / norm_second.astype(F32)
    gain_lanes = jnp.concatenate(
        [
            jnp.zeros((share, LANES - 2), F32),
            (1.0 / norm_first.astype(F32))[:, None],
            gain_two_part[:, None],
        ],
        1,
    )
    grad_in = mat_tn(first, grad_lin).astype(BF16)
    in_cols = weight_own.shape[1]
    grad_lin, ffn_out = lax.optimization_barrier((grad_lin, ffn_out))
    block_out = (middle + ffn_out.astype(F32)).astype(BF16)
    grad_tokens, in_sum, shared_sum = line_sum(
        grad_lin, weight_in, [tokens_in, grad_middle, gain_one], dot_rows, first_finish,
        [], group, model, 6, "first_sum", spread=False, pieces=[grad_in, grad_mix_weight, small], dp_size=dp_size,
        common=(weight_own, gain_lanes, ((2 * channels, 2 * NS), (lead, pair_cols))),
    )
    extra = in_sum[:, in_cols + query_cols + channels :][:, :small_cols].reshape(-1)
    rest = shared_sum[:, 2 * NS + pair_cols :]
    conv_inner_own = extra[:conv_cut].reshape(KC + 1, heads, piece)
    gate_gain_own = extra[conv_cut:gain_cut].reshape(heads, piece)
    head_own = extra[gain_cut:head_cut].reshape(3, heads)
    conv_state_own = (
        rest[:, small_cols : small_cols + state_extra].reshape(-1)[:state_count].reshape(KC + 1, state_piece)
    )
    mix_sum = in_sum[:, in_cols : in_cols + query_cols + channels].T
    return (
        block_out,
        grad_tokens,
        rest[:, LANES - 2],
        in_sum[:, mixer_cols : mixer_cols + query_cols],
        shared_sum[:, 2 * NS : 2 * NS + pair_cols],
        mix_sum[:query_cols],
        in_sum[:, : 2 * channels].reshape(share, 2, channels),
        shared_sum[:, : 2 * NS],
        in_sum[:, state_cols : state_cols + heads],
        conv_inner_own,
        conv_state_own,
        head_own,
        gate_gain_own,
        mix_sum[query_cols:],
        rest[:, LANES - 1],
        jnp.moveaxis(ffn_sum[:, : 2 * hidden].reshape(share, -1, 2, HIDDEN_TILE), 2, 1).reshape(share, 2, hidden),
        ffn_sum[:, 2 * hidden :].T,
    )


def solution(mesh):
    return jax.shard_map(
        per_device,
        mesh=mesh,
        in_specs=(
            P(("dp", "tensor"), None),
            P("dp"),
            P(("dp", "tensor"), None),
            P("dp"),
            P("dp", "tensor"),
            P("dp", None),
            P("tensor", "dp"),
            P("dp", None, "tensor"),
            P("dp", None),
            P("dp", "tensor"),
            P(None, "tensor", None),
            P(),
            P(None, "tensor"),
            P("tensor", None),
            P("tensor", "dp"),
            P("dp"),
            P("dp", None, "tensor"),
            P("tensor", "dp"),
        ),
        out_specs=(
            P(("dp", "tensor"), None),
            P(("dp", "tensor"), None),
            P(("dp", "tensor")),
            P("dp", "tensor"),
            P(("dp", "tensor"), None),
            P("tensor", "dp"),
            P("dp", None, "tensor"),
            P(("dp", "tensor"), None),
            P("dp", "tensor"),
            P(None, "tensor", "dp"),
            P(None, ("dp", "tensor")),
            P(None, "tensor"),
            P("tensor", "dp"),
            P("tensor", "dp"),
            P(("dp", "tensor")),
            P("dp", None, "tensor"),
            P("tensor", "dp"),
        ),
        check_vma=False,
    )
```

time: 1960 us -> 754 us (0.38)
  waiting for transfers between devices: 1200 us -> 54.6 us
  Pallas kernels: 0 us -> 574 us
  matrix products: 383 us -> 42.9 us
  other arithmetic: 147 us -> 9.55 us
  blocking collectives: 88.8 us -> 0 us
  local copies, waits for them, and re-layouts: 119 us -> 50 us
    pallas_call x0 -> x12, Pallas kernels: none -> 574 us  [the longest x3 335 us: line_sum(): pl.pallas_call(functools.partial(line_sum_kernel, group, spread, dot, fin...]
    reduce_scatter x12 -> x1, waiting for transfers between devices: 451 us -> 0.01 us  [scatter(): lax.psum_scatter(array, axis_name, scatter_dimension=axis, tiled=True)]
    all_gather x12 -> x4, waiting for transfers between devices: 435 us -> 53.8 us  [gather(): return lax.all_gather(array, axis_name, axis=axis, tiled=True)]
    dot_general x30 -> x0, matrix products: 320 us -> none  [the longest x3 148 us: state_space(): jnp.einsum('hts,shp->thp', mixing, inner_x, precision=PRECISION_HIGH)]
    unnamed x30 -> x5, waiting for transfers between devices: 309 us -> 0.75 us
    reduce_sum x11 -> x0, other arithmetic: 46.4 us -> none  [the longest x2 15 us: short_conv(): conv_weight[taps - 1 - lag_steps] * moved * keep_mask[:, None]]
    convert_element_type x13 -> x0, local copies, waits for them, and re-layouts: 42.4 us -> none  [the longest x1 21.7 us: per_device(): grad_expand_full.astype(jnp.bfloat16)]
    unnamed x2 -> x0, blocking collectives: 39.5 us -> none
  transfers between devices with their start and end apart: 27 -> 5, of which waited for: 21 -> 2; matrix products, arithmetic and copies ran while one was open for 20% -> 6% of each run, Pallas kernels for 0% -> 32%
where the time goes in v1:
time: 754 us; the launch traced here: 746 us
  Pallas kernels  574 us (76%)
  waiting for transfers between devices  54.6 us (7%)
  local copies, waits for them, and re-layouts  50 us (7%)
  matrix products  42.9 us (6%)
  between operations  14.8 us (2%)
  other arithmetic  9.55 us (1%)
    pallas_call x3, Pallas kernels, line_sum(): pl.pallas_call(functools.partial(line_sum_kernel, group, spread, dot, fin...  335 us
    pallas_call x1, Pallas kernels, entry_gather(): pl.pallas_call(functools.partial(entry_gather_kernel, group, parts), in_s...  84.4 us
    all_gather x4, waiting for transfers between devices, gather(): return lax.all_gather(array, axis_name, axis=axis, tiled=True)  53.8 us
    dot_general x4, matrix products, mat_tn(): lax.dot_general(left_side, right_side, (((0,), (0,)), ((), ())), preferre...  42.9 us
    pallas_call x1, Pallas kernels, mixer_backward(): pl.pallas_call(functools.partial(mixer_backward_kernel, heads), grid=(ste...  36.3 us
    pallas_call x1, Pallas kernels, feed_forward(): pl.pallas_call(feed_forward_kernel, grid=(hidden // HIDDEN_TILE,), in_spe...  32 us
    pallas_call x1, Pallas kernels, project(): pl.pallas_call(project_kernel, grid=(cols // tile,), in_specs=[whole_bloc...  20.8 us
    pallas_call x1, Pallas kernels, gate_back(): pl.pallas_call(functools.partial(gate_back_kernel, group, query_cols), gr...  17.9 us
  transfers between devices with their start and end apart: 5, of which 2 were waited for; matrix products, arithmetic and copies ran while one was open for 6% of the time, Pallas kernels for 32%

profile of v1, /device:TPU:0, one launch (start us, length us, event | category | flops | bytes accessed | tf_op | source)
XLA Modules:
  0.0 745.6 jit_solution(16207554434939123650)
XLA Ops:
  7.3 1.3 copy.94
  8.5 0.8 copy.69
  9.4 0.7 broadcast_in_dim.46
  10.1 0.8 broadcast_in_dim.47
  10.9 3.6 concatenate.26.weight_ref.refs_8_
  14.5 84.4 %entry_gather.1 = (bf16[4,256,2048]{2,1,0:T(8,128)(2,1)}, bf16[2048,3072]{1,0:T(8,128)(2,1)}) custom-call(bf16[256,2048]{1,0:T(8,128)(2,1)} %refs_2_.5, bf16[256,3072]{1,0:T(8,128)(2,1)} %concatenate.26.weight_ref.refs_8_), custom_call_target="tpu_custom_call" | custom-call | tf_op jit(solution)/shard_map/entry_gather/pallas_call | solution.py:832
  99.0 0.8 pad_maximum_fusion.2
  99.9 0.7 all-gather.11.cloned.1.call-update
  100.7 1.6 reshape.197
  102.4 0.2 copy.72.seg_ref.segb_ref
  102.7 0.7 reshape.214.gain_ref
  103.4 20.8 %project.1 = (f32[1024,3072]{1,0:T(8,128)}, bf16[1024,2048]{1,0:T(8,128)(2,1)}, f32[8,2048]{1,0:T(8,128)}) custom-call(bf16[1024,2048]{1,0:T(8,128)(2,1)} %bitcast.51, bf16[2048,3072]{1,0:T(8,128)(2,1)} %get-tuple-element.58.gains_ref.w_ref.refs_1_, bf16[2048,3072]{1,0:T(8,128)(2,1)} %get-tuple-element.58.gains_ref.w_ref.refs_1_), custom_call_target="tpu_custom_call" | custom-call | tf_op jit(solution)/shard_map/project/pallas_call | solution.py:1273
  124.2 14.3 %mixer_forward.1 = (f32[1024,768]{1,0:T(8,128)}, bf16[1024,1280]{1,0:T(8,128)(2,1)S(1)}, f32[8,1,128]{2,1,0:T(1,128)S(1)}, bf16[8,256,768]{2,1,0:T(8,128)(2,1)}) custom-call(f32[1024,3072]{1,0:T(8,128)} %get-tuple-element.59.lin_ref.q_ref.k_ref.v_ref.gate_ref.before_ref, s32[1024,1]{1,0:T(8,128)S(1)} %copy.72.seg_ref.segb_ref, s32[1,1024]{1,0:T(1,128)S(1)} %bitcast.42, ...), custom_call_target="tpu_custom_call" | custom-call | tf_op jit(solution)/shard_map/mixer_forward/pallas_call | solution.py:347
  138.5 1.5 copy-done
  140.1 1.9 fusion.1
  142.0 0.3 pad_maximum_fusion
  142.3 6.8 attend_forward.1.attended_ref
  149.2 0.8 copy-done.2
  149.9 13.6 %gate_norm.1 = (bf16[1024,1024]{1,0:T(8,128)(2,1)}, f32[8,1,128]{2,1,0:T(1,128)}) custom-call(f32[8,1,128]{2,1,0:T(1,128)} %copy-done.7, f32[1024,768]{1,0:T(8,128)} %get-tuple-element.61.ssm_ref, f32[1024,3072]{1,0:T(8,128)} %get-tuple-element.59.lin_ref.q_ref.k_ref.v_ref.gate_ref.before_ref, f32[1,768]{1,0:T(1,128)} %reshape.214.gain_ref, ...), custom_call_target="tpu_custom_call" | custom-call | tf_op jit(solution)/shard_map/gate_norm/pallas_call | solution.py:1345
  163.5 1.5 fusion.12
  165.0 15.5 %all-gather.5.cloned.1.call-done.cot_ref = bf16[1024,2048]{1,0:T(8,128)(2,1)} async-done(((bf16[256,2048]{1,0:T(8,128)(2,1)}), bf16[1024,2048]{1,0:T(8,128)(2,1)}) %all-gather.5.cloned.1.call-update) | async-done | bytes 4194320 | tf_op jit(solution)/shard_map/all_gather | solution.py:1516
  180.5 38.3 %all-gather.7.cloned.1.call-done.refs_1_.w_ref = bf16[1024,2048]{1,0:T(8,128)(2,1)} async-done(((bf16[1024,256]{1,0:T(8,128)(2,1)}), bf16[1024,2048]{1,0:T(8,128)(2,1)}) %all-gather.7.cloned.1.call-update) | async-done | bytes 4194320 | tf_op jit(solution)/shard_map/all_gather | solution.py:1516
  218.8 113.2 %mix_sum.1 = (bf16[4,256,2048]{2,1,0:T(8,128)(2,1)}, f32[256,2048]{1,0:T(8,128)}) custom-call(bf16[4,256,1024]{2,1,0:T(8,128)(2,1)} %bitcast.57, bf16[1024,2048]{1,0:T(8,128)(2,1)} %all-gather.7.cloned.1.call-done.refs_1_.w_ref, bf16[256,2048]{1,0:T(8,128)(2,1)} %refs_2_.5, f32[1,2048]{1,0:T(1,128)} %get-tuple-element.151.refs_3_.refs_4_), custom_call_target="tpu_custom_call" | custom-call | tf_op jit(solution)/shard_map/mix_sum/pallas_call | solution.py:1234
  332.1 32.0 %feed_forward.1 = (bf16[1024,1024]{1,0:T(8,128)(2,1)}, bf16[1024,2048]{1,0:T(8,128)(2,1)}, bf16[1024,2048]{1,0:T(8,128)(2,1)}) custom-call(bf16[1024,2048]{1,0:T(8,128)(2,1)} %bitcast.52, bf16[1024,2048]{1,0:T(8,128)(2,1)} %all-gather.5.cloned.1.call-done.cot_ref, bf16[2048,2048]{1,0:T(8,128)(2,1)} %all-gather.9.cloned.1.call-done.expand_ref.refs_1_, ...), custom_call_target="tpu_custom_call" | custom-call | tf_op jit(solution)/shard_map/feed_forward/pallas_call | solution.py:1461
  364.1 14.4 %convolution_convert_fusion.1.refs_5_ = bf16[2048,2048]{1,0:T(8,128)(2,1)} fusion(bf16[1024,2048]{1,0:T(8,128)(2,1)} %bitcast.53, bf16[1024,2048]{1,0:T(8,128)(2,1)} %get-tuple-element.70), kind=kOutput, calls=%fused_computation.1 | convolution fusion | flops 8594128896 | bytes 16777216 | tf_op jit(solution)/shard_map/dot_general | solution.py:42
  378.6 6.2 convolution_convert_fusion.3.refs_6_
  384.8 117.9 %second_sum.1 = (bf16[4,256,2048]{2,1,0:T(8,128)(2,1)}, f32[256,2048]{1,0:T(8,128)}, f32[256,3072]{1,0:T(8,128)}) custom-call(bf16[4,256,2048]{2,1,0:T(8,128)(2,1)} %bitcast.54, bf16[2048,2048]{1,0:T(8,128)(2,1)} %all-gather.9.cloned.1.call-done.expand_ref.refs_1_, bf16[256,2048]{1,0:T(8,128)(2,1)} %refs_2_.4, f32[256,2048]{1,0:T(8,128)} %get-tuple-element.66.refs_3_, ...), custom_call_target="tpu_custom_call" | custom-call | tf_op jit(solution)/shard_map/second_sum/pallas_call | solution.py:1234
  502.8 0.6 copy-done.26
  503.7 17.9 %gate_back.1 = (bf16[1024,256]{1,0:T(8,128)(2,1)}, f32[1024,768]{1,0:T(8,128)}, f32[8,1,128]{2,1,0:T(1,128)}) custom-call(bf16[1024,2048]{1,0:T(8,128)(2,1)} %bitcast.49, bf16[1024,2048]{1,0:T(8,128)(2,1)} %all-gather.7.cloned.1.call-done.refs_1_.w_ref, f32[1024,768]{1,0:T(8,128)} %get-tuple-element.61.ssm_ref, ...), custom_call_target="tpu_custom_call" | custom-call | tf_op jit(solution)/shard_map/gate_back/pallas_call | solution.py:1407
  521.7 0.7 copy-done.8
  522.3 36.3 %mixer_backward.1 = (bf16[1024,3072]{1,0:T(8,128)(2,1)}, f32[8,1280]{1,0:T(8,128)S(1)}, f32[8,128]{1,0:T(8,128)S(1)}, f32[8,768]{1,0:T(8,128)S(1)}) custom-call(f32[1024,3072]{1,0:T(8,128)} %get-tuple-element.59.lin_ref.q_ref.k_ref.v_ref.gate_ref.before_ref, f32[1024,3072]{1,0:T(8,128)} %get-tuple-element.59.lin_ref.q_ref.k_ref.v_ref.gate_ref.before_ref, ...), custom_call_target="tpu_custom_call" | custom-call | tf_op jit(solution)/shard_map/mixer_backward/pallas_call | solution.py:393
  559.0 1.9 reshape.205
  561.2 0.2 reshape_reshape.12
  561.8 1.8 reshape.203
  563.6 3.2 fusion.10
  566.9 4.1 reshape.211
  571.0 1.3 slice_bitcast_fusion
  572.3 1.3 copy.90
  573.6 12.7 %attend_backward.1 = bf16[1024,3072]{1,0:T(8,128)(2,1)} custom-call(s32[1]{0:T(128)} %bitcast.3.head_ref, f32[1024,3072]{1,0:T(8,128)} %get-tuple-element.59.lin_ref.q_ref.k_ref.v_ref.gate_ref.before_ref, f32[1024,3072]{1,0:T(8,128)} %get-tuple-element.59.lin_ref.q_ref.k_ref.v_ref.gate_ref.before_ref, ...), custom_call_target="tpu_custom_call", output_to_operand_aliasing={{}: (9, {})} | custom-call | tf_op jit(solution)/shard_map/attend_backward/pallas_call | solution.py:552
  586.3 0.8 pad_maximum_fusion.3.refs_9_
  587.1 1.1 maximum_maximum_fusion.refs_7_
  588.2 6.2 convolution_convert_fusion.2.refs_6_
  594.5 15.9 %convolution_convert_fusion.refs_5_ = bf16[2048,3072]{1,0:T(8,128)(2,1)} fusion(bf16[1024,2048]{1,0:T(8,128)(2,1)S(1)} %copy-done.27, bf16[1024,3072]{1,0:T(8,128)(2,1)S(1)} %bitcast.48), kind=kOutput, calls=%fused_computation | convolution fusion | flops 12891193344 | bytes 23068672 | tf_op jit(solution)/shard_map/dot_general | solution.py:42
  610.5 103.7 %first_sum.1 = (f32[256,2048]{1,0:T(8,128)}, f32[256,4224]{1,0:T(8,128)}, f32[64,1152]{1,0:T(8,128)}) custom-call(bf16[4,256,3072]{2,1,0:T(8,128)(2,1)} %bitcast.46, bf16[2048,3072]{1,0:T(8,128)(2,1)} %get-tuple-element.58.gains_ref.w_ref.refs_1_, bf16[256,2048]{1,0:T(8,128)(2,1)} %refs_2_.5, f32[256,2048]{1,0:T(8,128)} %get-tuple-element.84.refs_3_, ...), custom_call_target="tpu_custom_call" | custom-call | tf_op jit(solution)/shard_map/first_sum/pallas_call | solution.py:1234
  714.1 1.5 slice_reduce_fusion
  715.7 1.7 fusion.11
  717.4 1.8 slice.94
  719.2 1.3 slice_bitcast_fusion.1
  720.5 1.9 slice.98
  722.4 0.9 slice.100
  723.3 0.9 slice.101
  724.2 0.8 slice.102
  725.0 0.7 slice.103
  725.7 0.7 slice.104
  726.5 1.3 add_convert_fusion
  727.7 0.8 copy.85
  728.6 2.2 reshape.206
  730.8 0.7 copy.86
  731.5 0.7 copy.87
  732.3 0.7 reshape.208
  732.9 0.7 reshape.209
  733.7 0.7 copy.88
  734.3 1.1 copy.89
  735.5 3.1 copy.97
  (112 shorter events, 2.2 us)
Async XLA Ops:
  7.2 173.3 %all-gather.5.cloned.1.call-start = ((), (), s32[]{:S(2)}) async-start(), calls=%async_computation.1 | async-start | bytes 5242880 | tf_op jit(solution)/shard_map/all_gather | solution.py:1516
  7.2 91.8 %copy-start.19 = (bf16[768,256]{1,0:T(8,128)(2,1)S(1)}, bf16[768,256]{1,0:T(8,128)(2,1)}, u32[]{:S(2)}) copy-start(bf16[768,256]{1,0:T(8,128)(2,1)} %param.32) | copy-start | bytes 1179652
  7.2 91.8 %copy-start.20 = (bf16[256,256]{1,0:T(8,128)(2,1)S(1)}, bf16[256,256]{1,0:T(8,128)(2,1)}, u32[]{:S(2)}) copy-start(bf16[256,256]{1,0:T(8,128)(2,1)} %param.24) | copy-start | bytes 393220
  10.9 89.7 %copy-start.17 = (bf16[256,2,1024]{2,1,0:T(2,128)(2,1)S(1)}, bf16[256,2,1024]{2,1,0:T(2,128)(2,1)}, u32[]{:S(2)}) copy-start(bf16[256,2,1024]{2,1,0:T(2,128)(2,1)} %param.34) | copy-start | bytes 3145732
  14.5 87.8 %copy-start.4 = (s32[1024]{0:T(1024)S(1)}, s32[1024]{0:T(1024)}, u32[]{:S(2)}) copy-start(s32[1024]{0:T(1024)} %param.19) | copy-start | bytes 12292
  14.5 88.1 %copy-start.21 = (bf16[5,12,64]{2,1,0:T(8,128)(2,1)S(1)}, bf16[5,12,64]{2,1,0:T(8,128)(2,1)}, u32[]{:S(2)}) copy-start(bf16[5,12,64]{2,1,0:T(8,128)(2,1)} %param.28) | copy-start | bytes 23044
  14.5 88.2 %copy-start.23 = (bf16[12,64]{1,0:T(8,128)(2,1)S(1)}, bf16[12,64]{1,0:T(8,128)(2,1)}, u32[]{:S(2)}) copy-start(bf16[12,64]{1,0:T(8,128)(2,1)} %param.31) | copy-start | bytes 4612
  98.9 119.9 %all-gather.7.cloned.1.call-start = ((), (), s32[]{:S(2)}) async-start(), calls=%async_computation.2 | async-start | bytes 4718592 | tf_op jit(solution)/shard_map/all_gather | solution.py:1516
  99.9 232.2 %all-gather.11.cloned.1.call-start = ((), (), s32[]{:S(2)}) async-start(), calls=%async_computation.4 | async-start | bytes 4718592 | tf_op jit(solution)/shard_map/all_gather | solution.py:1516
  100.6 231.5 %all-gather.9.cloned.1.call-start = ((), (), s32[]{:S(2)}) async-start(), calls=%async_computation.3 | async-start | bytes 9437184 | tf_op jit(solution)/shard_map/all_gather | solution.py:1516
  102.3 508.2 %reduce-scatter.2.cloned.1.call-start = ((), (), s32[]{:S(2)}) async-start(), calls=%async_computation.5 | async-start | bytes 5242880 | tf_op jit(solution)/shard_map/reduce_scatter | solution.py:1520
  103.4 20.8 %copy-start.25 = (f32[3,12]{1,0:T(4,128)S(1)}, f32[3,12]{1,0:T(4,128)}, u32[]{:S(2)}) copy-start(f32[3,12]{1,0:T(4,128)} %param.30) | copy-start | bytes 436
  103.4 20.8 %copy-start.22 = (bf16[5,512]{1,0:T(8,128)(2,1)S(1)}, bf16[5,512]{1,0:T(8,128)(2,1)}, u32[]{:S(2)}) copy-start(bf16[5,512]{1,0:T(8,128)(2,1)} %param.29) | copy-start | bytes 15364
  138.5 1.5 copy-start
  140.0 9.1 %copy-start.7 = (f32[8,1,128]{2,1,0:T(1,128)}, f32[8,1,128]{2,1,0:T(1,128)S(1)}, u32[]{:S(2)}) copy-start(f32[8,1,128]{2,1,0:T(1,128)S(1)} %get-tuple-element.60.square_ref) | copy-start | bytes 12292
  149.1 0.8 copy-start.2
  364.1 14.5 %copy-start.11 = (bf16[1024,2048]{1,0:T(8,128)(2,1)S(1)}, bf16[1024,2048]{1,0:T(8,128)(2,1)}, u32[]{:S(2)}) copy-start(bf16[1024,2048]{1,0:T(8,128)(2,1)} %all-gather.5.cloned.1.call-done.cot_ref) | copy-start | bytes 12582916
  364.1 14.5 %copy-start.28 = (bf16[1024,1024]{1,0:T(8,128)(2,1)S(1)}, bf16[1024,1024]{1,0:T(8,128)(2,1)}, u32[]{:S(2)}) copy-start(bf16[1024,1024]{1,0:T(8,128)(2,1)} %get-tuple-element.71) | copy-start | bytes 6291460
  502.8 0.7 copy-start.26
  503.7 18.0 %copy-start.1 = (bf16[1024,1280]{1,0:T(8,128)(2,1)S(1)}, bf16[1024,1280]{1,0:T(8,128)(2,1)}, u32[]{:S(2)}) copy-start(bf16[1024,1280]{1,0:T(8,128)(2,1)} %copy-done) | copy-start | bytes 7864324
  503.7 18.0 %copy-start.5 = (f32[1,768]{1,0:T(1,128)S(1)}, f32[1,768]{1,0:T(1,128)}, u32[]{:S(2)}) copy-start(f32[1,768]{1,0:T(1,128)} %reshape.214.gain_ref) | copy-start | bytes 9220
  503.7 18.0 %copy-start.6 = (f32[8,1,128]{2,1,0:T(1,128)S(1)}, f32[8,1,128]{2,1,0:T(1,128)}, u32[]{:S(2)}) copy-start(f32[8,1,128]{2,1,0:T(1,128)} %get-tuple-element.76.inv_ref) | copy-start | bytes 12292
  521.7 0.7 copy-start.8
  522.3 41.2 %copy-start.9 = (bf16[256,2048]{1,0:T(8,128)(2,1)S(1)}, bf16[256,2048]{1,0:T(8,128)(2,1)}, u32[]{:S(2)}) copy-start(bf16[256,2048]{1,0:T(8,128)(2,1)} %reshape.197) | copy-start | bytes 3145732
  558.7 8.1 %copy-start.24 = (bf16[256]{0:T(256)(128)(2,1)S(1)}, bf16[256]{0:T(256)(128)(2,1)}, u32[]{:S(2)}) copy-start(bf16[256]{0:T(256)(128)(2,1)} %param.33) | copy-start | bytes 1540
  566.9 6.7 copy-start.3
  573.6 13.5 %copy-start.14 = (bf16[2048,2]{1,0:T(8,128)(2,1)S(1)}, bf16[2048,2]{1,0:T(8,128)(2,1)}, u32[]{:S(2)}) copy-start(bf16[2048,2]{1,0:T(8,128)(2,1)} %reshape.205) | copy-start | bytes 24580
  573.6 13.5 %copy-start.15 = (bf16[2048,3]{1,0:T(8,128)(2,1)S(1)}, bf16[2048,3]{1,0:T(8,128)(2,1)}, u32[]{:S(2)}) copy-start(bf16[2048,3]{1,0:T(8,128)(2,1)} %reshape.203) | copy-start | bytes 36868
  573.6 14.7 %copy-start.12 = (bf16[4,256,2048]{2,1,0:T(8,128)(2,1)S(1)}, bf16[4,256,2048]{2,1,0:T(8,128)(2,1)}, u32[]{:S(2)}) copy-start(bf16[4,256,2048]{2,1,0:T(8,128)(2,1)} %get-tuple-element.72) | copy-start | bytes 12582916
  573.6 14.7 %copy-start.16 = (bf16[1024,1024]{1,0:T(8,128)(2,1)S(1)}, bf16[1024,1024]{1,0:T(8,128)(2,1)}, u32[]{:S(2)}) copy-start(bf16[1024,1024]{1,0:T(8,128)(2,1)} %get-tuple-element.64) | copy-start | bytes 6291460
  587.1 7.4 slice-start
  588.2 6.2 slice-start.1
  588.2 6.2 copy-start.27
  717.4 9.1 %copy-start.10 = (f32[256,2048]{1,0:T(8,128)S(1)}, f32[256,2048]{1,0:T(8,128)}, u32[]{:S(2)}) copy-start(f32[256,2048]{1,0:T(8,128)} %get-tuple-element.66.refs_3_) | copy-start | bytes 6291460
  717.4 9.1 %copy-start.18 = (bf16[256,2048]{1,0:T(8,128)(2,1)S(1)}, bf16[256,2048]{1,0:T(8,128)(2,1)}, u32[]{:S(2)}) copy-start(bf16[256,2048]{1,0:T(8,128)(2,1)} %reduce-scatter.2.cloned.1.call-done) | copy-start | bytes 3145732
  720.5 7.2 copy-start.13
  727.7 6.6 slice-start.2
Sparse Core Ops, SparseCore 0:
  99.1 81.3 all-gather.4
  182.9 35.8 all-gather.6
  220.7 37.4 all-gather.10
  260.5 54.4 all-gather.8
  502.9 76.1 reduce-scatter.1

commit v2 on v1

--- a/solution.py
+++ b/solution.py
@@ -64,7 +64,7 @@
 
 
 def sigmoid(value):
-    return 1.0 / (1.0 + jnp.exp(-value))
+    return 0.5 + 0.5 * jnp.tanh(0.5 * value)
 
 
 def softplus(value):
@@ -191,7 +191,7 @@
 def mixer_backward_kernel(
     heads, lin_ref, before_ref, seg_ref, segb_ref, segr_ref, conv_ref, hp_ref, map_ref, gain_ref,
     gn_ref, inv_ref, cross_ref, ssm_ref, mixed_ref, states_ref,
-    dlin_ref, dconv_ref, dhp_ref, dgain_ref, dstate, dnext, seg_next,
+    dlin_ref, small_ref, dstate, dnext, seg_next, dconv_ref, dhp_ref, dgain_ref,
 ):
     channels = heads * PM
     rows = lin_ref.shape[0]
@@ -331,6 +331,15 @@
     dlin_ref[:, channels : 2 * channels + 2 * NS] = grad_inputs.astype(BF16)
     dnext[...] = grad_conv[:8]
     seg_next[...] = seg[:8]
+
+    @pl.when(pl.program_id(0) == pl.num_programs(0) - 1)
+    def _():
+        small_ref[...] = jnp.zeros_like(small_ref)
+        row = 0
+        for array in (dconv_ref, dhp_ref, dgain_ref):
+            for first in range(0, array.shape[1], LANES):
+                small_ref[row : row + 8, :] = array[:, first : first + LANES]
+                row += 8
 
 
 def whole_block(array):
@@ -378,7 +387,7 @@
 
 
 def mixer_backward(
-    lin, seg, conv_weight, heads_vec, heads_map, gain, grad_normed, inverse, cross, ssm, mixed, states, heads, lead
+    lin, seg, conv_weight, heads_vec, heads_map, gain, grad_normed, inverse, cross, ssm, mixed, states, heads, lead, share
 ):
     total = lin.shape[0]
     channels = heads * PM
@@ -412,20 +421,19 @@
         ],
         out_specs=[
             by_rows(lead),
-            pl.BlockSpec((8, mixed_width), lambda c: (0, 0)),
-            pl.BlockSpec((8, LANES), lambda c: (0, 0)),
-            pl.BlockSpec((8, channels), lambda c: (0, 0)),
+            pl.BlockSpec((share, LANES), lambda c: (0, 0)),
         ],
         out_shape=[
             jax.ShapeDtypeStruct((total, lin.shape[1]), BF16),
-            jax.ShapeDtypeStruct((8, mixed_width), F32),
-            jax.ShapeDtypeStruct((8, LANES), F32),
-            jax.ShapeDtypeStruct((8, channels), F32),
+            jax.ShapeDtypeStruct((share, LANES), F32),
         ],
         scratch_shapes=[
             pltpu.VMEM((NS, channels), F32),
             pltpu.VMEM((8, mixed_width), F32),
             pltpu.VMEM((8, 1), jnp.int32),
+            pltpu.VMEM((8, mixed_width), F32),
+            pltpu.VMEM((8, LANES), F32),
+            pltpu.VMEM((8, channels), F32),
         ],
         compiler_params=pltpu.CompilerParams(vmem_limit_bytes=48 << 20),
         name="mixer_backward",
@@ -634,69 +642,109 @@
     pl.semaphore_wait(barrier, count)
 
 
-def plane_gather_steps(own_ref, out_ref, local_sem, send_sem, recv_sem):
+def plane_gather_steps(pieces, local_sem, send_sem, recv_sem):
     owner = lax.axis_index("dp")
-    share = own_ref.shape[0]
     parts = PLANE_PARTS
-    rows = share // parts
     half = parts // 2
 
-    def copy(slot, origin, to, part, own=False):
-        block = out_ref.at[pl.ds(origin * share + part * rows, rows)]
-        return pltpu.make_async_remote_copy(
-            own_ref.at[pl.ds(part * rows, rows)] if own else block,
-            block,
-            send_sem.at[slot, part],
-            recv_sem.at[slot, part],
-            device_id={"dp": partner(owner, to)},
-            device_id_type=MESH,
-        )
-
-    keep = pltpu.make_async_copy(own_ref, out_ref.at[pl.ds(owner * share, share)], local_sem)
-    first = [
-        copy(slot, owner, to, part, True)
-        for part in range(parts)
-        for slot, to in ((1, ACROSS), (2, ALONG), (0, CORE))
-    ]
-    later = []
+    def copies(slot, origin, to, part, own=False):
+        result = []
+        for index, (own_ref, full_ref, by_rows) in enumerate(pieces):
+            share, cols = own_ref.shape
+            rows = share // parts
+            if by_rows:
+                block = full_ref.at[pl.ds(origin * share + part * rows, rows)]
+            else:
+                block = full_ref.at[pl.ds(part * rows, rows), pl.ds(pl.multiple_of(origin * cols, cols), cols)]
+            result.append(
+                pltpu.make_async_remote_copy(
+                    own_ref.at[pl.ds(part * rows, rows)] if own else block,
+                    block,
+                    send_sem.at[index, slot, part],
+                    recv_sem.at[index, slot, part],
+                    device_id={"dp": partner(owner, to)},
+                    device_id_type=MESH,
+                )
+            )
+        return result
+
+    def start(*args):
+        for item in copies(*args):
+            item.start()
+
+    def arrive(*args):
+        for item in copies(*args):
+            item.wait_recv()
+
+    def keeps():
+        result = []
+        for index, (own_ref, full_ref, by_rows) in enumerate(pieces):
+            share, cols = own_ref.shape
+            if by_rows:
+                block = full_ref.at[pl.ds(owner * share, share)]
+            else:
+                block = full_ref.at[:, pl.ds(pl.multiple_of(owner * cols, cols), cols)]
+            result.append(pltpu.make_async_copy(own_ref, block, local_sem.at[index]))
+        return result
 
     def begin():
-        keep.start()
-        for item in first:
+        for part in range(parts):
+            start(1, owner, ACROSS, part, True)
+            start(2, owner, ALONG, (part + half) % parts, True)
+            start(0, owner, CORE, part, True)
+        for item in keeps():
             item.start()
 
-    def go(item):
-        item.start()
-        later.append(item)
-
     def neighbours(part):
-        copy(1, owner, ACROSS, part, True).wait_recv()
-        if part < half:
-            go(copy(3, partner(owner, ACROSS), ALONG, part))
-        go(copy(4, partner(owner, ACROSS), CORE, part))
+        arrive(1, owner, ACROSS, part, True)
+
+        @pl.when(part < half)
+        def _():
+            start(3, partner(owner, ACROSS), ALONG, part)
+
+        start(4, partner(owner, ACROSS), CORE, part)
         other = (part + half) % parts
-        copy(2, owner, ALONG, other, True).wait_recv()
-        if other >= half:
-            go(copy(3, partner(owner, ALONG), ACROSS, other))
-        go(copy(5, partner(owner, ALONG), CORE, other))
-
-    def corner(part):
-        copy(3, partner(owner, ACROSS), ALONG if part < half else ACROSS, part).wait_recv()
-        go(copy(6, partner(owner, CORNER), CORE, part))
+        arrive(2, owner, ALONG, other, True)
+
+        @pl.when(part < half)
+        def _():
+            start(3, partner(owner, ALONG), ACROSS, other)
+
+        start(5, partner(owner, ALONG), CORE, other)
+
+    def corner(step):
+        for part in (step, step + half):
+            arrive(3, partner(owner, CORNER), ALONG, part)
+            start(6, partner(owner, CORNER), CORE, part)
 
     def end():
         for part in range(parts):
             for slot in (0, 4, 5, 6):
-                copy(slot, owner, CORE, part).wait_recv()
-        for item in first + later:
-            item.wait_send()
-        keep.wait()
+                arrive(slot, owner, CORE, part)
+            for slot in range(7):
+                for item in copies(slot, owner, CORE, part):
+                    item.wait_send()
+        for item in keeps():
+            item.wait()
 
     return begin, neighbours, corner, end
 
 
+def plane_gather_scratch(count):
+    return [
+        pltpu.SemaphoreType.DMA((count,)),
+        pltpu.SemaphoreType.DMA((count, 7, PLANE_PARTS)),
+        pltpu.SemaphoreType.DMA((count, 7, PLANE_PARTS)),
+    ]
+
+
+def plane_gather_plain(array, by_rows):
+    return gather(array, "dp", 0 if by_rows else 1)
+
+
 def entry_gather_kernel(
-    group, parts, own_ref, weight_ref, out_ref, full_ref, local_sem, send_sem, recv_sem, keep_sem, plane_send, plane_recv
+    group, parts, own_ref, weight_ref, out_ref, full_ref,
+    local_sem, send_sem, recv_sem, keep_sem, plane_send, plane_recv,
 ):
     place = lax.axis_index("tensor")
     rows = own_ref.shape[0] // parts
@@ -713,9 +761,9 @@
             device_id_type=MESH,
         )
 
-    begin, neighbours, corner, end = plane_gather_steps(weight_ref, full_ref, keep_sem, plane_send, plane_recv)
-    keep = pltpu.make_async_copy(own_ref, out_ref.at[place], local_sem)
-    keep.start()
+    begin, neighbours, corner, end = plane_gather_steps(
+        [(weight_ref, full_ref, True)], keep_sem, plane_send, plane_recv
+    )
     more = (place < group - 1, place > 0)
     for part in range(parts):
         for side in (0, 1):
@@ -725,10 +773,10 @@
                 copy(side, place, part, True).start()
 
     begin()
+    keep = pltpu.make_async_copy(own_ref, out_ref.at[place], local_sem)
+    keep.start()
     plane_steps = [functools.partial(neighbours, part) for part in range(PLANE_PARTS)] + [
-        functools.partial(corner, part)
-        for pair in range(PLANE_PARTS // 2)
-        for part in (pair, pair + PLANE_PARTS // 2)
+        functools.partial(corner, step) for step in range(PLANE_PARTS // 2)
     ]
     line_steps = (group - 1) * parts
     done = 0
@@ -817,7 +865,6 @@
     parts = 2
     anywhere = pl.BlockSpec(memory_space=pl.ANY)
     line_sems = pltpu.SemaphoreType.DMA((2, group, parts))
-    plane_sems = pltpu.SemaphoreType.DMA((7, PLANE_PARTS))
     if dp_size != 8:
         all_rows = pl.pallas_call(
             functools.partial(line_gather_kernel, group, parts),
@@ -828,18 +875,16 @@
             compiler_params=pltpu.CompilerParams(collective_id=collective_id, has_side_effects=True),
             name="line_gather",
         )(own)
-        return all_rows.reshape(group * rows, cols), gather(weight, "dp", 0)
+        return all_rows.reshape(group * rows, cols), plane_gather_plain(weight, True)
     all_rows, full = pl.pallas_call(
         functools.partial(entry_gather_kernel, group, parts),
         in_specs=[anywhere] * 2,
         out_specs=[anywhere] * 2,
         out_shape=[
             jax.ShapeDtypeStruct((group, rows, cols), own.dtype),
-            jax.ShapeDtypeStruct((dp_size * weight.shape[0], weight.shape[1]), weight.dtype),
+            jax.ShapeDtypeStruct((dp_size * weight.shape[0], weight.shape[1]), BF16),
         ],
-        scratch_shapes=[
-            pltpu.SemaphoreType.DMA, line_sems, line_sems, pltpu.SemaphoreType.DMA, plane_sems, plane_sems,
-        ],
+        scratch_shapes=[pltpu.SemaphoreType.DMA, line_sems, line_sems] + plane_gather_scratch(1),
         compiler_params=pltpu.CompilerParams(collective_id=collective_id, has_side_effects=True),
         name="entry_gather",
     )(own, weight)
@@ -856,7 +901,8 @@
     core_send, core_recv, stage_sem, x_send, x_recv, y_send, y_recv, last_send, last_recv = sems
 
     def block(piece_ref, target, side, part):
-        return piece_ref.at[pl.ds(target * share + side * half + part * rows, rows)]
+        first = 0 if piece_ref.shape[0] == share else target * share
+        return piece_ref.at[pl.ds(first + side * half + part * rows, rows)]
 
     def whole_core(part):
         return pltpu.make_async_remote_copy(
@@ -976,18 +1022,23 @@
     ]
 
 
-def common_sum(group, place, piece_out, weight_ref, lanes_ref, common_ref, outbox, inbox, send_sem, recv_sem, ranges):
+def gain_lanes(lanes, weight, summed, index):
+    own = jnp.sum(weight.astype(F32) * summed, 1, keepdims=True)
+    return jnp.where(iota(lanes.shape, 1) == index, own * lanes, lanes)
+
+
+def common_sum(group, place, ranges, state_rows, piece_out, lanes, refs):
+    common_ref, state_ref, gains_ref, outbox, inbox, send_sem, recv_sem = refs
     rows, width = common_ref.shape
+    start, stop = state_rows
     first = 0
-    for start, count in ranges:
-        outbox[:, first : first + count] = piece_out[:, start : start + count].astype(BF16)
+    for column, count in ranges:
+        outbox[:, first : first + count] = piece_out[:, column : column + count].astype(BF16)
         first += count
-    lanes = lanes_ref[...]
-    lane = iota(lanes.shape, 1)
-    own = jnp.sum(weight_ref[...].astype(F32) * piece_out[:, : weight_ref.shape[1]], 1, keepdims=True)
-    last = piece_out[:, piece_out.shape[1] - LANES :]
-    last = jnp.where(lane == LANES - 2, own * lanes, jnp.where(lane == LANES - 1, lanes, last))
-    outbox[:, first:] = last.astype(BF16)
+    state = piece_out[start:stop, piece_out.shape[1] - LANES :]
+    for peer in range(group):
+        outbox[peer * rows : peer * rows + stop - start, width : width + LANES] = state.astype(BF16)
+    outbox[:, width + LANES :] = lanes.astype(BF16)
     copies = []
     for hop in range(1, group):
         peer = lax.rem(place + hop, group)
@@ -1003,35 +1054,102 @@
     for hop, copy in enumerate(copies):
         copy.wait_recv()
         total = total + inbox[hop].astype(F32)
-    common_ref[...] = total
+    common_ref[...] = total[:, :width]
+    state_ref[...] = total[: stop - start, width : width + LANES]
+    gains_ref[...] = total[:, width + LANES :]
     for copy in copies:
         copy.wait_send()
 
 
-def common_plain(group, summed, weight, lanes, ranges):
-    own = jnp.sum(weight.astype(F32) * summed[:, : weight.shape[1]], 1, keepdims=True)
-    lane = jnp.arange(LANES)[None]
-    last = summed[:, summed.shape[1] - LANES :]
-    last = jnp.where(lane == LANES - 2, own * lanes, jnp.where(lane == LANES - 1, lanes, last))
-    parts = [summed[:, start : start + count] for start, count in ranges] + [last]
-    return scatter(jnp.concatenate(parts, 1).astype(BF16), "tensor", 0).astype(F32)
+PRODUCT_TURNS = (
+    (0, 2, 0, 0), (0, 2, 1, 1), (1, 2, 2, 0), (0, 2, 3, 2), (1, 3, 0, 1), (2, 3, 0, 0), (0, 3, 1, 3), (1, 3, 2, 2),
+    (2, 3, 2, 1), (1, 4, 0, 3), (2, 4, 0, 2), (2, 4, 3, 3),
+)
+
+
+def product_steps(left_refs, x_held, right_ref, piece_refs, left_held, made, left_sem, made_sem):
+    total, share = left_held.shape[2:]
+    owners = piece_refs[0].shape[0] // share
+    widths = [ref.shape[1] for ref in piece_refs]
+
+    def left_copy(tile, which):
+        cols = pl.ds(pl.multiple_of(tile * share, share), share)
+        slot = lax.rem(tile, 2)
+        return pltpu.make_async_copy(left_refs[which].at[:, cols], left_held.at[slot, which], left_sem.at[slot, which])
+
+    def made_copy(tile, which):
+        slot = lax.rem(tile, 2)
+        first = sum(widths[:which])
+        return pltpu.make_async_copy(
+            made.at[slot, :, pl.ds(first, widths[which])],
+            piece_refs[which].at[pl.ds(tile * share, share)],
+            made_sem.at[slot, which],
+        )
+
+    def load_left(tile):
+        left_copy(tile, 0).start()
+        left_copy(tile, 1).start()
+
+    def product(tile):
+        slot = lax.rem(tile, 2)
+
+        @pl.when(tile + 1 < owners)
+        def _():
+            load_left(tile + 1)
+
+        @pl.when(tile >= 2)
+        def _():
+            made_copy(tile - 2, 0).wait()
+            made_copy(tile - 2, 1).wait()
+
+        step = 512
+        for which in (0, 1):
+            left_copy(tile, which).wait()
+            left = left_held[slot, which]
+            first = sum(widths[:which])
+            for col in range(0, widths[which], step):
+                if which == 0:
+                    right = x_held[:, :, col : col + step].reshape(total, step)
+                else:
+                    right = right_ref[:, col : col + step]
+                made[slot, :, first + col : first + col + step] = mat_tn(left, right).astype(BF16)
+            made_copy(tile, which).start()
+
+    def end():
+        for tile in (owners - 2, owners - 1):
+            made_copy(tile, 0).wait()
+            made_copy(tile, 1).wait()
+
+    return load_left, product, end
 
 
 def line_sum_kernel(
-    group, spread, dot, finish, own_count, side_count, piece_count, ranges, *refs,
+    group, spread, by_rows, finish, own_count, side_count, piece_count, products, gather_rows, gain_index, ranges,
+    state_rows, *refs,
 ):
-    x_ref, w_ref, refs = refs[0], refs[1], refs[2:]
-    own_refs, refs = refs[:own_count], refs[own_count:]
-    piece_refs, refs = refs[:piece_count], refs[piece_count:]
-    if ranges:
-        weight_ref, lanes_ref, refs = refs[0], refs[1], refs[2:]
-    out_ref, refs = refs[0], refs[1:]
-    side_refs, refs = refs[:side_count], refs[side_count:]
+    def take(count):
+        nonlocal refs
+        taken, refs = refs[:count], refs[count:]
+        return taken
+
+    x_ref, w_ref = take(2)
+    own_refs = take(own_count)
+    if products:
+        left_refs, (right_ref,) = take(2), take(1)
+    else:
+        piece_refs = take(piece_count)
+    gather_refs = take(len(gather_rows))
     if piece_count:
-        piece_out, refs = refs[0], refs[1:]
-    if ranges:
-        common_ref, refs = refs[0], refs[1:]
-    held, part, sum_send, sum_recv, out_send, out_recv = refs[:6]
+        weight_ref, lanes_ref = take(2)
+    (out_ref,) = take(1)
+    side_refs = take(side_count)
+    if products:
+        piece_refs = take(piece_count)
+    if piece_count:
+        (piece_out,) = take(1)
+        common_refs = take(3 if ranges else 1)
+    full_refs = take(len(gather_rows))
+    x_held, w_held, load_sem, held, part, sum_send, sum_recv, out_send, out_recv = take(9)
     place = lax.axis_index("tensor")
     away = group - 1 - place
     chunks = LINE_CHUNKS
@@ -1041,17 +1159,37 @@
     tile = model // group
     more = (place < group - 1, place > 0)
     ahead = (place > 0, place < group - 1)
-    greet(place, group, lax.axis_index("dp"), piece_count > 0, bool(ranges))
+
+    def load_x():
+        return pltpu.make_async_copy(x_ref, x_held, load_sem.at[group])
+
+    def load_w(index):
+        cols = pl.ds(index * tile, tile)
+        if by_rows:
+            return pltpu.make_async_copy(w_ref.at[cols], w_held.at[cols], load_sem.at[index])
+        return pltpu.make_async_copy(w_ref.at[:, cols], w_held.at[:, cols], load_sem.at[index])
+
+    load_x().start()
+    for index in range(group):
+        load_w(index).start()
+    greet(place, group, lax.axis_index("dp"), piece_count + len(gather_rows) > 0, bool(ranges))
     if piece_count:
-        begin, add_core, add_near, add_last, end = plane_scatter_steps(
-            piece_refs, piece_out, *refs[6:11], refs[11:20]
-        )
+        begin, add_core, add_near, add_last, end = plane_scatter_steps(piece_refs, piece_out, *take(5), take(9))
+        if products:
+            load_left, product, product_end = product_steps(left_refs, x_held, right_ref, piece_refs, *take(4))
+            load_left(0)
+        else:
+            begin()
+    if gather_rows:
+        pieces = list(zip(gather_refs, full_refs, gather_rows))
+        begin, neighbours, corner, end = plane_gather_steps(pieces, *take(3))
         begin()
 
     def multiply(chunk, index):
-        left = x_ref[:, pl.ds(chunk * rows, rows), :].reshape(group * rows, x_ref.shape[2])
+        left = x_held[:, pl.ds(chunk * rows, rows), :].reshape(group * rows, x_ref.shape[2])
         cols = pl.ds(index * tile, tile)
-        part[lax.rem(chunk, 2), :, :, cols] = dot(left, w_ref, cols).reshape(group, rows, tile)
+        product = mat_nt(left, w_held[cols, :]) if by_rows else mat(left, w_held[:, cols])
+        part[lax.rem(chunk, 2), :, :, cols] = product.reshape(group, rows, tile)
 
     def sum_copy(side, chunk, share, half):
         block = held.at[chunk, share + 1 - side, pl.ds(half * few, few)]
@@ -1069,7 +1207,9 @@
             device_id={"tensor": place + 1 - 2 * side}, device_id_type=MESH,
         )
 
+    load_x().wait()
     for index in range(group):
+        load_w(index).wait()
         multiply(0, index)
 
     def pass_out(chunk, slot, half):
@@ -1145,29 +1285,65 @@
             def _():
                 multiply(chunk + 1, slot)
 
-            if piece_count and slot == 0:
+            if products:
+
+                @pl.when(chunk < 2)
+                def _():
+                    product(chunk * group + slot)
+
+                if slot == group - 1:
+
+                    @pl.when(chunk == 1)
+                    def _():
+                        product_end()
+                        begin()
+
+                for step, turn_chunk, turn_slot, index in PRODUCT_TURNS:
+                    if turn_slot == slot:
+
+                        @pl.when(chunk == turn_chunk)
+                        def _():
+                            (add_core, add_near, add_last)[step](index)
+
+            if piece_count and not products and slot == 0:
 
                 @pl.when(chunk < chunks)
                 def _():
                     add_core(chunk)
 
-            if piece_count and slot == group // 2:
+            if piece_count and not products and slot == group // 2:
 
                 @pl.when(chunk < chunks)
                 def _():
                     add_near(chunk)
 
-            if piece_count and slot == 1:
+            if piece_count and not products and slot == 1:
 
                 @pl.when(chunk > 0)
                 def _():
                     add_last(chunk - 1)
 
+            if gather_rows and slot == 1:
+
+                @pl.when(chunk < PLANE_PARTS)
+                def _():
+                    neighbours(chunk)
+
+            if gather_rows and slot == group // 2:
+
+                @pl.when((chunk >= PLANE_PARTS // 2) & (chunk < PLANE_PARTS))
+                def _():
+                    corner(chunk - PLANE_PARTS // 2)
+
         return carry
 
     lax.fori_loop(0, chunks + 1 if spread or piece_count else chunks, one_chunk, 0)
-    if ranges:
-        common_sum(group, place, piece_out, weight_ref, lanes_ref, common_ref, *refs[20:], ranges)
+    if piece_count:
+        lanes = gain_lanes(lanes_ref[...], weight_ref[...], piece_out[:, : weight_ref.shape[1]], gain_index)
+        if ranges:
+            common_sum(group, place, ranges, state_rows, piece_out, lanes, common_refs + take(4))
+        else:
+            common_refs[0][...] = lanes
 
     def finish_sends(chunk, carry):
         for half in (0, 1):
@@ -1193,10 +1369,13 @@
         return carry
 
     lax.fori_loop(0, chunks, finish_sends, 0)
+    if gather_rows:
+        end()
 
 
 def line_sum(
-    x, w, own, dot, finish, side_shapes, group, model, collective_id, name, spread=True, pieces=(), dp_size=8, common=None
+    x, w, own, by_rows, finish, side_shapes, group, model, collective_id, name, dp_size,
+    spread=True, pieces=(), products=(), gains=None, ranges=(), state_rows=None, gathers=(),
 ):
     total = x.shape[0]
     rows = total // group
@@ -1207,45 +1386,173 @@
     out_shape = [jax.ShapeDtypeStruct((group, rows, model), BF16) if spread else jax.ShapeDtypeStruct((rows, model), F32)]
     out_shape += side_shapes
     scratch = [
+        pltpu.VMEM((group, rows, x.shape[1]), BF16),
+        pltpu.VMEM(w.shape, BF16),
+        pltpu.SemaphoreType.DMA((group + 1,)),
         pltpu.VMEM((LINE_CHUNKS, group + 1, piece_rows, model), BF16),
         pltpu.VMEM((2, group, piece_rows, model), F32),
         sems, sems, sems, sems,
     ]
-    summed, ranges, last = None, (), []
-    if pieces and dp_size != 8:
-        summed = [jnp.concatenate([scatter(piece, "dp", 0) for piece in pieces], 1).astype(F32)]
-        if common:
-            summed.append(common_plain(group, summed[0], *common))
-        pieces, common = (), None
+    late = []
+    if products and (dp_size != 8 or group != 4):
+        lefts, right = products[:2], products[2]
+        pieces = [mat_tn(lefts[0], x).astype(BF16), mat_tn(lefts[1], right).astype(BF16)]
+        products = ()
+    if dp_size != 8:
+        if pieces:
+            share = pieces[0].shape[0] // dp_size
+            parts = [scatter(piece, "dp", 0) if piece.shape[0] > share else lax.psum(piece, "dp") for piece in pieces]
+            late = [jnp.concatenate(parts, 1).astype(F32)]
+            weight, lanes, gain_index = gains
+            lanes = gain_lanes(lanes, weight, late[0][:, : weight.shape[1]], gain_index)
+            if ranges:
+                columns = [late[0][:, start : start + count] for start, count in ranges]
+                late += [
+                    scatter(jnp.concatenate(columns, 1).astype(BF16), "tensor", 0).astype(F32),
+                    lax.psum(late[0][state_rows[0] : state_rows[1], late[0].shape[1] - LANES :], "tensor"),
+                    scatter(lanes, "tensor", 0),
+                ]
+            else:
+                late += [lanes]
+        late += [plane_gather_plain(array, kind) for array, kind in gathers]
+        pieces, ranges, gathers = (), (), ()
+    outs = [vmem] * len(out_shape)
+    last, gain_index = [], 0
+    piece_inputs, piece_specs = list(pieces), [anywhere] * len(pieces)
+    if products:
+        pieces = [jax.ShapeDtypeStruct((model, x.shape[1]), BF16), jax.ShapeDtypeStruct((model, products[2].shape[1]), BF16)]
+        piece_inputs, piece_specs = list(products), [anywhere, anywhere, vmem]
+        out_shape += pieces
+        outs += [anywhere] * 2
     if pieces:
         share, width = pieces[0].shape[0] // dp_size, sum(piece.shape[1] for piece in pieces)
+        last, gain_index = list(gains[:2]), gains[2]
         out_shape += [jax.ShapeDtypeStruct((share, width), F32)]
         scratch += plane_scatter_scratch(share, width)
-    if common:
-        ranges, last = common[2], list(common[:2])
-        common_width = sum(count for _, count in ranges) + LANES
-        out_shape += [jax.ShapeDtypeStruct((share // group, common_width), F32)]
-        scratch += [
-            pltpu.VMEM((share, common_width), BF16),
-            pltpu.VMEM((group - 1, share // group, common_width), BF16),
-            pltpu.SemaphoreType.DMA((group - 1,)),
-            pltpu.SemaphoreType.DMA((group - 1,)),
-        ]
+        if products:
+            scratch += [
+                pltpu.VMEM((2, 2, total, share), BF16),
+                pltpu.VMEM((2, share, width), BF16),
+                pltpu.SemaphoreType.DMA((2, 2)),
+                pltpu.SemaphoreType.DMA((2, 2)),
+            ]
+        if ranges:
+            common_width = sum(count for _, count in ranges)
+            out_shape += [
+                jax.ShapeDtypeStruct((share // group, common_width), F32),
+                jax.ShapeDtypeStruct((state_rows[1] - state_rows[0], LANES), F32),
+                jax.ShapeDtypeStruct((share // group, LANES), F32),
+            ]
+            scratch += [
+                pltpu.VMEM((share, common_width + 2 * LANES), BF16),
+                pltpu.VMEM((group - 1, share // group, common_width + 2 * LANES), BF16),
+                pltpu.SemaphoreType.DMA((group - 1,)),
+                pltpu.SemaphoreType.DMA((group - 1,)),
+            ]
+        else:
+            out_shape += [jax.ShapeDtypeStruct((share, LANES), F32)]
+        outs += [vmem] * (len(out_shape) - len(outs))
+    if gathers:
+        for array, kind in gathers:
+            shape = (dp_size * array.shape[0], array.shape[1]) if kind else (array.shape[0], dp_size * array.shape[1])
+            out_shape += [jax.ShapeDtypeStruct(shape, BF16)]
+            outs += [anywhere]
+        scratch += plane_gather_scratch(len(gathers))
     results = pl.pallas_call(
-        functools.partial(line_sum_kernel, group, spread, dot, finish, len(own), len(side_shapes), len(pieces), ranges),
-        in_specs=[vmem] * (2 + len(own)) + [anywhere] * len(pieces) + [vmem] * len(last),
-        out_specs=[vmem] * len(out_shape),
+        functools.partial(
+            line_sum_kernel, group, spread, by_rows, finish, len(own), len(side_shapes), len(pieces), bool(products),
+            tuple(kind for _, kind in gathers), gain_index, ranges, state_rows,
+        ),
+        in_specs=[anywhere] * 2 + [vmem] * len(own) + piece_specs + [anywhere] * len(gathers) + [vmem] * len(last),
+        out_specs=outs,
         out_shape=out_shape,
         scratch_shapes=scratch,
         compiler_params=pltpu.CompilerParams(
-            collective_id=collective_id, has_side_effects=True, vmem_limit_bytes=60 << 20
+            collective_id=collective_id, has_side_effects=True, vmem_limit_bytes=62 << 20
         ),
         name=name,
-    )(x.reshape(group, rows, x.shape[1]), w, *own, *pieces, *last)
+    )(x.reshape(group, rows, x.shape[1]), w, *own, *piece_inputs, *[array for array, _ in gathers], *last)
     results = list(results)
     if spread:
         results[0] = results[0].reshape(total, model)
-    return results if summed is None else results + summed
+    if products:
+        del results[1 + len(side_shapes) : 3 + len(side_shapes)]
+    return results + late
+
+
+def unpack_kernel(
+    heads, query_cols, first_query, dp_size, group, in_ref, ffn_ref, common_ref, state_ref, gains_ref,
+    gain_one, query, pair, output, inner, state, step, conv_inner, conv_state, head, gate_gain, mamba, gain_two,
+    expand, shrink,
+):
+    owner, place = lax.axis_index("dp"), lax.axis_index("tensor")
+    channels = heads * PM
+    hidden = shrink.shape[0]
+    state_cols = 2 * channels + 2 * NS
+    inner[:, 0, :] = in_ref[:, :channels]
+    inner[:, 1, :] = in_ref[:, channels : 2 * channels]
+    step[...] = in_ref[:, state_cols : state_cols + heads]
+    query[...] = in_ref[:, first_query : first_query + query_cols]
+    first = in_ref.shape[1] - LANES - query_cols - channels
+    for row in range(0, query_cols, LANES):
+        output[row : row + LANES, :] = in_ref[:, first + row : first + row + LANES].T
+    first += query_cols
+    for row in range(0, channels, LANES):
+        mamba[row : row + LANES, :] = in_ref[:, first + row : first + row + LANES].T
+    for tile in range(hidden // HIDDEN_TILE):
+        cols = slice(tile * HIDDEN_TILE, (tile + 1) * HIDDEN_TILE)
+        for kind in (0, 1):
+            start = (2 * tile + kind) * HIDDEN_TILE
+            expand[:, kind, cols] = ffn_ref[:, start : start + HIDDEN_TILE]
+    for row in range(0, hidden, LANES):
+        shrink[row : row + LANES, :] = ffn_ref[:, 2 * hidden + row : 2 * hidden + row + LANES].T
+    state[...] = common_ref[:, : 2 * NS]
+    pair[...] = common_ref[:, 2 * NS :]
+    for lane, gain in ((0, gain_one), (1, gain_two)):
+        column = gains_ref[:, lane : lane + 1]
+        rows = column.shape[0]
+        gain[...] = jnp.sum(jnp.where(iota((rows, rows), 0) == iota((rows, rows), 1), column, 0.0), 0, keepdims=True)
+    piece = PM // dp_size
+    last = in_ref.shape[1] - LANES
+    gate_first = (channels + 2 * NS) // LANES * 8 + 8
+    head[...] = in_ref[gate_first - 8 : gate_first - 5, last : last + heads]
+    for index in range(heads // 2):
+        for start, rows, target in ((0, KC + 1, conv_inner), (gate_first, 1, gate_gain)):
+            block = in_ref[start + 8 * index : start + 8 * index + 8, last:]
+            block = pltpu.roll(block, lax.rem(LANES - owner * piece, LANES), 1)
+            for side in (0, 1):
+                values = block[:rows, side * PM : side * PM + piece]
+                if rows == 1:
+                    target[2 * index + side : 2 * index + side + 1, :] = values
+                else:
+                    target[:, 2 * index + side, :] = values
+    width = conv_state.shape[1]
+    column = (owner * group + place) * width
+    block = state_ref[pl.ds(pl.multiple_of(column // LANES * 8, 8), 8), :]
+    block = pltpu.roll(block, lax.rem(LANES - lax.rem(column, LANES), LANES), 1)
+    conv_state[...] = block[: KC + 1, :width]
+
+
+def unpack(in_sum, ffn_sum, common, state, gains, heads, query_cols, first_query, hidden, dp_size, group):
+    share, rows, channels, own_cols = in_sum.shape[0], common.shape[0], heads * PM, in_sum.shape[0]
+    vmem = pl.BlockSpec(memory_space=pltpu.VMEM)
+    shapes = [
+        (1, rows), (share, query_cols), (rows, common.shape[1] - 2 * NS), (query_cols, own_cols), (share, 2, channels),
+        (rows, 2 * NS), (share, heads), (KC + 1, heads, PM // dp_size), (KC + 1, 2 * NS // (dp_size * group)),
+        (3, heads), (heads, PM // dp_size), (channels, own_cols), (1, rows), (share, 2, hidden), (hidden, own_cols),
+    ]
+    results = list(
+        pl.pallas_call(
+            functools.partial(unpack_kernel, heads, query_cols, first_query, dp_size, group),
+            in_specs=[vmem] * 5,
+            out_specs=[vmem] * len(shapes),
+            out_shape=[jax.ShapeDtypeStruct(shape, F32) for shape in shapes],
+            compiler_params=pltpu.CompilerParams(vmem_limit_bytes=48 << 20),
+            name="unpack",
+        )(in_sum, ffn_sum, common, state, gains)
+    )
+    results[0], results[12] = results[0].reshape(rows), results[12].reshape(rows)
+    return results
 
 
 def project_kernel(tokens_ref, gains_ref, w_ref, lin_ref, first_ref, gain_rows_ref):
@@ -1575,114 +1882,52 @@
     ssm, mixed, square, states = mixer_forward(lin, segment_ids, conv_weight, heads_vec, heads_map, heads)
     attended = attend_forward(lin, query_block, lead, query_heads, key_head, segment_ids, cosine, sine)
     expand_own = jnp.moveaxis(expand_weight.reshape(share, 2, -1, HIDDEN_TILE), 1, 2).reshape(share, 2 * hidden)
-    weight_expand = gather(expand_own, "dp", 0)
-    weight_shrink = gather(shrink_weight, "dp", 1)
     mix_in, inverse = gate_norm(square, ssm, lin, gate_row, attended, group, 4)
-    mix_in, cot_all = lax.optimization_barrier((mix_in, cot_all))
-    second_all, middle = line_sum(
-        mix_in, weight_mix, [tokens_in, gain_two], dot_columns, mix_finish,
-        [jax.ShapeDtypeStruct((own_rows, model), F32)], group, model, 2, "mix_sum",
+    second_all, middle, weight_expand, weight_shrink = line_sum(
+        mix_in, weight_mix, [tokens_in, gain_two], False, mix_finish,
+        [jax.ShapeDtypeStruct((own_rows, model), F32)], group, model, 2, "mix_sum", dp_size,
+        gathers=[(expand_own, True), (shrink_weight, False)],
     )
     act, grad_hidden, ffn_part = feed_forward(second_all, cot_all, weight_expand, weight_shrink)
-    grad_expand = mat_tn(second_all, grad_hidden).astype(BF16)
-    grad_shrink = mat_tn(cot_all, act).astype(BF16)
-    mix_all, grad_middle, ffn_sum = line_sum(
-        grad_hidden, weight_expand, [cotangent, middle, gain_two], dot_rows, second_finish,
-        [jax.ShapeDtypeStruct((own_rows, model), F32)], group, model, 3, "second_sum",
-        pieces=[grad_expand, grad_shrink], dp_size=dp_size,
+    lanes = jnp.concatenate(
+        [
+            (1.0 / norm_first.astype(F32))[:, None],
+            (1.0 / norm_second.astype(F32))[:, None],
+            jnp.zeros((share, LANES - 2), F32),
+        ],
+        1,
+    )
+    mix_all, grad_middle, ffn_sum, lanes = line_sum(
+        grad_hidden, weight_expand, [cotangent, middle, gain_two], True, second_finish,
+        [jax.ShapeDtypeStruct((own_rows, model), F32)], group, model, 3, "second_sum", dp_size,
+        products=(second_all, cot_all, act), gains=(expand_own, lanes, 1),
     )
     ffn_part, mix_all = lax.optimization_barrier((ffn_part, mix_all))
     ffn_out = scatter(ffn_part, "tensor", 0)
 
     grad_attended, grad_normed, cross = gate_back(mix_all, weight_mix, ssm, lin, gate_row, query_cols, group, 5)
     grad_mix_weight = mat_tn(mix_all, mix_in).astype(BF16)
-    grad_lin, grad_conv, grad_heads, grad_gate_gain = mixer_backward(
+    grad_lin, small = mixer_backward(
         lin, segment_ids, conv_weight, heads_vec, heads_map, gate_row, grad_normed, inverse, cross,
-        ssm, mixed, states, heads, lead,
+        ssm, mixed, states, heads, lead, share,
     )
     grad_lin = attend_backward(
         lin, query_block, lead, query_heads, key_head, segment_ids, cosine, sine, grad_attended, grad_lin
     )
-    piece = PM // dp_size
-    by_owner = lambda array: jnp.moveaxis(array.reshape(array.shape[0], -1, dp_size, array.shape[-1] // dp_size), 2, 0)
-    small = jnp.concatenate(
-        [
-            by_owner(grad_conv[: KC + 1, :channels].reshape(KC + 1, heads, PM)).reshape(dp_size, -1),
-            by_owner(grad_gate_gain[0].reshape(1, heads, PM)).reshape(dp_size, -1),
-            jnp.broadcast_to(grad_heads[None, :3, :heads], (dp_size, 3, heads)).reshape(dp_size, -1),
-            by_owner(grad_conv[: KC + 1, channels:].reshape(KC + 1, 1, 2 * NS)).reshape(dp_size, -1),
-        ],
-        1,
-    )
-    conv_cut = (KC + 1) * heads * piece
-    gain_cut = conv_cut + heads * piece
-    head_cut = gain_cut + 3 * heads
-    state_piece = 2 * NS // (dp_size * group)
-    gain_piece = share // group
-    small_cols = -(-head_cut // share)
-    local = jnp.pad(small[:, :head_cut], ((0, 0), (0, small_cols * share - head_cut)))
-    state_count = (KC + 1) * state_piece
-    state_extra = -(-state_count // gain_piece)
-    common = small[:, head_cut:].reshape(dp_size, KC + 1, group, state_piece).transpose(0, 2, 1, 3)
-    common = jnp.pad(
-        common.reshape(dp_size, group, state_count), ((0, 0), (0, 0), (0, state_extra * gain_piece - state_count))
-    )
-    small = jnp.concatenate(
-        [
-            local.reshape(model, small_cols),
-            common.reshape(model, state_extra),
-            jnp.zeros((model, LANES - small_cols - state_extra), F32),
-        ],
-        1,
-    ).astype(BF16)
-    gain_two_part = jnp.sum(
-        expand_own.astype(F32) * ffn_sum[:, : 2 * hidden], 1
-    ) / norm_second.astype(F32)
-    gain_lanes = jnp.concatenate(
-        [
-            jnp.zeros((share, LANES - 2), F32),
-            (1.0 / norm_first.astype(F32))[:, None],
-            gain_two_part[:, None],
-        ],
-        1,
-    )
     grad_in = mat_tn(first, grad_lin).astype(BF16)
-    in_cols = weight_own.shape[1]
     grad_lin, ffn_out = lax.optimization_barrier((grad_lin, ffn_out))
     block_out = (middle + ffn_out.astype(F32)).astype(BF16)
-    grad_tokens, in_sum, shared_sum = line_sum(
-        grad_lin, weight_in, [tokens_in, grad_middle, gain_one], dot_rows, first_finish,
-        [], group, model, 6, "first_sum", spread=False, pieces=[grad_in, grad_mix_weight, small], dp_size=dp_size,
-        common=(weight_own, gain_lanes, ((2 * channels, 2 * NS), (lead, pair_cols))),
-    )
-    extra = in_sum[:, in_cols + query_cols + channels :][:, :small_cols].reshape(-1)
-    rest = shared_sum[:, 2 * NS + pair_cols :]
-    conv_inner_own = extra[:conv_cut].reshape(KC + 1, heads, piece)
-    gate_gain_own = extra[conv_cut:gain_cut].reshape(heads, piece)
-    head_own = extra[gain_cut:head_cut].reshape(3, heads)
-    conv_state_own = (
-        rest[:, small_cols : small_cols + state_extra].reshape(-1)[:state_count].reshape(KC + 1, state_piece)
-    )
-    mix_sum = in_sum[:, in_cols : in_cols + query_cols + channels].T
-    return (
-        block_out,
-        grad_tokens,
-        rest[:, LANES - 2],
-        in_sum[:, mixer_cols : mixer_cols + query_cols],
-        shared_sum[:, 2 * NS : 2 * NS + pair_cols],
-        mix_sum[:query_cols],
-        in_sum[:, : 2 * channels].reshape(share, 2, channels),
-        shared_sum[:, : 2 * NS],
-        in_sum[:, state_cols : state_cols + heads],
-        conv_inner_own,
-        conv_state_own,
-        head_own,
-        gate_gain_own,
-        mix_sum[query_cols:],
-        rest[:, LANES - 1],
-        jnp.moveaxis(ffn_sum[:, : 2 * hidden].reshape(share, -1, 2, HIDDEN_TILE), 2, 1).reshape(share, 2, hidden),
-        ffn_sum[:, 2 * hidden :].T,
-    )
+    grad_tokens, in_sum, common, state, gain_sums = line_sum(
+        grad_lin, weight_in, [tokens_in, grad_middle, gain_one], True, first_finish,
+        [], group, model, 6, "first_sum", dp_size, spread=False,
+        pieces=[grad_in, grad_mix_weight, small.astype(BF16)], gains=(weight_own, lanes, 0),
+        ranges=((2 * channels, 2 * NS), (lead, pair_cols)),
+        state_rows=(channels // LANES * 8, (channels + 2 * NS) // LANES * 8),
+    )
+    grads = unpack(
+        in_sum, ffn_sum, common, state, gain_sums, heads, query_cols, mixer_cols, hidden, dp_size, group
+    )
+    return (block_out, grad_tokens, *grads)
 
 
 def solution(mesh):

time: 754 us -> 666 us (0.88)
  waiting for transfers between devices: 54.6 us -> 0.07 us
  local copies, waits for them, and re-layouts: 50 us -> 22.2 us
  matrix products: 42.9 us -> 24.8 us
  Pallas kernels: 574 us -> 588 us
    all_gather x4 -> x2, waiting for transfers between devices: 53.8 us -> 0.02 us  [gather(): return lax.all_gather(array, axis_name, axis=axis, tiled=True)]
    dot_general x4 -> x2, matrix products: 42.9 us -> 24.8 us  [mat_tn(): lax.dot_general(left_side, right_side, (((0,), (0,)), ((), ())), preferre...]
    pallas_call x3 -> x4, Pallas kernels: 335 us -> 353 us  [the longest x3 347 us: line_sum(): pl.pallas_call(functools.partial(line_sum_kernel, group, spread, by_rows,...]
    reshape x10 -> x0, local copies, waits for them, and re-layouts: 11.7 us -> none  [the longest x1 4.06 us: per_device(): ffn_sum[:, :2 * hidden].reshape(share, -1, 2, HIDDEN_TILE)]
    slice x16 -> x0, local copies, waits for them, and re-layouts: 11 us -> none  [the longest x1 1.89 us: per_device(): in_sum[:, :2 * channels].reshape(share, 2, channels)]
  transfers between devices with their start and end apart: 5 -> 3, of which waited for: 2 -> 0; matrix products, arithmetic and copies ran while one was open for 6% -> 6% of each run, Pallas kernels for 32% -> 49%
where the time goes in v2:
time: 666 us; the launch traced here: 658 us
  Pallas kernels  588 us (88%)
  matrix products  24.8 us (4%)
  local copies, waits for them, and re-layouts  22.2 us (3%)
  between operations  14.6 us (2%)
  other arithmetic  8.08 us (1%)
    pallas_call x3, Pallas kernels, line_sum(): pl.pallas_call(functools.partial(line_sum_kernel, group, spread, by_rows,...  347 us
    pallas_call x1, Pallas kernels, entry_gather(): pl.pallas_call(functools.partial(entry_gather_kernel, group, parts), in_s...  84.3 us
    pallas_call x1, Pallas kernels, mixer_backward(): pl.pallas_call(functools.partial(mixer_backward_kernel, heads), grid=(ste...  36.1 us
    pallas_call x1, Pallas kernels, feed_forward(): pl.pallas_call(feed_forward_kernel, grid=(hidden // HIDDEN_TILE,), in_spe...  31.7 us
    dot_general x2, matrix products, mat_tn(): lax.dot_general(left_side, right_side, (((0,), (0,)), ((), ())), preferre...  24.8 us
    pallas_call x1, Pallas kernels, project(): pl.pallas_call(project_kernel, grid=(cols // tile,), in_specs=[whole_bloc...  20.6 us
    pallas_call x1, Pallas kernels, gate_back(): pl.pallas_call(functools.partial(gate_back_kernel, group, query_cols), gr...  16.8 us
    pallas_call x1, Pallas kernels, mixer_forward(): pl.pallas_call(functools.partial(mixer_forward_kernel, heads), grid=(step...  14.2 us
  transfers between devices with their start and end apart: 3, of which 0 were waited for; matrix products, arithmetic and copies ran while one was open for 6% of the time, Pallas kernels for 49%

profile of v2, /device:TPU:0, one launch (start us, length us, event | category | flops | bytes accessed | tf_op | source)
XLA Modules:
  0.0 658.0 jit_solution(18438546619036712420)
XLA Ops:
  7.2 0.0 all-gather.3.cloned.1.call-start
  7.2 1.9 pad_maximum_fusion.2
  9.1 0.0 all-gather.3.cloned.1.call-update
  9.1 0.0 all-gather.5.cloned.1.call-start
  9.2 0.8 copy.41
  10.0 0.7 broadcast_in_dim.32
  10.8 0.8 broadcast_in_dim.33
  11.5 0.0 copy-start.21
  11.5 0.0 copy-start.19
  11.5 0.0 copy-start.23
  11.6 0.0 copy-start.24
  11.6 0.0 copy-start.6
  11.6 1.2 copy.55
  12.8 0.0 copy-start.18
  12.9 0.0 copy-start.22
  12.9 3.6 concatenate.18.weight_ref.refs_8_
  16.5 84.3 %entry_gather.1 = (bf16[4,256,2048]{2,1,0:T(8,128)(2,1)}, bf16[2048,3072]{1,0:T(8,128)(2,1)}) custom-call(bf16[256,2048]{1,0:T(8,128)(2,1)} %refs_2_.5, bf16[256,3072]{1,0:T(8,128)(2,1)} %concatenate.18.weight_ref.refs_8_), custom_call_target="tpu_custom_call" | custom-call | tf_op jit(solution)/shard_map/entry_gather/pallas_call | solution.py:879
  100.8 0.0 all-gather.5.cloned.1.call-update
  100.8 0.0 reduce-scatter.2.cloned.1.call-start
  100.9 0.0 copy-done.21
  100.9 0.7 reshape.155.gain_ref
  101.6 0.1 reshape.141
  101.7 0.1 copy.48
  101.8 0.1 copy.47
  102.0 0.2 copy.44.seg_ref.segb_ref
  102.2 0.0 copy-done.18
  102.2 1.6 reshape.147.refs_4_.refs_8_
  103.8 0.1 pad.15.clone
  103.9 20.6 %project.1 = (f32[1024,3072]{1,0:T(8,128)}, bf16[1024,2048]{1,0:T(8,128)(2,1)}, f32[8,2048]{1,0:T(8,128)}) custom-call(bf16[1024,2048]{1,0:T(8,128)(2,1)} %bitcast.30, bf16[2048,3072]{1,0:T(8,128)(2,1)} %get-tuple-element.74.gains_ref.w_ref.refs_1_, bf16[2048,3072]{1,0:T(8,128)(2,1)} %get-tuple-element.74.gains_ref.w_ref.refs_1_), custom_call_target="tpu_custom_call" | custom-call | tf_op jit(solution)/shard_map/project/pallas_call | solution.py:1580
  124.5 1.9 fusion.1
  126.4 0.3 pad_maximum_fusion
  126.8 0.0 copy-start.20
  126.8 6.8 %attend_forward.1.attended_ref = bf16[1024,256]{1,0:T(8,128)(2,1)S(1)} custom-call(s32[1]{0:T(128)} %bitcast.3.head_ref, f32[1024,3072]{1,0:T(8,128)} %get-tuple-element.75.lin_ref.q_ref.k_ref.v_ref.gate_ref.before_ref, f32[1024,3072]{1,0:T(8,128)} %get-tuple-element.75.lin_ref.q_ref.k_ref.v_ref.gate_ref.before_ref, ...), custom_call_target="tpu_custom_call" | custom-call | tf_op jit(solution)/shard_map/attend_forward/pallas_call | solution.py:544
  133.6 0.0 copy-start.3
  133.7 14.2 %mixer_forward.1 = (f32[1024,768]{1,0:T(8,128)}, bf16[1024,1280]{1,0:T(8,128)(2,1)S(1)}, f32[8,1,128]{2,1,0:T(1,128)S(1)}, bf16[8,256,768]{2,1,0:T(8,128)(2,1)}) custom-call(f32[1024,3072]{1,0:T(8,128)} %get-tuple-element.75.lin_ref.q_ref.k_ref.v_ref.gate_ref.before_ref, s32[1024,1]{1,0:T(8,128)S(1)} %copy.44.seg_ref.segb_ref, s32[1,1024]{1,0:T(1,128)S(1)} %bitcast.24, ...), custom_call_target="tpu_custom_call" | custom-call | tf_op jit(solution)/shard_map/mixer_forward/pallas_call | solution.py:356
  147.9 1.5 copy-done.1
  149.5 0.6 copy-done.12
  150.1 12.4 %gate_norm.1 = (bf16[1024,1024]{1,0:T(8,128)(2,1)}, f32[8,1,128]{2,1,0:T(1,128)}) custom-call(f32[8,1,128]{2,1,0:T(1,128)} %copy-done.12, f32[1024,768]{1,0:T(8,128)} %get-tuple-element.77.ssm_ref, f32[1024,3072]{1,0:T(8,128)} %get-tuple-element.75.lin_ref.q_ref.k_ref.v_ref.gate_ref.before_ref, f32[1,768]{1,0:T(1,128)} %reshape.155.gain_ref, ...), custom_call_target="tpu_custom_call" | custom-call | tf_op jit(solution)/shard_map/gate_norm/pallas_call | solution.py:1652
  162.4 0.8 maximum_maximum_fusion.refs_9_
  163.2 1.5 fusion.9
  164.7 121.8 %mix_sum.1 = (bf16[4,256,2048]{2,1,0:T(8,128)(2,1)}, f32[256,2048]{1,0:T(8,128)}, bf16[2048,2048]{1,0:T(8,128)(2,1)}, bf16[1024,2048]{1,0:T(8,128)(2,1)}) custom-call(bf16[4,256,1024]{2,1,0:T(8,128)(2,1)} %bitcast.35, bf16[1024,2048]{1,0:T(8,128)(2,1)} %all-gather.3.cloned.1.call-done.refs_1_.w_ref, bf16[256,2048]{1,0:T(8,128)(2,1)} %refs_2_.5, ...), custom_call_target="tpu_custom_call" | custom-call | tf_op jit(solution)/shard_map/mix_sum/pallas_call | solution.py:1461
  286.6 0.0 all-gather.5.cloned.1.call-done.cot_ref.refs_6_
  286.6 31.7 %feed_forward.1 = (bf16[1024,1024]{1,0:T(8,128)(2,1)}, bf16[1024,2048]{1,0:T(8,128)(2,1)}, bf16[1024,2048]{1,0:T(8,128)(2,1)}) custom-call(bf16[1024,2048]{1,0:T(8,128)(2,1)} %bitcast.28, bf16[1024,2048]{1,0:T(8,128)(2,1)} %all-gather.5.cloned.1.call-done.cot_ref.refs_6_, bf16[2048,2048]{1,0:T(8,128)(2,1)} %get-tuple-element.83.expand_ref.refs_1_, ...), custom_call_target="tpu_custom_call" | custom-call | tf_op jit(solution)/shard_map/feed_forward/pallas_call | solution.py:1768
  318.4 122.8 %second_sum.1 = (bf16[4,256,2048]{2,1,0:T(8,128)(2,1)}, f32[256,2048]{1,0:T(8,128)}, bf16[2048,2048]{1,0:T(8,128)(2,1)}, bf16[2048,1024]{1,0:T(8,128)(2,1)}, f32[256,3072]{1,0:T(8,128)}, /*index=5*/f32[256,128]{1,0:T(8,128)}) custom-call(bf16[4,256,2048]{2,1,0:T(8,128)(2,1)} %bitcast.33, bf16[2048,2048]{1,0:T(8,128)(2,1)} %get-tuple-element.83.expand_ref.refs_1_, ...), custom_call_target="tpu_custom_call" | custom-call | tf_op jit(solution)/shard_map/second_sum/pallas_call | solution.py:1461
  441.1 0.0 reduce-scatter.2.cloned.1.call-update
  441.2 0.0 copy-start.7
  441.2 16.8 %gate_back.1 = (bf16[1024,256]{1,0:T(8,128)(2,1)}, f32[1024,768]{1,0:T(8,128)}, f32[8,1,128]{2,1,0:T(1,128)}) custom-call(bf16[1024,2048]{1,0:T(8,128)(2,1)} %bitcast.31, bf16[1024,2048]{1,0:T(8,128)(2,1)} %all-gather.3.cloned.1.call-done.refs_1_.w_ref, f32[1024,768]{1,0:T(8,128)} %get-tuple-element.77.ssm_ref, ...), custom_call_target="tpu_custom_call" | custom-call | tf_op jit(solution)/shard_map/gate_back/pallas_call | solution.py:1714
  458.0 0.7 copy-done.11
  458.7 36.1 %mixer_backward.1 = (bf16[1024,3072]{1,0:T(8,128)(2,1)}, f32[256,128]{1,0:T(8,128)S(1)}) custom-call(f32[1024,3072]{1,0:T(8,128)} %get-tuple-element.75.lin_ref.q_ref.k_ref.v_ref.gate_ref.before_ref, f32[1024,3072]{1,0:T(8,128)} %get-tuple-element.75.lin_ref.q_ref.k_ref.v_ref.gate_ref.before_ref, s32[1024,1]{1,0:T(8,128)S(1)} %copy.44.seg_ref.segb_ref, ...), custom_call_target="tpu_custom_call" | custom-call | tf_op jit(solution)/shard_map/mixer_backward/pallas_call | solution.py:402
  494.8 0.6 convert_element_type.67.refs_7_
  495.5 12.5 %attend_backward.1 = bf16[1024,3072]{1,0:T(8,128)(2,1)} custom-call(s32[1]{0:T(128)} %bitcast.3.head_ref, f32[1024,3072]{1,0:T(8,128)} %get-tuple-element.75.lin_ref.q_ref.k_ref.v_ref.gate_ref.before_ref, f32[1024,3072]{1,0:T(8,128)} %get-tuple-element.75.lin_ref.q_ref.k_ref.v_ref.gate_ref.before_ref, ...), custom_call_target="tpu_custom_call", output_to_operand_aliasing={{}: (9, {})} | custom-call | tf_op jit(solution)/shard_map/attend_backward/pallas_call | solution.py:560
  508.0 6.3 convolution_convert_fusion.1.refs_6_
  514.3 18.6 %convolution_convert_fusion.refs_5_ = bf16[2048,3072]{1,0:T(8,128)(2,1)} fusion(bf16[1024,2048]{1,0:T(8,128)(2,1)} %get-tuple-element.101, bf16[1024,3072]{1,0:T(8,128)(2,1)S(1)} %copy-done.13), kind=kOutput, calls=%fused_computation | convolution fusion | flops 12891193344 | bytes 23068672 | tf_op jit(solution)/shard_map/dot_general | solution.py:42
  532.9 2.5 add_convert_fusion
  535.4 102.2 %first_sum.1 = (f32[256,2048]{1,0:T(8,128)}, f32[256,4224]{1,0:T(8,128)}, f32[64,1024]{1,0:T(8,128)}, f32[32,128]{1,0:T(8,128)}, f32[64,128]{1,0:T(8,128)}) custom-call(bf16[4,256,3072]{2,1,0:T(8,128)(2,1)} %bitcast.27, bf16[2048,3072]{1,0:T(8,128)(2,1)} %get-tuple-element.74.gains_ref.w_ref.refs_1_, bf16[256,2048]{1,0:T(8,128)(2,1)} %refs_2_.5, ...), custom_call_target="tpu_custom_call" | custom-call | tf_op jit(solution)/shard_map/first_sum/pallas_call | solution.py:1461
  637.6 1.9 copy-done
  639.5 0.9 copy-done.5
  640.4 0.8 copy-done.8
  641.2 0.7 copy-done.9
  641.9 5.8 unpack.1
  647.7 0.7 copy.54
  648.3 0.7 copy.52
  649.0 0.7 copy.53
  649.7 1.3 copy.58
  (44 shorter events, 0.2 us)
Async XLA Ops:
  7.2 157.5 %all-gather.3.cloned.1.call-start = ((), (), s32[]{:S(2)}) async-start(), calls=%async_computation.1 | async-start | bytes 4718592 | tf_op jit(solution)/shard_map/all_gather | solution.py:1823
  9.1 277.5 %all-gather.5.cloned.1.call-start = ((), (), s32[]{:S(2)}) async-start(), calls=%async_computation.2 | async-start | bytes 5242880 | tf_op jit(solution)/shard_map/all_gather | solution.py:1823
  11.5 89.4 %copy-start.21 = (bf16[12,64]{1,0:T(8,128)(2,1)S(1)}, bf16[12,64]{1,0:T(8,128)(2,1)}, u32[]{:S(2)}) copy-start(bf16[12,64]{1,0:T(8,128)(2,1)} %param.31) | copy-start | bytes 4612
  11.5 90.0 %copy-start.19 = (bf16[5,12,64]{2,1,0:T(8,128)(2,1)S(1)}, bf16[5,12,64]{2,1,0:T(8,128)(2,1)}, u32[]{:S(2)}) copy-start(bf16[5,12,64]{2,1,0:T(8,128)(2,1)} %param.28) | copy-start | bytes 23044
  11.5 90.1 %copy-start.23 = (bf16[256]{0:T(256)(128)(2,1)S(1)}, bf16[256]{0:T(256)(128)(2,1)}, u32[]{:S(2)}) copy-start(bf16[256]{0:T(256)(128)(2,1)} %param.33) | copy-start | bytes 1540
  11.6 90.3 %copy-start.24 = (bf16[256]{0:T(256)(128)(2,1)S(1)}, bf16[256]{0:T(256)(128)(2,1)}, u32[]{:S(2)}) copy-start(bf16[256]{0:T(256)(128)(2,1)} %param.21) | copy-start | bytes 1540
  11.6 90.4 %copy-start.6 = (s32[1024]{0:T(1024)S(1)}, s32[1024]{0:T(1024)}, u32[]{:S(2)}) copy-start(s32[1024]{0:T(1024)} %param.19) | copy-start | bytes 12292
  12.8 89.4 %copy-start.18 = (bf16[256,2,1024]{2,1,0:T(2,128)(2,1)S(1)}, bf16[256,2,1024]{2,1,0:T(2,128)(2,1)}, u32[]{:S(2)}) copy-start(bf16[256,2,1024]{2,1,0:T(2,128)(2,1)} %param.34) | copy-start | bytes 3145732
  12.9 91.0 %copy-start.22 = (f32[3,12]{1,0:T(4,128)S(1)}, f32[3,12]{1,0:T(4,128)}, u32[]{:S(2)}) copy-start(f32[3,12]{1,0:T(4,128)} %param.30) | copy-start | bytes 436
  100.8 432.0 %reduce-scatter.2.cloned.1.call-start = ((), (), s32[]{:S(2)}) async-start(), calls=%async_computation.3 | async-start | bytes 5242880 | tf_op jit(solution)/shard_map/reduce_scatter | solution.py:1827
  126.8 6.9 %copy-start.20 = (bf16[5,512]{1,0:T(8,128)(2,1)S(1)}, bf16[5,512]{1,0:T(8,128)(2,1)}, u32[]{:S(2)}) copy-start(bf16[5,512]{1,0:T(8,128)(2,1)} %param.29) | copy-start | bytes 15364
  133.6 14.3 %copy-start.3 = (bf16[1024,256]{1,0:T(8,128)(2,1)}, bf16[1024,256]{1,0:T(8,128)(2,1)S(1)}, u32[]{:S(2)}) copy-start(bf16[1024,256]{1,0:T(8,128)(2,1)S(1)} %attend_forward.1.attended_ref) | copy-start | bytes 1572868
  147.9 1.5 copy-start.1
  149.5 0.6 copy-start.12
  441.2 16.8 %copy-start.2 = (bf16[1024,1280]{1,0:T(8,128)(2,1)S(1)}, bf16[1024,1280]{1,0:T(8,128)(2,1)}, u32[]{:S(2)}) copy-start(bf16[1024,1280]{1,0:T(8,128)(2,1)} %copy-done.1) | copy-start | bytes 7864324
  441.2 16.8 %copy-start.7 = (f32[1,768]{1,0:T(1,128)S(1)}, f32[1,768]{1,0:T(1,128)}, u32[]{:S(2)}) copy-start(f32[1,768]{1,0:T(1,128)} %reshape.155.gain_ref) | copy-start | bytes 9220
  441.2 16.8 %copy-start.10 = (f32[8,1,128]{2,1,0:T(1,128)S(1)}, f32[8,1,128]{2,1,0:T(1,128)}, u32[]{:S(2)}) copy-start(f32[8,1,128]{2,1,0:T(1,128)} %get-tuple-element.92.inv_ref) | copy-start | bytes 12292
  458.0 0.7 copy-start.11
  458.7 36.8 %copy-start.4 = (bf16[1024,256]{1,0:T(8,128)(2,1)S(1)}, bf16[1024,256]{1,0:T(8,128)(2,1)}, u32[]{:S(2)}) copy-start(bf16[1024,256]{1,0:T(8,128)(2,1)} %get-tuple-element.90.do_ref) | copy-start | bytes 1572868
  495.5 12.5 %copy-start.15 = (bf16[4,256,2048]{2,1,0:T(8,128)(2,1)S(1)}, bf16[4,256,2048]{2,1,0:T(8,128)(2,1)}, u32[]{:S(2)}) copy-start(bf16[4,256,2048]{2,1,0:T(8,128)(2,1)} %get-tuple-element.88) | copy-start | bytes 12582916
  495.5 12.5 %copy-start.16 = (bf16[1024,1024]{1,0:T(8,128)(2,1)S(1)}, bf16[1024,1024]{1,0:T(8,128)(2,1)}, u32[]{:S(2)}) copy-start(bf16[1024,1024]{1,0:T(8,128)(2,1)} %get-tuple-element.78) | copy-start | bytes 6291460
  508.0 6.3 copy-start.13
  514.3 18.6 %copy-start.14 = (f32[256,2048]{1,0:T(8,128)S(1)}, f32[256,2048]{1,0:T(8,128)}, u32[]{:S(2)}) copy-start(f32[256,2048]{1,0:T(8,128)} %get-tuple-element.80.refs_3_) | copy-start | bytes 6291460
  637.6 1.9 copy-start
  639.5 0.9 copy-start.5
  640.4 0.8 copy-start.8
  641.2 0.7 copy-start.9
  641.9 7.8 %copy-start.17 = (f32[256,2048]{1,0:T(8,128)S(1)}, f32[256,2048]{1,0:T(8,128)}, u32[]{:S(2)}) copy-start(f32[256,2048]{1,0:T(8,128)} %get-tuple-element.184) | copy-start | bytes 6291460
Sparse Core Ops, SparseCore 0:
  10.5 57.3 all-gather.2
  101.0 85.1 all-gather.4
  441.3 76.5 reduce-scatter.1

commit v3 on v2

--- a/solution.py
+++ b/solution.py
@@ -190,8 +190,8 @@
 
 def mixer_backward_kernel(
     heads, lin_ref, before_ref, seg_ref, segb_ref, segr_ref, conv_ref, hp_ref, map_ref, gain_ref,
-    gn_ref, inv_ref, cross_ref, ssm_ref, mixed_ref, states_ref,
-    dlin_ref, small_ref, dstate, dnext, seg_next, dconv_ref, dhp_ref, dgain_ref,
+    gn_ref, inv_ref, cross_ref, ssm_ref, mixed_ref, states_ref, mix_grad_ref, mix_in_ref,
+    dlin_ref, small_ref, product_ref, dstate, dnext, seg_next, dconv_ref, dhp_ref, dgain_ref,
 ):
     channels = heads * PM
     rows = lin_ref.shape[0]
@@ -210,6 +210,8 @@
         dstate[...] = jnp.zeros_like(dstate)
         dnext[...] = jnp.zeros_like(dnext)
         seg_next[...] = jnp.full_like(seg_next, -1)
+
+    product_ref[...] = mat_tn(mix_grad_ref[...], mix_in_ref[...]).astype(BF16)
 
     heads_map = map_ref[...]
     seg = seg_ref[...]
@@ -387,7 +389,8 @@
 
 
 def mixer_backward(
-    lin, seg, conv_weight, heads_vec, heads_map, gain, grad_normed, inverse, cross, ssm, mixed, states, heads, lead, share
+    lin, seg, conv_weight, heads_vec, heads_map, gain, grad_normed, inverse, cross, ssm, mixed, states, heads, lead, share,
+    grad_mix, mix_in,
 ):
     total = lin.shape[0]
     channels = heads * PM
@@ -418,14 +421,18 @@
             by_rows(channels),
             by_rows(mixed_width),
             pl.BlockSpec((1, NS, channels), lambda c: (steps - 1 - c, 0, 0)),
+            pl.BlockSpec((total, grad_mix.shape[1] // steps), lambda c: (0, c)),
+            whole_block(mix_in),
         ],
         out_specs=[
             by_rows(lead),
             pl.BlockSpec((share, LANES), lambda c: (0, 0)),
+            pl.BlockSpec((grad_mix.shape[1] // steps, mix_in.shape[1]), lambda c: (c, 0)),
         ],
         out_shape=[
             jax.ShapeDtypeStruct((total, lin.shape[1]), BF16),
             jax.ShapeDtypeStruct((share, LANES), F32),
+            jax.ShapeDtypeStruct((grad_mix.shape[1], mix_in.shape[1]), BF16),
         ],
         scratch_shapes=[
             pltpu.VMEM((NS, channels), F32),
@@ -439,7 +446,7 @@
         name="mixer_backward",
     )(
         lin, lin, seg_column, seg_column, seg.reshape(1, total), conv_weight, heads_vec, heads_map, gain,
-        grad_normed, inverse, cross, ssm, mixed, states,
+        grad_normed, inverse, cross, ssm, mixed, states, grad_mix, mix_in,
     )
 
 
@@ -502,12 +509,14 @@
         inner = jnp.sum(grads * weights, 1, keepdims=True)
         scores = (weights * (grads - inner)).astype(BF16)
         dq = mat(scores, keys[:stop]) * scale
-        dq_ref[rows, :] = turn(dq, cosine[rows], -sine[rows]).astype(BF16)
+        dq_ref[step, rows, :] = turn(dq, cosine[rows], -sine[rows]).astype(BF16)
         dkeys[:stop] += mat_tn(scores, query[rows]) * scale
-    place = pl.ds(pl.multiple_of((first_block + step) * HEAD_SIZE, HEAD_SIZE), HEAD_SIZE)
-    out = pltpu.make_async_copy(dq_ref, dlin_ref.at[here, place], sem)
-    out.start()
-    out.wait()
+
+    def out_copy(head):
+        place = pl.ds(pl.multiple_of((first_block + head) * HEAD_SIZE, HEAD_SIZE), HEAD_SIZE)
+        return pltpu.make_async_copy(dq_ref.at[head], dlin_ref.at[here, place], sem.at[head])
+
+    out_copy(step).start()
 
     @pl.when(step == pl.num_programs(1) - 1)
     def _():
@@ -520,8 +529,10 @@
             dkv_ref[:, cols] = jnp.where(same, grad_keys, 0.0).astype(BF16)
             cols = slice((KEY_HEADS + head) * HEAD_SIZE, (KEY_HEADS + head + 1) * HEAD_SIZE)
             dkv_ref[:, cols] = jnp.where(same, grad_values, 0.0).astype(BF16)
-        both = pltpu.make_async_copy(dkv_ref, dlin_ref.at[here, pl.ds(lead, dkv_ref.shape[1])], sem)
+        both = pltpu.make_async_copy(dkv_ref, dlin_ref.at[here, pl.ds(lead, dkv_ref.shape[1])], sem.at[dq_ref.shape[0]])
         both.start()
+        for head in range(dq_ref.shape[0]):
+            out_copy(head).wait()
         both.wait()
 
 
@@ -571,9 +582,9 @@
             scratch_shapes=[
                 pltpu.VMEM((SEQ_LEN, HEAD_SIZE), F32),
                 pltpu.VMEM((SEQ_LEN, HEAD_SIZE), F32),
-                pltpu.VMEM((SEQ_LEN, HEAD_SIZE), BF16),
+                pltpu.VMEM((heads, SEQ_LEN, HEAD_SIZE), BF16),
                 pltpu.VMEM((SEQ_LEN, 2 * KEY_HEADS * HEAD_SIZE), BF16),
-                pltpu.SemaphoreType.DMA,
+                pltpu.SemaphoreType.DMA((heads + 1,)),
             ],
         ),
         out_shape=jax.ShapeDtypeStruct(grad_lin.shape, BF16),
@@ -1063,7 +1074,14 @@
 
 PRODUCT_TURNS = (
     (0, 2, 0, 0), (0, 2, 1, 1), (1, 2, 2, 0), (0, 2, 3, 2), (1, 3, 0, 1), (2, 3, 0, 0), (0, 3, 1, 3), (1, 3, 2, 2),
-    (2, 3, 2, 1), (1, 4, 0, 3), (2, 4, 0, 2), (2, 4, 3, 3),
+    (2, 3, 2, 1), (1, 4, 0, 3), (2, 4, 0, 2), (2, 4, 3, 3), (3, 2, 0, 0), (3, 2, 1, 1), (3, 2, 2, 2), (3, 2, 3, 3),
+    (3, 3, 0, 4), (3, 3, 1, 5), (3, 3, 2, 6), (3, 3, 3, 7),
+)
+
+
+GATHER_TURNS = (
+    (0, 0, 1, 0), (0, 0, 3, 1), (0, 1, 1, 2), (0, 1, 3, 3), (1, 2, 1, 0), (1, 2, 2, 1), (2, 2, 3, 0),
+    (3, 3, 0, 0), (3, 3, 1, 1), (3, 3, 2, 2), (3, 3, 3, 3), (3, 4, 1, 4), (3, 4, 2, 5),
 )
 
 
@@ -1135,7 +1153,7 @@
     x_ref, w_ref = take(2)
     own_refs = take(own_count)
     if products:
-        left_refs, (right_ref,) = take(2), take(1)
+        left_refs, (right_ref, extra_ref) = take(2), take(2)
     else:
         piece_refs = take(piece_count)
     gather_refs = take(len(gather_rows))
@@ -1145,10 +1163,13 @@
     side_refs = take(side_count)
     if products:
         piece_refs = take(piece_count)
+        (extra_out,) = take(1)
     if piece_count:
         (piece_out,) = take(1)
         common_refs = take(3 if ranges else 1)
     full_refs = take(len(gather_rows))
+    if gather_rows:
+        (next_ref,) = take(1)
     x_held, w_held, load_sem, held, part, sum_send, sum_recv, out_send, out_recv = take(9)
     place = lax.axis_index("tensor")
     away = group - 1 - place
@@ -1178,12 +1199,56 @@
         if products:
             load_left, product, product_end = product_steps(left_refs, x_held, right_ref, piece_refs, *take(4))
             load_left(0)
+            extra_held, extra_made, extra_sem = take(3)
+            extra_load = pltpu.make_async_copy(extra_ref, extra_held, extra_sem.at[2])
+            extra_load.start()
+
+            def extra_copy(index):
+                slot = lax.rem(index, 2)
+                return pltpu.make_async_copy(
+                    extra_made.at[slot], extra_out.at[pl.ds(index * CHUNK, CHUNK)], extra_sem.at[slot]
+                )
+
+            def extra_product(index):
+                if index == 0:
+                    extra_load.wait()
+                if index >= 2:
+                    extra_copy(index - 2).wait()
+                left = right_ref[index * CHUNK : (index + 1) * CHUNK, :]
+                for col in range(0, model, tile):
+                    extra_made[index % 2, :, col : col + tile] = mat(left, extra_held[:, col : col + tile]).astype(BF16)
+                extra_copy(index).start()
+
         else:
             begin()
     if gather_rows:
         pieces = list(zip(gather_refs, full_refs, gather_rows))
         begin, neighbours, corner, end = plane_gather_steps(pieces, *take(3))
         begin()
+        next_w, next_held, next_sem = take(3)
+
+        def load_next():
+            return pltpu.make_async_copy(full_refs[0], next_w, next_sem.at[2])
+
+        def next_copy(chunk):
+            slot = lax.rem(chunk, 2)
+            return pltpu.make_async_copy(
+                next_held.at[slot], next_ref.at[:, pl.ds(chunk * rows, rows)], next_sem.at[slot]
+            )
+
+        def multiply_next(chunk, half):
+            width = next_w.shape[1] // 2
+
+            @pl.when((chunk >= 2) & (half == 0))
+            def _():
+                next_copy(chunk - 2).wait()
+
+            left = out_ref[:, pl.ds(chunk * rows, rows), :].reshape(group * rows, model)
+            for first in range(half * width, (half + 1) * width, tile):
+                product = mat(left, next_w[:, first : first + tile])
+                next_held[lax.rem(chunk, 2), :, :, first : first + tile] = product.reshape(group, rows, tile)
+            if half == 1:
+                next_copy(chunk).start()
 
     def multiply(chunk, index):
         left = x_held[:, pl.ds(chunk * rows, rows), :].reshape(group * rows, x_ref.shape[2])
@@ -1303,7 +1368,7 @@
 
                         @pl.when(chunk == turn_chunk)
                         def _():
-                            (add_core, add_near, add_last)[step](index)
+                            (add_core, add_near, add_last, extra_product)[step](index)
 
             if piece_count and not products and slot == 0:
 
@@ -1323,17 +1388,23 @@
                 def _():
                     add_last(chunk - 1)
 
-            if gather_rows and slot == 1:
-
-                @pl.when(chunk < PLANE_PARTS)
-                def _():
-                    neighbours(chunk)
-
-            if gather_rows and slot == group // 2:
-
-                @pl.when((chunk >= PLANE_PARTS // 2) & (chunk < PLANE_PARTS))
-                def _():
-                    corner(chunk - PLANE_PARTS // 2)
+            if gather_rows:
+                for step, turn_chunk, turn_slot, index in GATHER_TURNS:
+                    if turn_slot == slot:
+
+                        @pl.when(chunk == turn_chunk)
+                        def _():
+                            if step == 0:
+                                neighbours(index)
+                            elif step == 1:
+                                corner(index)
+                            elif step == 2:
+                                end()
+                                load_next().start()
+                            else:
+                                if index == 0:
+                                    load_next().wait()
+                                multiply_next(index // 2, index % 2)
 
         return carry
 
@@ -1368,9 +1439,16 @@
             end(chunk)
         return carry
 
+    if gather_rows:
+        multiply_next(chunks - 1, 0)
+        multiply_next(chunks - 1, 1)
     lax.fori_loop(0, chunks, finish_sends, 0)
+    if products:
+        extra_copy(6).wait()
+        extra_copy(7).wait()
     if gather_rows:
-        end()
+        next_copy(chunks - 2).wait()
+        next_copy(chunks - 1).wait()
 
 
 def line_sum(
@@ -1397,33 +1475,35 @@
     if products and (dp_size != 8 or group != 4):
         lefts, right = products[:2], products[2]
         pieces = [mat_tn(lefts[0], x).astype(BF16), mat_tn(lefts[1], right).astype(BF16)]
+        late = [mat(right, products[3]).astype(BF16)]
         products = ()
     if dp_size != 8:
         if pieces:
             share = pieces[0].shape[0] // dp_size
             parts = [scatter(piece, "dp", 0) if piece.shape[0] > share else lax.psum(piece, "dp") for piece in pieces]
-            late = [jnp.concatenate(parts, 1).astype(F32)]
+            total_sum = jnp.concatenate(parts, 1).astype(F32)
+            late += [total_sum]
             weight, lanes, gain_index = gains
-            lanes = gain_lanes(lanes, weight, late[0][:, : weight.shape[1]], gain_index)
+            lanes = gain_lanes(lanes, weight, total_sum[:, : weight.shape[1]], gain_index)
             if ranges:
-                columns = [late[0][:, start : start + count] for start, count in ranges]
+                columns = [total_sum[:, start : start + count] for start, count in ranges]
                 late += [
                     scatter(jnp.concatenate(columns, 1).astype(BF16), "tensor", 0).astype(F32),
-                    lax.psum(late[0][state_rows[0] : state_rows[1], late[0].shape[1] - LANES :], "tensor"),
+                    lax.psum(total_sum[state_rows[0] : state_rows[1], total_sum.shape[1] - LANES :], "tensor"),
                     scatter(lanes, "tensor", 0),
                 ]
             else:
                 late += [lanes]
         late += [plane_gather_plain(array, kind) for array, kind in gathers]
-        pieces, ranges, gathers = (), (), ()
+        multiplied, pieces, ranges, gathers = bool(gathers), (), (), ()
     outs = [vmem] * len(out_shape)
     last, gain_index = [], 0
     piece_inputs, piece_specs = list(pieces), [anywhere] * len(pieces)
     if products:
         pieces = [jax.ShapeDtypeStruct((model, x.shape[1]), BF16), jax.ShapeDtypeStruct((model, products[2].shape[1]), BF16)]
-        piece_inputs, piece_specs = list(products), [anywhere, anywhere, vmem]
-        out_shape += pieces
-        outs += [anywhere] * 2
+        piece_inputs, piece_specs = list(products), [anywhere, anywhere, vmem, anywhere]
+        out_shape += pieces + [jax.ShapeDtypeStruct((total, model), BF16)]
+        outs += [anywhere] * 3
     if pieces:
         share, width = pieces[0].shape[0] // dp_size, sum(piece.shape[1] for piece in pieces)
         last, gain_index = list(gains[:2]), gains[2]
@@ -1435,6 +1515,9 @@
                 pltpu.VMEM((2, share, width), BF16),
                 pltpu.SemaphoreType.DMA((2, 2)),
                 pltpu.SemaphoreType.DMA((2, 2)),
+                pltpu.VMEM(products[3].shape, BF16),
+                pltpu.VMEM((2, CHUNK, model), BF16),
+                pltpu.SemaphoreType.DMA((3,)),
             ]
         if ranges:
             common_width = sum(count for _, count in ranges)
@@ -1457,7 +1540,14 @@
             shape = (dp_size * array.shape[0], array.shape[1]) if kind else (array.shape[0], dp_size * array.shape[1])
             out_shape += [jax.ShapeDtypeStruct(shape, BF16)]
             outs += [anywhere]
-        scratch += plane_gather_scratch(len(gathers))
+        next_width = gathers[0][0].shape[1]
+        out_shape += [jax.ShapeDtypeStruct((group, rows, next_width), F32)]
+        outs += [anywhere]
+        scratch += plane_gather_scratch(len(gathers)) + [
+            pltpu.VMEM((model, next_width), BF16),
+            pltpu.VMEM((2, group, piece_rows, next_width), F32),
+            pltpu.SemaphoreType.DMA((3,)),
+        ]
     results = pl.pallas_call(
         functools.partial(
             line_sum_kernel, group, spread, by_rows, finish, len(own), len(side_shapes), len(pieces), bool(products),
@@ -1475,6 +1565,10 @@
     results = list(results)
     if spread:
         results[0] = results[0].reshape(total, model)
+    if gathers:
+        results[-1] = results[-1].reshape(total, next_width)
+    elif dp_size != 8 and multiplied:
+        late += [mat(results[0], late[0])]
     if products:
         del results[1 + len(side_shapes) : 3 + len(side_shapes)]
     return results + late
@@ -1732,14 +1826,11 @@
 HIDDEN_TILE = 256
 
 
-def feed_forward_kernel(second_ref, cot_ref, expand_ref, shrink_ref, act_ref, hidden_ref, out_ref, total):
-    step = pl.program_id(0)
-    expand = expand_ref[...]
+def feed_forward_kernel(cot_ref, lin_ref, shrink_ref, act_ref, hidden_ref):
     shrink = shrink_ref[...]
-    for first in range(0, second_ref.shape[0], ROWS):
+    for first in range(0, cot_ref.shape[0], ROWS):
         rows = slice(first, first + ROWS)
-        lin = mat(second_ref[rows, :], expand)
-        gate, up = lin[:, :HIDDEN_TILE], lin[:, HIDDEN_TILE:]
+        gate, up = lin_ref[rows, :HIDDEN_TILE], lin_ref[rows, HIDDEN_TILE:]
         sig = sigmoid(gate)
         silu = gate * sig
         act = (silu * up).astype(BF16)
@@ -1747,47 +1838,30 @@
         grad = mat_nt(cot_ref[rows, :], shrink)
         hidden_ref[rows, :HIDDEN_TILE] = (grad * up * (sig * (1.0 + gate * (1.0 - sig)))).astype(BF16)
         hidden_ref[rows, HIDDEN_TILE:] = (grad * silu).astype(BF16)
-        part = mat(act, shrink)
-
-        @pl.when(step == 0)
-        def _():
-            total[rows, :] = part
-
-        @pl.when(step > 0)
-        def _():
-            total[rows, :] += part
-
-    @pl.when(step == pl.num_programs(0) - 1)
-    def _():
-        out_ref[...] = total[...].astype(BF16)
-
-
-def feed_forward(second, cot, expand, shrink):
-    total, model = second.shape
+
+
+def feed_forward(cot, hidden_lin, shrink):
+    total, model = cot.shape
     hidden = shrink.shape[0]
     return pl.pallas_call(
         feed_forward_kernel,
         grid=(hidden // HIDDEN_TILE,),
         in_specs=[
             pl.BlockSpec(memory_space=pltpu.VMEM),
-            pl.BlockSpec(memory_space=pltpu.VMEM),
-            pl.BlockSpec((model, 2 * HIDDEN_TILE), lambda c: (0, c)),
+            pl.BlockSpec((total, 2 * HIDDEN_TILE), lambda c: (0, c)),
             pl.BlockSpec((HIDDEN_TILE, model), lambda c: (c, 0)),
         ],
         out_specs=[
             pl.BlockSpec((total, HIDDEN_TILE), lambda c: (0, c)),
             pl.BlockSpec((total, 2 * HIDDEN_TILE), lambda c: (0, c)),
-            pl.BlockSpec((total, model), lambda c: (0, 0)),
         ],
         out_shape=[
             jax.ShapeDtypeStruct((total, hidden), BF16),
             jax.ShapeDtypeStruct((total, 2 * hidden), BF16),
-            jax.ShapeDtypeStruct((total, model), BF16),
         ],
-        scratch_shapes=[pltpu.VMEM((total, model), F32)],
         compiler_params=pltpu.CompilerParams(vmem_limit_bytes=60 << 20),
         name="feed_forward",
-    )(second, cot, expand, shrink)
+    )(cot, hidden_lin, shrink)
 
 
 def mix_finish(total, mine, own_refs, side_refs):
@@ -1883,12 +1957,12 @@
     attended = attend_forward(lin, query_block, lead, query_heads, key_head, segment_ids, cosine, sine)
     expand_own = jnp.moveaxis(expand_weight.reshape(share, 2, -1, HIDDEN_TILE), 1, 2).reshape(share, 2 * hidden)
     mix_in, inverse = gate_norm(square, ssm, lin, gate_row, attended, group, 4)
-    second_all, middle, weight_expand, weight_shrink = line_sum(
+    second_all, middle, weight_expand, weight_shrink, hidden_lin = line_sum(
         mix_in, weight_mix, [tokens_in, gain_two], False, mix_finish,
         [jax.ShapeDtypeStruct((own_rows, model), F32)], group, model, 2, "mix_sum", dp_size,
         gathers=[(expand_own, True), (shrink_weight, False)],
     )
-    act, grad_hidden, ffn_part = feed_forward(second_all, cot_all, weight_expand, weight_shrink)
+    act, grad_hidden = feed_forward(cot_all, hidden_lin, weight_shrink)
     lanes = jnp.concatenate(
         [
             (1.0 / norm_first.astype(F32))[:, None],
@@ -1897,19 +1971,18 @@
         ],
         1,
     )
-    mix_all, grad_middle, ffn_sum, lanes = line_sum(
+    mix_all, grad_middle, ffn_part, ffn_sum, lanes = line_sum(
         grad_hidden, weight_expand, [cotangent, middle, gain_two], True, second_finish,
         [jax.ShapeDtypeStruct((own_rows, model), F32)], group, model, 3, "second_sum", dp_size,
-        products=(second_all, cot_all, act), gains=(expand_own, lanes, 1),
+        products=(second_all, cot_all, act, weight_shrink), gains=(expand_own, lanes, 1),
     )
     ffn_part, mix_all = lax.optimization_barrier((ffn_part, mix_all))
     ffn_out = scatter(ffn_part, "tensor", 0)
 
     grad_attended, grad_normed, cross = gate_back(mix_all, weight_mix, ssm, lin, gate_row, query_cols, group, 5)
-    grad_mix_weight = mat_tn(mix_all, mix_in).astype(BF16)
-    grad_lin, small = mixer_backward(
+    grad_lin, small, grad_mix_weight = mixer_backward(
         lin, segment_ids, conv_weight, heads_vec, heads_map, gate_row, grad_normed, inverse, cross,
-        ssm, mixed, states, heads, lead, share,
+        ssm, mixed, states, heads, lead, share, mix_all, mix_in,
     )
     grad_lin = attend_backward(
         lin, query_block, lead, query_heads, key_head, segment_ids, cosine, sine, grad_attended, grad_lin

time: 666 us -> 655 us (0.983)
    pallas_call x1, Pallas kernels: 31.7 us -> 12.4 us  [feed_forward(): pl.pallas_call(feed_forward_kernel, grid=(hidden // HIDDEN_TILE,), in_spe...]
    pallas_call x3, Pallas kernels: 347 us -> 362 us  [line_sum(): pl.pallas_call(functools.partial(line_sum_kernel, group, spread, by_rows,...]
    dot_general x2 -> x1, matrix products: 24.8 us -> 18.9 us  [mat_tn(): lax.dot_general(left_side, right_side, (((0,), (0,)), ((), ())), preferre...]
  transfers between devices with their start and end apart: 3 -> 3, of which waited for: 0 -> 0; matrix products, arithmetic and copies ran while one was open for 6% -> 5% of each run, Pallas kernels for 49% -> 51%
where the time goes in v3:
time: 655 us; the launch traced here: 651 us
  Pallas kernels  588 us (90%)
  local copies, waits for them, and re-layouts  22.1 us (3%)
  matrix products  18.9 us (3%)
  between operations  14.4 us (2%)
  other arithmetic  8.04 us (1%)
    pallas_call x3, Pallas kernels, line_sum(): pl.pallas_call(functools.partial(line_sum_kernel, group, spread, by_rows,...  362 us
    pallas_call x1, Pallas kernels, entry_gather(): pl.pallas_call(functools.partial(entry_gather_kernel, group, parts), in_s...  84.3 us
    pallas_call x1, Pallas kernels, mixer_backward(): pl.pallas_call(functools.partial(mixer_backward_kernel, heads), grid=(ste...  40.8 us
    pallas_call x1, Pallas kernels, project(): pl.pallas_call(project_kernel, grid=(cols // tile,), in_specs=[whole_bloc...  20.6 us
    dot_general x1, matrix products, mat_tn(): lax.dot_general(left_side, right_side, (((0,), (0,)), ((), ())), preferre...  18.9 us
    pallas_call x1, Pallas kernels, gate_back(): pl.pallas_call(functools.partial(gate_back_kernel, group, query_cols), gr...  16.7 us
    pallas_call x1, Pallas kernels, mixer_forward(): pl.pallas_call(functools.partial(mixer_forward_kernel, heads), grid=(step...  14.1 us
  transfers between devices with their start and end apart: 3, of which 0 were waited for; matrix products, arithmetic and copies ran while one was open for 5% of the time, Pallas kernels for 51%

profile of v3, /device:TPU:0, one launch (start us, length us, event | category | flops | bytes accessed | tf_op | source)
XLA Modules:
  0.0 651.3 jit_solution(14386995977023542133)
XLA Ops:
  7.2 0.0 all-gather.3.cloned.1.call-start
  7.2 1.9 pad_maximum_fusion.2
  9.1 0.0 all-gather.3.cloned.1.call-update
  9.1 0.0 all-gather.5.cloned.1.call-start
  9.2 0.8 copy.41
  10.0 0.7 broadcast_in_dim.32
  10.8 0.8 broadcast_in_dim.33
  11.5 0.0 copy-start.19
  11.5 0.0 copy-start.17
  11.5 0.0 copy-start.21
  11.6 0.0 copy-start.22
  11.6 0.0 copy-start.7
  11.6 1.2 copy.55
  12.8 0.0 copy-start.16
  12.9 0.0 copy-start.20
  12.9 3.6 concatenate.18.weight_ref.refs_8_
  16.5 84.3 %entry_gather.1 = (bf16[4,256,2048]{2,1,0:T(8,128)(2,1)}, bf16[2048,3072]{1,0:T(8,128)(2,1)}) custom-call(bf16[256,2048]{1,0:T(8,128)(2,1)} %refs_2_.5, bf16[256,3072]{1,0:T(8,128)(2,1)} %concatenate.18.weight_ref.refs_8_), custom_call_target="tpu_custom_call" | custom-call | tf_op jit(solution)/shard_map/entry_gather/pallas_call | solution.py:890
  100.8 0.0 all-gather.5.cloned.1.call-update
  100.8 0.0 reduce-scatter.2.cloned.1.call-start
  100.9 0.7 reshape.159.gain_ref
  101.6 0.1 reshape.144
  101.7 0.1 copy.48
  101.8 0.0 copy-done.22
  101.8 0.1 copy.47
  102.0 0.2 copy.44.seg_ref.segb_ref
  102.2 1.6 reshape.150.refs_4_.refs_9_
  103.8 0.1 pad.15.clone
  103.9 20.6 %project.1 = (f32[1024,3072]{1,0:T(8,128)}, bf16[1024,2048]{1,0:T(8,128)(2,1)}, f32[8,2048]{1,0:T(8,128)}) custom-call(bf16[1024,2048]{1,0:T(8,128)(2,1)} %bitcast.31, bf16[2048,3072]{1,0:T(8,128)(2,1)} %get-tuple-element.76.gains_ref.w_ref.refs_1_, bf16[2048,3072]{1,0:T(8,128)(2,1)} %get-tuple-element.76.gains_ref.w_ref.refs_1_), custom_call_target="tpu_custom_call" | custom-call | tf_op jit(solution)/shard_map/project/pallas_call | solution.py:1674
  124.5 1.9 fusion.1
  126.4 0.3 pad_maximum_fusion
  126.8 0.0 copy-start.18
  126.8 6.8 %attend_forward.1.attended_ref = bf16[1024,256]{1,0:T(8,128)(2,1)S(1)} custom-call(s32[1]{0:T(128)} %bitcast.3.head_ref, f32[1024,3072]{1,0:T(8,128)} %get-tuple-element.77.lin_ref.q_ref.k_ref.v_ref.gate_ref.before_ref, f32[1024,3072]{1,0:T(8,128)} %get-tuple-element.77.lin_ref.q_ref.k_ref.v_ref.gate_ref.before_ref, ...), custom_call_target="tpu_custom_call" | custom-call | tf_op jit(solution)/shard_map/attend_forward/pallas_call | solution.py:555
  133.6 0.0 copy-start.4
  133.7 14.1 %mixer_forward.1 = (f32[1024,768]{1,0:T(8,128)}, bf16[1024,1280]{1,0:T(8,128)(2,1)S(1)}, f32[8,1,128]{2,1,0:T(1,128)S(1)}, bf16[8,256,768]{2,1,0:T(8,128)(2,1)}) custom-call(f32[1024,3072]{1,0:T(8,128)} %get-tuple-element.77.lin_ref.q_ref.k_ref.v_ref.gate_ref.before_ref, s32[1024,1]{1,0:T(8,128)S(1)} %copy.44.seg_ref.segb_ref, s32[1,1024]{1,0:T(1,128)S(1)} %bitcast.24, ...), custom_call_target="tpu_custom_call" | custom-call | tf_op jit(solution)/shard_map/mixer_forward/pallas_call | solution.py:358
  147.8 1.5 copy-done.2
  149.3 0.6 copy-done.13
  149.9 12.6 %gate_norm.1 = (bf16[1024,1024]{1,0:T(8,128)(2,1)}, f32[8,1,128]{2,1,0:T(1,128)}) custom-call(f32[8,1,128]{2,1,0:T(1,128)} %copy-done.13, f32[1024,768]{1,0:T(8,128)} %get-tuple-element.79.ssm_ref, f32[1024,3072]{1,0:T(8,128)} %get-tuple-element.77.lin_ref.q_ref.k_ref.v_ref.gate_ref.before_ref, f32[1,768]{1,0:T(1,128)} %reshape.159.gain_ref, ...), custom_call_target="tpu_custom_call" | custom-call | tf_op jit(solution)/shard_map/gate_norm/pallas_call | solution.py:1746
  162.5 0.8 maximum_maximum_fusion.refs_10_
  163.2 1.5 fusion.9
  164.8 126.7 %mix_sum.1 = (bf16[4,256,2048]{2,1,0:T(8,128)(2,1)}, f32[256,2048]{1,0:T(8,128)}, bf16[2048,2048]{1,0:T(8,128)(2,1)}, bf16[1024,2048]{1,0:T(8,128)(2,1)}, f32[4,256,2048]{2,1,0:T(8,128)}) custom-call(bf16[4,256,1024]{2,1,0:T(8,128)(2,1)} %bitcast.21, bf16[1024,2048]{1,0:T(8,128)(2,1)} %all-gather.3.cloned.1.call-done.refs_1_.w_ref, ...), custom_call_target="tpu_custom_call" | custom-call | tf_op jit(solution)/shard_map/mix_sum/pallas_call | solution.py:1551
  291.5 0.0 all-gather.5.cloned.1.call-done.cot_ref.refs_6_
  291.6 12.4 %feed_forward.1 = (bf16[1024,1024]{1,0:T(8,128)(2,1)}, bf16[1024,2048]{1,0:T(8,128)(2,1)}) custom-call(bf16[1024,2048]{1,0:T(8,128)(2,1)} %all-gather.5.cloned.1.call-done.cot_ref.refs_6_, f32[1024,2048]{1,0:T(8,128)} %bitcast.30, bf16[1024,2048]{1,0:T(8,128)(2,1)} %get-tuple-element.85.shrink_ref.refs_8_), custom_call_target="tpu_custom_call" | custom-call | tf_op jit(solution)/shard_map/feed_forward/pallas_call | solution.py:1846
  304.0 133.3 %second_sum.1 = (bf16[4,256,2048]{2,1,0:T(8,128)(2,1)}, f32[256,2048]{1,0:T(8,128)}, bf16[2048,2048]{1,0:T(8,128)(2,1)}, bf16[2048,1024]{1,0:T(8,128)(2,1)}, bf1...) custom-call(bf16[4,256,2048]{2,1,0:T(8,128)(2,1)} %bitcast.33, ...), custom_call_target="tpu_custom_call" | custom-call | tf_op jit(solution)/shard_map/second_sum/pallas_call | solution.py:1551
  437.3 0.0 reduce-scatter.2.cloned.1.call-update
  437.3 0.0 copy-start
  437.3 0.0 copy-start.3
  437.3 0.0 copy-start.8
  437.4 16.7 %gate_back.1 = (bf16[1024,256]{1,0:T(8,128)(2,1)}, f32[1024,768]{1,0:T(8,128)}, f32[8,1,128]{2,1,0:T(1,128)}) custom-call(bf16[1024,2048]{1,0:T(8,128)(2,1)} %bitcast.28, bf16[1024,2048]{1,0:T(8,128)(2,1)} %all-gather.3.cloned.1.call-done.refs_1_.w_ref, f32[1024,768]{1,0:T(8,128)} %get-tuple-element.79.ssm_ref, ...), custom_call_target="tpu_custom_call" | custom-call | tf_op jit(solution)/shard_map/gate_back/pallas_call | solution.py:1808
  454.2 0.7 copy-done.12
  454.8 40.8 %mixer_backward.1 = (bf16[1024,3072]{1,0:T(8,128)(2,1)}, f32[256,128]{1,0:T(8,128)S(1)}, bf16[2048,1024]{1,0:T(8,128)(2,1)}) custom-call(f32[1024,3072]{1,0:T(8,128)} %get-tuple-element.77.lin_ref.q_ref.k_ref.v_ref.gate_ref.before_ref, f32[1024,3072]{1,0:T(8,128)} %get-tuple-element.77.lin_ref.q_ref.k_ref.v_ref.gate_ref.before_ref, ...), custom_call_target="tpu_custom_call" | custom-call | tf_op jit(solution)/shard_map/mixer_backward/pallas_call | solution.py:405
  495.6 0.6 convert_element_type.63.refs_7_
  496.3 11.3 %attend_backward.1 = bf16[1024,3072]{1,0:T(8,128)(2,1)} custom-call(s32[1]{0:T(128)} %bitcast.3.head_ref, f32[1024,3072]{1,0:T(8,128)} %get-tuple-element.77.lin_ref.q_ref.k_ref.v_ref.gate_ref.before_ref, f32[1024,3072]{1,0:T(8,128)} %get-tuple-element.77.lin_ref.q_ref.k_ref.v_ref.gate_ref.before_ref, ...), custom_call_target="tpu_custom_call", output_to_operand_aliasing={{}: (9, {})} | custom-call | tf_op jit(solution)/shard_map/attend_backward/pallas_call | solution.py:571
  507.5 18.9 %convolution_convert_fusion.refs_5_ = bf16[2048,3072]{1,0:T(8,128)(2,1)} fusion(bf16[1024,2048]{1,0:T(8,128)(2,1)S(1)} %copy-done.23, bf16[1024,3072]{1,0:T(8,128)(2,1)} %attend_backward.1), kind=kOutput, calls=%fused_computation | convolution fusion | flops 12891193344 | bytes 23068672 | tf_op jit(solution)/shard_map/dot_general | solution.py:42
  526.4 2.5 add_convert_fusion
  528.9 102.1 %first_sum.1 = (f32[256,2048]{1,0:T(8,128)}, f32[256,4224]{1,0:T(8,128)}, f32[64,1024]{1,0:T(8,128)}, f32[32,128]{1,0:T(8,128)}, f32[64,128]{1,0:T(8,128)}) custom-call(bf16[4,256,3072]{2,1,0:T(8,128)(2,1)} %bitcast.27, bf16[2048,3072]{1,0:T(8,128)(2,1)} %get-tuple-element.76.gains_ref.w_ref.refs_1_, bf16[256,2048]{1,0:T(8,128)(2,1)} %refs_2_.5, ...), custom_call_target="tpu_custom_call" | custom-call | tf_op jit(solution)/shard_map/first_sum/pallas_call | solution.py:1551
  631.0 1.9 copy-done.1
  632.9 0.9 copy-done.6
  633.9 0.8 copy-done.9
  634.6 0.7 copy-done.10
  635.3 5.8 unpack.1
  641.1 0.7 copy.54
  641.8 0.7 copy.52
  642.5 0.7 copy.53
  643.2 1.3 copy.58
  (41 shorter events, 0.2 us)
Async XLA Ops:
  7.2 157.6 %all-gather.3.cloned.1.call-start = ((), (), s32[]{:S(2)}) async-start(), calls=%async_computation.1 | async-start | bytes 4718592 | tf_op jit(solution)/shard_map/all_gather | solution.py:1897
  9.1 282.4 %all-gather.5.cloned.1.call-start = ((), (), s32[]{:S(2)}) async-start(), calls=%async_computation.2 | async-start | bytes 5242880 | tf_op jit(solution)/shard_map/all_gather | solution.py:1897
  11.5 89.4 %copy-start.19 = (bf16[12,64]{1,0:T(8,128)(2,1)S(1)}, bf16[12,64]{1,0:T(8,128)(2,1)}, u32[]{:S(2)}) copy-start(bf16[12,64]{1,0:T(8,128)(2,1)} %param.31) | copy-start | bytes 4612
  11.5 90.0 %copy-start.17 = (bf16[5,12,64]{2,1,0:T(8,128)(2,1)S(1)}, bf16[5,12,64]{2,1,0:T(8,128)(2,1)}, u32[]{:S(2)}) copy-start(bf16[5,12,64]{2,1,0:T(8,128)(2,1)} %param.28) | copy-start | bytes 23044
  11.5 90.1 %copy-start.21 = (bf16[256]{0:T(256)(128)(2,1)S(1)}, bf16[256]{0:T(256)(128)(2,1)}, u32[]{:S(2)}) copy-start(bf16[256]{0:T(256)(128)(2,1)} %param.33) | copy-start | bytes 1540
  11.6 90.3 %copy-start.22 = (bf16[256]{0:T(256)(128)(2,1)S(1)}, bf16[256]{0:T(256)(128)(2,1)}, u32[]{:S(2)}) copy-start(bf16[256]{0:T(256)(128)(2,1)} %param.21) | copy-start | bytes 1540
  11.6 90.4 %copy-start.7 = (s32[1024]{0:T(1024)S(1)}, s32[1024]{0:T(1024)}, u32[]{:S(2)}) copy-start(s32[1024]{0:T(1024)} %param.19) | copy-start | bytes 12292
  12.8 89.4 %copy-start.16 = (bf16[256,2,1024]{2,1,0:T(2,128)(2,1)S(1)}, bf16[256,2,1024]{2,1,0:T(2,128)(2,1)}, u32[]{:S(2)}) copy-start(bf16[256,2,1024]{2,1,0:T(2,128)(2,1)} %param.34) | copy-start | bytes 3145732
  12.9 91.0 %copy-start.20 = (f32[3,12]{1,0:T(4,128)S(1)}, f32[3,12]{1,0:T(4,128)}, u32[]{:S(2)}) copy-start(f32[3,12]{1,0:T(4,128)} %param.30) | copy-start | bytes 436
  100.8 425.6 %reduce-scatter.2.cloned.1.call-start = ((), (), s32[]{:S(2)}) async-start(), calls=%async_computation.3 | async-start | bytes 5242880 | tf_op jit(solution)/shard_map/reduce_scatter | solution.py:1901
  126.8 6.9 %copy-start.18 = (bf16[5,512]{1,0:T(8,128)(2,1)S(1)}, bf16[5,512]{1,0:T(8,128)(2,1)}, u32[]{:S(2)}) copy-start(bf16[5,512]{1,0:T(8,128)(2,1)} %param.29) | copy-start | bytes 15364
  133.6 14.2 %copy-start.4 = (bf16[1024,256]{1,0:T(8,128)(2,1)}, bf16[1024,256]{1,0:T(8,128)(2,1)S(1)}, u32[]{:S(2)}) copy-start(bf16[1024,256]{1,0:T(8,128)(2,1)S(1)} %attend_forward.1.attended_ref) | copy-start | bytes 1572868
  147.8 1.5 copy-start.2
  149.3 0.6 copy-start.13
  437.3 16.8 %copy-start = (bf16[1024,1024]{1,0:T(8,128)(2,1)S(1)}, bf16[1024,1024]{1,0:T(8,128)(2,1)}, u32[]{:S(2)}) copy-start(bf16[1024,1024]{1,0:T(8,128)(2,1)} %get-tuple-element.80.mix_in_ref) | copy-start | bytes 6291460
  437.3 16.8 %copy-start.3 = (bf16[1024,1280]{1,0:T(8,128)(2,1)S(1)}, bf16[1024,1280]{1,0:T(8,128)(2,1)}, u32[]{:S(2)}) copy-start(bf16[1024,1280]{1,0:T(8,128)(2,1)} %copy-done.2) | copy-start | bytes 7864324
  437.3 16.8 %copy-start.8 = (f32[1,768]{1,0:T(1,128)S(1)}, f32[1,768]{1,0:T(1,128)}, u32[]{:S(2)}) copy-start(f32[1,768]{1,0:T(1,128)} %reshape.159.gain_ref) | copy-start | bytes 9220
  437.4 16.8 %copy-start.11 = (f32[8,1,128]{2,1,0:T(1,128)S(1)}, f32[8,1,128]{2,1,0:T(1,128)}, u32[]{:S(2)}) copy-start(f32[8,1,128]{2,1,0:T(1,128)} %get-tuple-element.95.inv_ref) | copy-start | bytes 12292
  454.2 0.7 copy-start.12
  454.8 41.4 %copy-start.5 = (bf16[1024,256]{1,0:T(8,128)(2,1)S(1)}, bf16[1024,256]{1,0:T(8,128)(2,1)}, u32[]{:S(2)}) copy-start(bf16[1024,256]{1,0:T(8,128)(2,1)} %get-tuple-element.93.do_ref) | copy-start | bytes 1572868
  496.2 11.3 %copy-start.23 = (bf16[1024,2048]{1,0:T(8,128)(2,1)S(1)}, bf16[1024,2048]{1,0:T(8,128)(2,1)}, u32[]{:S(2)}) copy-start(bf16[1024,2048]{1,0:T(8,128)(2,1)} %get-tuple-element.104) | copy-start | bytes 12582916
  507.5 18.9 %copy-start.14 = (f32[256,2048]{1,0:T(8,128)S(1)}, f32[256,2048]{1,0:T(8,128)}, u32[]{:S(2)}) copy-start(f32[256,2048]{1,0:T(8,128)} %get-tuple-element.82.refs_3_) | copy-start | bytes 6291460
  631.0 1.9 copy-start.1
  632.9 0.9 copy-start.6
  633.9 0.8 copy-start.9
  634.6 0.7 copy-start.10
  635.3 7.8 %copy-start.15 = (f32[256,2048]{1,0:T(8,128)S(1)}, f32[256,2048]{1,0:T(8,128)}, u32[]{:S(2)}) copy-start(f32[256,2048]{1,0:T(8,128)} %get-tuple-element.188) | copy-start | bytes 6291460
Sparse Core Ops, SparseCore 0:
  10.5 57.3 all-gather.2
  101.0 84.9 all-gather.4
  437.4 76.5 reduce-scatter.1

commit v4 on v3

--- a/solution.py
+++ b/solution.py
@@ -338,8 +338,9 @@
     def _():
         small_ref[...] = jnp.zeros_like(small_ref)
         row = 0
-        for array in (dconv_ref, dhp_ref, dgain_ref):
-            for first in range(0, array.shape[1], LANES):
+        state_first = list(range(channels, dconv_ref.shape[1], LANES)) + list(range(0, channels, LANES))
+        for array, columns in ((dconv_ref, state_first), (dhp_ref, [0]), (dgain_ref, range(0, channels, LANES))):
+            for first in columns:
                 small_ref[row : row + 8, :] = array[:, first : first + LANES]
                 row += 8
 
@@ -1038,38 +1039,47 @@
     return jnp.where(iota(lanes.shape, 1) == index, own * lanes, lanes)
 
 
-def common_sum(group, place, ranges, state_rows, piece_out, lanes, refs):
+def common_sum(group, place, ranges, state_rows, piece_out, make_lanes, refs):
     common_ref, state_ref, gains_ref, outbox, inbox, send_sem, recv_sem = refs
     rows, width = common_ref.shape
     start, stop = state_rows
-    first = 0
-    for column, count in ranges:
-        outbox[:, first : first + count] = piece_out[:, column : column + count].astype(BF16)
-        first += count
-    state = piece_out[start:stop, piece_out.shape[1] - LANES :]
-    for peer in range(group):
-        outbox[peer * rows : peer * rows + stop - start, width : width + LANES] = state.astype(BF16)
-    outbox[:, width + LANES :] = lanes.astype(BF16)
-    copies = []
-    for hop in range(1, group):
+
+    def copy(hop):
         peer = lax.rem(place + hop, group)
-        copies.append(
-            pltpu.make_async_remote_copy(
-                outbox.at[pl.ds(peer * rows, rows)], inbox.at[hop - 1], send_sem.at[hop - 1], recv_sem.at[hop - 1],
-                device_id={"tensor": peer}, device_id_type=MESH,
-            )
+        return peer, pltpu.make_async_remote_copy(
+            outbox.at[pl.ds(peer * rows, rows)], inbox.at[hop - 1], send_sem.at[hop - 1], recv_sem.at[hop - 1],
+            device_id={"tensor": peer}, device_id_type=MESH,
         )
-    for copy in copies:
-        copy.start()
-    total = outbox[pl.ds(place * rows, rows), :].astype(F32)
-    for hop, copy in enumerate(copies):
-        copy.wait_recv()
-        total = total + inbox[hop].astype(F32)
-    common_ref[...] = total[:, :width]
-    state_ref[...] = total[: stop - start, width : width + LANES]
-    gains_ref[...] = total[:, width + LANES :]
-    for copy in copies:
-        copy.wait_send()
+
+    def send(odd):
+        state = piece_out[start:stop, piece_out.shape[1] - LANES :].astype(BF16)
+        for peer in range(odd, group, 2):
+            here = slice(peer * rows, (peer + 1) * rows)
+            first = 0
+            for column, count in ranges:
+                outbox[here, first : first + count] = piece_out[here, column : column + count].astype(BF16)
+                first += count
+            outbox[peer * rows : peer * rows + stop - start, width : width + LANES] = state
+            outbox[here, width + LANES :] = make_lanes(here).astype(BF16)
+        for hop in range(1, group):
+            peer, item = copy(hop)
+
+            @pl.when(lax.rem(peer, 2) == odd)
+            def _():
+                item.start()
+
+    def finish():
+        total = outbox[pl.ds(place * rows, rows), :].astype(F32)
+        for hop in range(1, group):
+            copy(hop)[1].wait_recv()
+            total = total + inbox[hop - 1].astype(F32)
+        common_ref[...] = total[:, :width]
+        state_ref[...] = total[: stop - start, width : width + LANES]
+        gains_ref[...] = total[:, width + LANES :]
+        for hop in range(1, group):
+            copy(hop)[1].wait_send()
+
+    return send, finish
 
 
 PRODUCT_TURNS = (
@@ -1272,6 +1282,14 @@
             device_id={"tensor": place + 1 - 2 * side}, device_id_type=MESH,
         )
 
+    if ranges:
+        make_lanes = lambda here: gain_lanes(
+            lanes_ref[here, :], weight_ref[here, :], piece_out[here, : weight_ref.shape[1]], gain_index
+        )
+        common_send, common_finish = common_sum(
+            group, place, ranges, state_rows, piece_out, make_lanes, common_refs + take(4)
+        )
+
     load_x().wait()
     for index in range(group):
         load_w(index).wait()
@@ -1387,6 +1405,12 @@
                 @pl.when(chunk > 0)
                 def _():
                     add_last(chunk - 1)
+
+            if ranges and slot == 1:
+
+                @pl.when(chunk == chunks // 2)
+                def _():
+                    common_send(0)
 
             if gather_rows:
                 for step, turn_chunk, turn_slot, index in GATHER_TURNS:
@@ -1410,11 +1434,13 @@
 
     lax.fori_loop(0, chunks + 1 if spread or piece_count else chunks, one_chunk, 0)
     if piece_count:
-        lanes = gain_lanes(lanes_ref[...], weight_ref[...], piece_out[:, : weight_ref.shape[1]], gain_index)
         if ranges:
-            common_sum(group, place, ranges, state_rows, piece_out, lanes, common_refs + take(4))
+            common_send(1)
+            common_finish()
         else:
-            common_refs[0][...] = lanes
+            common_refs[0][...] = gain_lanes(
+                lanes_ref[...], weight_ref[...], piece_out[:, : weight_ref.shape[1]], gain_index
+            )
 
     def finish_sends(chunk, carry):
         for half in (0, 1):
@@ -1611,7 +1637,7 @@
     gate_first = (channels + 2 * NS) // LANES * 8 + 8
     head[...] = in_ref[gate_first - 8 : gate_first - 5, last : last + heads]
     for index in range(heads // 2):
-        for start, rows, target in ((0, KC + 1, conv_inner), (gate_first, 1, gate_gain)):
+        for start, rows, target in ((2 * NS // LANES * 8, KC + 1, conv_inner), (gate_first, 1, gate_gain)):
             block = in_ref[start + 8 * index : start + 8 * index + 8, last:]
             block = pltpu.roll(block, lax.rem(LANES - owner * piece, LANES), 1)
             for side in (0, 1):
@@ -1995,7 +2021,7 @@
         [], group, model, 6, "first_sum", dp_size, spread=False,
         pieces=[grad_in, grad_mix_weight, small.astype(BF16)], gains=(weight_own, lanes, 0),
         ranges=((2 * channels, 2 * NS), (lead, pair_cols)),
-        state_rows=(channels // LANES * 8, (channels + 2 * NS) // LANES * 8),
+        state_rows=(0, 2 * NS // LANES * 8),
     )
     grads = unpack(
         in_sum, ffn_sum, common, state, gain_sums, heads, query_cols, mixer_cols, hidden, dp_size, group

time: 655 us -> 655 us (level)
  transfers between devices with their start and end apart: 3 -> 3, of which waited for: 0 -> 0; matrix products, arithmetic and copies ran while one was open for 5% -> 5% of each run, Pallas kernels for 51% -> 52%
where the time goes in v4:
time: 655 us; the launch traced here: 647 us
  Pallas kernels  583 us (89%)
  local copies, waits for them, and re-layouts  22.1 us (3%)
  matrix products  18.9 us (3%)
  between operations  14.4 us (2%)
  other arithmetic  8.04 us (1%)
    pallas_call x3, Pallas kernels, line_sum(): pl.pallas_call(functools.partial(line_sum_kernel, group, spread, by_rows,...  358 us
    pallas_call x1, Pallas kernels, entry_gather(): pl.pallas_call(functools.partial(entry_gather_kernel, group, parts), in_s...  84.3 us
    pallas_call x1, Pallas kernels, mixer_backward(): pl.pallas_call(functools.partial(mixer_backward_kernel, heads), grid=(ste...  40.8 us
    pallas_call x1, Pallas kernels, project(): pl.pallas_call(project_kernel, grid=(cols // tile,), in_specs=[whole_bloc...  20.6 us
    dot_general x1, matrix products, mat_tn(): lax.dot_general(left_side, right_side, (((0,), (0,)), ((), ())), preferre...  18.9 us
    pallas_call x1, Pallas kernels, gate_back(): pl.pallas_call(functools.partial(gate_back_kernel, group, query_cols), gr...  16.7 us
    pallas_call x1, Pallas kernels, mixer_forward(): pl.pallas_call(functools.partial(mixer_forward_kernel, heads), grid=(step...  14.1 us
  transfers between devices with their start and end apart: 3, of which 0 were waited for; matrix products, arithmetic and copies ran while one was open for 5% of the time, Pallas kernels for 52%

profile of v4, /device:TPU:0, one launch (start us, length us, event | category | flops | bytes accessed | tf_op | source)
XLA Modules:
  0.0 647.1 jit_solution(3436177571283156261)
XLA Ops:
  7.2 0.0 all-gather.3.cloned.1.call-start
  7.2 1.9 pad_maximum_fusion.2
  9.1 0.0 all-gather.3.cloned.1.call-update
  9.1 0.0 all-gather.5.cloned.1.call-start
  9.2 0.8 copy.41
  10.0 0.7 broadcast_in_dim.32
  10.8 0.8 broadcast_in_dim.33
  11.5 0.0 copy-start.19
  11.5 0.0 copy-start.17
  11.5 0.0 copy-start.21
  11.6 0.0 copy-start.22
  11.6 0.0 copy-start.7
  11.6 1.2 copy.55
  12.8 0.0 copy-start.16
  12.9 0.0 copy-start.20
  12.9 3.6 concatenate.18.weight_ref.refs_8_
  16.5 84.3 %entry_gather.1 = (bf16[4,256,2048]{2,1,0:T(8,128)(2,1)}, bf16[2048,3072]{1,0:T(8,128)(2,1)}) custom-call(bf16[256,2048]{1,0:T(8,128)(2,1)} %refs_2_.5, bf16[256,3072]{1,0:T(8,128)(2,1)} %concatenate.18.weight_ref.refs_8_), custom_call_target="tpu_custom_call" | custom-call | tf_op jit(solution)/shard_map/entry_gather/pallas_call | solution.py:891
  100.8 0.0 all-gather.5.cloned.1.call-update
  100.8 0.0 reduce-scatter.2.cloned.1.call-start
  100.9 0.7 reshape.159.gain_ref
  101.6 0.1 reshape.144
  101.7 0.0 copy-done.21
  101.7 0.1 copy.48
  101.8 0.1 copy.47
  102.0 0.2 copy.44.seg_ref.segb_ref
  102.2 1.6 reshape.150.refs_4_.refs_9_
  103.8 0.1 pad.15.clone
  103.9 20.6 %project.1 = (f32[1024,3072]{1,0:T(8,128)}, bf16[1024,2048]{1,0:T(8,128)(2,1)}, f32[8,2048]{1,0:T(8,128)}) custom-call(bf16[1024,2048]{1,0:T(8,128)(2,1)} %bitcast.31, bf16[2048,3072]{1,0:T(8,128)(2,1)} %get-tuple-element.76.gains_ref.w_ref.refs_1_, bf16[2048,3072]{1,0:T(8,128)(2,1)} %get-tuple-element.76.gains_ref.w_ref.refs_1_), custom_call_target="tpu_custom_call" | custom-call | tf_op jit(solution)/shard_map/project/pallas_call | solution.py:1700
  124.5 1.9 fusion.1
  126.4 0.3 pad_maximum_fusion
  126.8 0.0 copy-start.18
  126.8 6.8 %attend_forward.1.attended_ref = bf16[1024,256]{1,0:T(8,128)(2,1)S(1)} custom-call(s32[1]{0:T(128)} %bitcast.3.head_ref, f32[1024,3072]{1,0:T(8,128)} %get-tuple-element.77.lin_ref.q_ref.k_ref.v_ref.gate_ref.before_ref, f32[1024,3072]{1,0:T(8,128)} %get-tuple-element.77.lin_ref.q_ref.k_ref.v_ref.gate_ref.before_ref, ...), custom_call_target="tpu_custom_call" | custom-call | tf_op jit(solution)/shard_map/attend_forward/pallas_call | solution.py:556
  133.6 0.0 copy-start.4
  133.6 0.0 copy-done.18
  133.7 14.1 %mixer_forward.1 = (f32[1024,768]{1,0:T(8,128)}, bf16[1024,1280]{1,0:T(8,128)(2,1)S(1)}, f32[8,1,128]{2,1,0:T(1,128)S(1)}, bf16[8,256,768]{2,1,0:T(8,128)(2,1)}) custom-call(f32[1024,3072]{1,0:T(8,128)} %get-tuple-element.77.lin_ref.q_ref.k_ref.v_ref.gate_ref.before_ref, s32[1024,1]{1,0:T(8,128)S(1)} %copy.44.seg_ref.segb_ref, s32[1,1024]{1,0:T(1,128)S(1)} %bitcast.24, ...), custom_call_target="tpu_custom_call" | custom-call | tf_op jit(solution)/shard_map/mixer_forward/pallas_call | solution.py:359
  147.8 1.5 copy-done.2
  149.3 0.6 copy-done.13
  149.9 12.6 %gate_norm.1 = (bf16[1024,1024]{1,0:T(8,128)(2,1)}, f32[8,1,128]{2,1,0:T(1,128)}) custom-call(f32[8,1,128]{2,1,0:T(1,128)} %copy-done.13, f32[1024,768]{1,0:T(8,128)} %get-tuple-element.79.ssm_ref, f32[1024,3072]{1,0:T(8,128)} %get-tuple-element.77.lin_ref.q_ref.k_ref.v_ref.gate_ref.before_ref, f32[1,768]{1,0:T(1,128)} %reshape.159.gain_ref, ...), custom_call_target="tpu_custom_call" | custom-call | tf_op jit(solution)/shard_map/gate_norm/pallas_call | solution.py:1772
  162.5 0.8 maximum_maximum_fusion.refs_10_
  163.2 1.5 fusion.9
  164.8 126.7 %mix_sum.1 = (bf16[4,256,2048]{2,1,0:T(8,128)(2,1)}, f32[256,2048]{1,0:T(8,128)}, bf16[2048,2048]{1,0:T(8,128)(2,1)}, bf16[1024,2048]{1,0:T(8,128)(2,1)}, f32[4,256,2048]{2,1,0:T(8,128)}) custom-call(bf16[4,256,1024]{2,1,0:T(8,128)(2,1)} %bitcast.21, bf16[1024,2048]{1,0:T(8,128)(2,1)} %all-gather.3.cloned.1.call-done.refs_1_.w_ref, ...), custom_call_target="tpu_custom_call" | custom-call | tf_op jit(solution)/shard_map/mix_sum/pallas_call | solution.py:1577
  291.5 0.0 all-gather.5.cloned.1.call-done.cot_ref.refs_6_
  291.6 12.4 %feed_forward.1 = (bf16[1024,1024]{1,0:T(8,128)(2,1)}, bf16[1024,2048]{1,0:T(8,128)(2,1)}) custom-call(bf16[1024,2048]{1,0:T(8,128)(2,1)} %all-gather.5.cloned.1.call-done.cot_ref.refs_6_, f32[1024,2048]{1,0:T(8,128)} %bitcast.30, bf16[1024,2048]{1,0:T(8,128)(2,1)} %get-tuple-element.85.shrink_ref.refs_8_), custom_call_target="tpu_custom_call" | custom-call | tf_op jit(solution)/shard_map/feed_forward/pallas_call | solution.py:1872
  304.0 133.3 %second_sum.1 = (bf16[4,256,2048]{2,1,0:T(8,128)(2,1)}, f32[256,2048]{1,0:T(8,128)}, bf16[2048,2048]{1,0:T(8,128)(2,1)}, bf16[2048,1024]{1,0:T(8,128)(2,1)}, bf1...) custom-call(bf16[4,256,2048]{2,1,0:T(8,128)(2,1)} %bitcast.33, ...), custom_call_target="tpu_custom_call" | custom-call | tf_op jit(solution)/shard_map/second_sum/pallas_call | solution.py:1577
  437.3 0.0 reduce-scatter.2.cloned.1.call-update
  437.3 0.0 copy-start.8
  437.4 16.7 %gate_back.1 = (bf16[1024,256]{1,0:T(8,128)(2,1)}, f32[1024,768]{1,0:T(8,128)}, f32[8,1,128]{2,1,0:T(1,128)}) custom-call(bf16[1024,2048]{1,0:T(8,128)(2,1)} %bitcast.28, bf16[1024,2048]{1,0:T(8,128)(2,1)} %all-gather.3.cloned.1.call-done.refs_1_.w_ref, f32[1024,768]{1,0:T(8,128)} %get-tuple-element.79.ssm_ref, ...), custom_call_target="tpu_custom_call" | custom-call | tf_op jit(solution)/shard_map/gate_back/pallas_call | solution.py:1834
  454.2 0.7 copy-done.12
  454.8 40.8 %mixer_backward.1 = (bf16[1024,3072]{1,0:T(8,128)(2,1)}, f32[256,128]{1,0:T(8,128)S(1)}, bf16[2048,1024]{1,0:T(8,128)(2,1)}) custom-call(f32[1024,3072]{1,0:T(8,128)} %get-tuple-element.77.lin_ref.q_ref.k_ref.v_ref.gate_ref.before_ref, f32[1024,3072]{1,0:T(8,128)} %get-tuple-element.77.lin_ref.q_ref.k_ref.v_ref.gate_ref.before_ref, ...), custom_call_target="tpu_custom_call" | custom-call | tf_op jit(solution)/shard_map/mixer_backward/pallas_call | solution.py:406
  495.6 0.6 convert_element_type.63.refs_7_
  496.3 11.3 %attend_backward.1 = bf16[1024,3072]{1,0:T(8,128)(2,1)} custom-call(s32[1]{0:T(128)} %bitcast.3.head_ref, f32[1024,3072]{1,0:T(8,128)} %get-tuple-element.77.lin_ref.q_ref.k_ref.v_ref.gate_ref.before_ref, f32[1024,3072]{1,0:T(8,128)} %get-tuple-element.77.lin_ref.q_ref.k_ref.v_ref.gate_ref.before_ref, ...), custom_call_target="tpu_custom_call", output_to_operand_aliasing={{}: (9, {})} | custom-call | tf_op jit(solution)/shard_map/attend_backward/pallas_call | solution.py:572
  507.5 0.0 copy-done.23
  507.5 18.9 %convolution_convert_fusion.refs_5_ = bf16[2048,3072]{1,0:T(8,128)(2,1)} fusion(bf16[1024,2048]{1,0:T(8,128)(2,1)S(1)} %copy-done.23, bf16[1024,3072]{1,0:T(8,128)(2,1)} %attend_backward.1), kind=kOutput, calls=%fused_computation | convolution fusion | flops 12891193344 | bytes 23068672 | tf_op jit(solution)/shard_map/dot_general | solution.py:42
  526.4 2.5 add_convert_fusion
  528.9 98.0 %first_sum.1 = (f32[256,2048]{1,0:T(8,128)}, f32[256,4224]{1,0:T(8,128)}, f32[64,1024]{1,0:T(8,128)}, f32[32,128]{1,0:T(8,128)}, f32[64,128]{1,0:T(8,128)}) custom-call(bf16[4,256,3072]{2,1,0:T(8,128)(2,1)} %bitcast.27, bf16[2048,3072]{1,0:T(8,128)(2,1)} %get-tuple-element.76.gains_ref.w_ref.refs_1_, bf16[256,2048]{1,0:T(8,128)(2,1)} %refs_2_.5, ...), custom_call_target="tpu_custom_call" | custom-call | tf_op jit(solution)/shard_map/first_sum/pallas_call | solution.py:1577
  626.9 1.9 copy-done.1
  628.8 0.9 copy-done.6
  629.7 0.8 copy-done.9
  630.5 0.7 copy-done.10
  631.2 5.8 unpack.1
  637.0 0.7 copy.54
  637.6 0.7 copy.52
  638.3 0.7 copy.53
  639.0 1.3 copy.58
  (41 shorter events, 0.2 us)
Async XLA Ops:
  7.2 157.6 %all-gather.3.cloned.1.call-start = ((), (), s32[]{:S(2)}) async-start(), calls=%async_computation.1 | async-start | bytes 4718592 | tf_op jit(solution)/shard_map/all_gather | solution.py:1923
  9.1 282.4 %all-gather.5.cloned.1.call-start = ((), (), s32[]{:S(2)}) async-start(), calls=%async_computation.2 | async-start | bytes 5242880 | tf_op jit(solution)/shard_map/all_gather | solution.py:1923
  11.5 89.4 %copy-start.19 = (bf16[12,64]{1,0:T(8,128)(2,1)S(1)}, bf16[12,64]{1,0:T(8,128)(2,1)}, u32[]{:S(2)}) copy-start(bf16[12,64]{1,0:T(8,128)(2,1)} %param.31) | copy-start | bytes 4612
  11.5 90.0 %copy-start.17 = (bf16[5,12,64]{2,1,0:T(8,128)(2,1)S(1)}, bf16[5,12,64]{2,1,0:T(8,128)(2,1)}, u32[]{:S(2)}) copy-start(bf16[5,12,64]{2,1,0:T(8,128)(2,1)} %param.28) | copy-start | bytes 23044
  11.5 90.1 %copy-start.21 = (bf16[256]{0:T(256)(128)(2,1)S(1)}, bf16[256]{0:T(256)(128)(2,1)}, u32[]{:S(2)}) copy-start(bf16[256]{0:T(256)(128)(2,1)} %param.33) | copy-start | bytes 1540
  11.6 90.3 %copy-start.22 = (bf16[256]{0:T(256)(128)(2,1)S(1)}, bf16[256]{0:T(256)(128)(2,1)}, u32[]{:S(2)}) copy-start(bf16[256]{0:T(256)(128)(2,1)} %param.21) | copy-start | bytes 1540
  11.6 90.4 %copy-start.7 = (s32[1024]{0:T(1024)S(1)}, s32[1024]{0:T(1024)}, u32[]{:S(2)}) copy-start(s32[1024]{0:T(1024)} %param.19) | copy-start | bytes 12292
  12.8 89.4 %copy-start.16 = (bf16[256,2,1024]{2,1,0:T(2,128)(2,1)S(1)}, bf16[256,2,1024]{2,1,0:T(2,128)(2,1)}, u32[]{:S(2)}) copy-start(bf16[256,2,1024]{2,1,0:T(2,128)(2,1)} %param.34) | copy-start | bytes 3145732
  12.9 91.0 %copy-start.20 = (f32[3,12]{1,0:T(4,128)S(1)}, f32[3,12]{1,0:T(4,128)}, u32[]{:S(2)}) copy-start(f32[3,12]{1,0:T(4,128)} %param.30) | copy-start | bytes 436
  100.8 425.6 %reduce-scatter.2.cloned.1.call-start = ((), (), s32[]{:S(2)}) async-start(), calls=%async_computation.3 | async-start | bytes 5242880 | tf_op jit(solution)/shard_map/reduce_scatter | solution.py:1927
  126.8 6.9 %copy-start.18 = (bf16[5,512]{1,0:T(8,128)(2,1)S(1)}, bf16[5,512]{1,0:T(8,128)(2,1)}, u32[]{:S(2)}) copy-start(bf16[5,512]{1,0:T(8,128)(2,1)} %param.29) | copy-start | bytes 15364
  133.6 14.2 %copy-start.4 = (bf16[1024,256]{1,0:T(8,128)(2,1)}, bf16[1024,256]{1,0:T(8,128)(2,1)S(1)}, u32[]{:S(2)}) copy-start(bf16[1024,256]{1,0:T(8,128)(2,1)S(1)} %attend_forward.1.attended_ref) | copy-start | bytes 1572868
  147.8 1.5 copy-start.2
  149.3 0.6 copy-start.13
  437.3 16.8 %copy-start = (bf16[1024,1024]{1,0:T(8,128)(2,1)S(1)}, bf16[1024,1024]{1,0:T(8,128)(2,1)}, u32[]{:S(2)}) copy-start(bf16[1024,1024]{1,0:T(8,128)(2,1)} %get-tuple-element.80.mix_in_ref) | copy-start | bytes 6291460
  437.3 16.8 %copy-start.3 = (bf16[1024,1280]{1,0:T(8,128)(2,1)S(1)}, bf16[1024,1280]{1,0:T(8,128)(2,1)}, u32[]{:S(2)}) copy-start(bf16[1024,1280]{1,0:T(8,128)(2,1)} %copy-done.2) | copy-start | bytes 7864324
  437.3 16.8 %copy-start.8 = (f32[1,768]{1,0:T(1,128)S(1)}, f32[1,768]{1,0:T(1,128)}, u32[]{:S(2)}) copy-start(f32[1,768]{1,0:T(1,128)} %reshape.159.gain_ref) | copy-start | bytes 9220
  437.4 16.8 %copy-start.11 = (f32[8,1,128]{2,1,0:T(1,128)S(1)}, f32[8,1,128]{2,1,0:T(1,128)}, u32[]{:S(2)}) copy-start(f32[8,1,128]{2,1,0:T(1,128)} %get-tuple-element.95.inv_ref) | copy-start | bytes 12292
  454.2 0.7 copy-start.12
  454.8 41.4 %copy-start.5 = (bf16[1024,256]{1,0:T(8,128)(2,1)S(1)}, bf16[1024,256]{1,0:T(8,128)(2,1)}, u32[]{:S(2)}) copy-start(bf16[1024,256]{1,0:T(8,128)(2,1)} %get-tuple-element.93.do_ref) | copy-start | bytes 1572868
  496.2 11.3 %copy-start.23 = (bf16[1024,2048]{1,0:T(8,128)(2,1)S(1)}, bf16[1024,2048]{1,0:T(8,128)(2,1)}, u32[]{:S(2)}) copy-start(bf16[1024,2048]{1,0:T(8,128)(2,1)} %get-tuple-element.104) | copy-start | bytes 12582916
  507.5 18.9 %copy-start.14 = (f32[256,2048]{1,0:T(8,128)S(1)}, f32[256,2048]{1,0:T(8,128)}, u32[]{:S(2)}) copy-start(f32[256,2048]{1,0:T(8,128)} %get-tuple-element.82.refs_3_) | copy-start | bytes 6291460
  626.9 1.9 copy-start.1
  628.8 0.9 copy-start.6
  629.7 0.8 copy-start.9
  630.5 0.7 copy-start.10
  631.2 7.8 %copy-start.15 = (f32[256,2048]{1,0:T(8,128)S(1)}, f32[256,2048]{1,0:T(8,128)}, u32[]{:S(2)}) copy-start(f32[256,2048]{1,0:T(8,128)} %get-tuple-element.188) | copy-start | bytes 6291460
Sparse Core Ops, SparseCore 0:
  10.5 57.3 all-gather.2
  101.0 84.9 all-gather.4
  437.4 76.5 reduce-scatter.1
